TPU v7x, 128 devices: a whole 4x4x4 slice. The times are simulated.
128 devices in a mesh: dp: 8 (over x_lo, y), tensor: 16 (over x_hi, z, core).
Axes of the slice: x: 4 (x_hi: 2, x_lo: 2; x = x_hi * 2 + x_lo), y: 4, z: 4, core: 2. Of those that a mesh axis runs over, the one named last changes fastest.
Arguments:
- tokens: bfloat16 [1024, 16, 1024], P('tensor', 'dp'), may hold values from -6 to 6
- segments: int32 [16, 1024], P('dp'), may hold values from 0 to 3, as said below
- cotangent: bfloat16 [1024, 16, 1024], P('tensor', 'dp'), may hold values from -6 to 6
- w_qkv: bfloat16 [2, 3, 1024, 1024], P(None, None, 'dp', 'tensor'), may hold values from -0.1875 to 0.1875
- b_qv: bfloat16 [2, 2, 16, 64], P(None, None, 'tensor', 'dp'), may hold values from -3 to 3
- w_out: bfloat16 [2, 1024, 1024], P(None, 'tensor', 'dp'), may hold values from -1.5 to 1.5
- w_fc: bfloat16 [2, 1024, 4096], P(None, 'dp', 'tensor'), may hold values from -0.1875 to 0.1875
- b_fc: bfloat16 [2, 16, 256], P(None, 'tensor', 'dp'), may hold values from -3 to 3
- w_proj: bfloat16 [2, 4096, 1024], P(None, 'tensor', 'dp'), may hold values from -0.09375 to 0.09375
- norm_gains: bfloat16 [2, 2, 1024], P(None, None, 'dp'), may hold values from 0.25 to 1.75
- shifts: bfloat16 [2, 4, 1024], P(None, None, 'dp'), may hold values from -2 to 2
Outputs:
- out: bfloat16 [1024, 16, 1024], P('tensor', 'dp')
- g_tokens: float32 [1024, 16, 1024], P('tensor', 'dp')
- g_w_qkv: float32 [2, 3, 1024, 1024], P(None, None, 'dp', 'tensor')
- g_b_qv: float32 [2, 2, 16, 64], P(None, None, 'tensor', 'dp')
- g_w_out: float32 [2, 1024, 1024], P(None, 'tensor', 'dp')
- g_w_fc: float32 [2, 1024, 4096], P(None, 'dp', 'tensor')
- g_b_fc: float32 [2, 16, 256], P(None, 'tensor', 'dp')
- g_w_proj: float32 [2, 4096, 1024], P(None, 'tensor', 'dp')
- g_norm_gains: float32 [2, 2, 1024], P(None, None, 'dp')
- g_shifts: float32 [2, 4, 1024], P(None, None, 'dp')
Inputs may be any that keep to these rules, and one draw needn't show every extreme that they name: `segments`: segment numbers never fall along a row; every document (a run of one number) holds at most 768 positions, and in every draw some row holds a document of exactly 768 positions.
All inputs are finite; a program needn't handle non-finite values.
Results may differ from a plain program's by a relative error of at most 0.023.
Values may be sent and summed in bfloat16 or wider, within the bound.
No kernel may reach another device: no remote copies, remote signals or barrier semaphores. Data moves between devices by JAX's collectives and lax.ppermute only.
A program may use at most 192 MiB of HBM per device.

v0:
```python
import jax
import jax.numpy as jnp
from jax import lax
from jax.sharding import Mesh
from jax.sharding import PartitionSpec as P

TENSOR = ("tensor_0", "tensor_1", "tensor_2")


EPS = 1e-05


def copy_for_each(value, axis):
    count = lax.axis_size(axis)
    return lax.all_to_all(
        jnp.broadcast_to(value[None], (count, *value.shape)), axis, 0, 0, tiled=True
    )


def in_order(blocks, dim):
    blocks = jnp.moveaxis(blocks, 0, dim)
    lengths = blocks.shape
    return blocks.reshape(*lengths[:dim], lengths[dim] * lengths[dim + 1], *lengths[dim + 2 :])


def gather_axes(value, axes, dim):
    far, near = axes
    initial = copy_for_each(value, far)
    blocks = jnp.swapaxes(copy_for_each(initial, near), 0, 1)
    return in_order(blocks.reshape(-1, *value.shape), dim)


def split_up(value, dim, count):
    lengths = value.shape
    blocks = value.reshape(*lengths[:dim], count, lengths[dim] // count, *lengths[dim + 1 :])
    return jnp.moveaxis(blocks, dim, 0)


def summed_on_arrival(value, axis, dim):
    count = lax.axis_size(axis)
    blocks = lax.all_to_all(split_up(value, dim, count), axis, 0, 0, tiled=True)
    return jnp.sum(blocks.astype(jnp.float32), axis=0)


def sum_in_two_steps(value, axes, dim):
    far, near = axes
    own = summed_on_arrival(split_up(value, dim, lax.axis_size(far)), near, dim + 1)
    return jnp.sum(
        lax.all_to_all(own.astype(jnp.bfloat16), far, 0, 0, tiled=True).astype(jnp.float32), axis=0
    )


def in_one_piece(arrays, axis, dim, along):
    both = jnp.concatenate(arrays, axis=along)
    out, at, done = (lax.all_gather(both, axis, axis=dim, tiled=True), 0, [])
    for a in arrays:
        done.append(lax.slice_in_dim(out, at, at + a.shape[along], axis=along))
        at += a.shape[along]
    return tuple(done)


def sent_together(arrays, axis, dim, along):
    ends, at = ([], 0)
    for a in arrays[:-1]:
        at += a.shape[along]
        ends.append(at)
    both = jnp.concatenate(arrays, axis=along)
    return tuple(
        jnp.split(lax.psum_scatter(both, axis, scatter_dimension=dim, tiled=True), ends, axis=along)
    )


def taken_together(value, axis):
    everything = copy_for_each(value, axis)
    return jnp.sum(everything, axis=0)


def in_one(arrays, axis):
    vector, at, done = (jnp.concatenate([a.reshape(-1) for a in arrays]), 0, [])
    subtotal = taken_together(vector, axis)
    for a in arrays:
        done.append(subtotal[at : at + a.size].reshape(a.shape))
        at += a.size
    return tuple(done)


def row_norm_values(values, gain_row, shift_row):
    center = values - jnp.mean(values, axis=-1, keepdims=True)
    spread = jnp.mean(center * center, axis=-1, keepdims=True)
    return center * lax.rsqrt(spread + EPS) * gain_row + shift_row


def gelu_tanh(values):
    return jax.nn.gelu(values, approximate=True)


def block_mask(segment_row, first_row, block_rows):
    length = segment_row.shape[0]
    positions = jnp.arange(length, dtype=jnp.int32)
    query_pos = first_row + jnp.arange(block_rows, dtype=jnp.int32)
    query_seg = lax.dynamic_slice_in_dim(segment_row, first_row, block_rows, 0)
    return (query_seg[:, None] == segment_row[None, :]) & (query_pos[:, None] >= positions[None, :])


def block_size():
    return 512


def attention_entry(operands):
    queries, keys_all, values_all, segment_row = operands
    length = queries.shape[0]
    block_rows = block_size()

    def attention_one_block(block_index):
        first_row = block_index * block_rows
        query_block = lax.dynamic_slice_in_dim(queries, first_row, block_rows, 0)
        allowed = block_mask(segment_row, first_row, block_rows)
        scores = (
            jnp.einsum("qd,kd->qk", query_block, keys_all, preferred_element_type=jnp.float32)
            * 0.125
        )
        scores = jnp.where(allowed, scores, -1e30)
        highest = jnp.max(scores, axis=1, keepdims=True)
        raised = jnp.exp(scores - highest)
        totals = jnp.sum(raised, axis=1, keepdims=True)
        probability = (raised / totals).astype(jnp.bfloat16)
        mixed_rows = jnp.dot(probability, values_all, preferred_element_type=jnp.float32)
        return (mixed_rows, (highest + jnp.log(totals))[:, 0])

    mixed_rows, logsum = lax.map(
        attention_one_block, jnp.arange(length // block_rows, dtype=jnp.int32)
    )
    return (mixed_rows.reshape(length, values_all.shape[1]), logsum.reshape(length))


def attend_back(operands):
    queries, keys_all, values_all, segment_row, logsum, grad_mixed = operands
    length, head_width = queries.shape
    block_rows = block_size()

    def attend_one_block(running, block_index):
        key_grad, value_grad = running
        first_row = block_index * block_rows
        query_block = lax.dynamic_slice_in_dim(queries, first_row, block_rows, 0)
        grad_block = lax.dynamic_slice_in_dim(grad_mixed, first_row, block_rows, 0)
        logsum_block = lax.dynamic_slice_in_dim(logsum, first_row, block_rows, 0)
        allowed = block_mask(segment_row, first_row, block_rows)
        scores = (
            jnp.einsum("qd,kd->qk", query_block, keys_all, preferred_element_type=jnp.float32)
            * 0.125
        )
        probability = jnp.exp(jnp.where(allowed, scores - logsum_block[:, None], -1e30))
        grad_prob = jnp.einsum(
            "qd,kd->qk", grad_block, values_all, preferred_element_type=jnp.float32
        )
        inner_sum = jnp.sum(probability * grad_prob, axis=1, keepdims=True)
        grad_scores = (probability * (grad_prob - inner_sum)).astype(jnp.bfloat16)
        query_grad = jnp.dot(grad_scores, keys_all, preferred_element_type=jnp.float32) * 0.125
        key_grad = (
            key_grad
            + jnp.einsum("qk,qd->kd", grad_scores, query_block, preferred_element_type=jnp.float32)
            * 0.125
        )
        value_grad = value_grad + jnp.einsum(
            "qk,qd->kd",
            probability.astype(jnp.bfloat16),
            grad_block,
            preferred_element_type=jnp.float32,
        )
        return ((key_grad, value_grad), query_grad)

    zero_grad = jnp.zeros((length, head_width), jnp.float32)
    (key_grad, value_grad), query_grad = lax.scan(
        attend_one_block, (zero_grad, zero_grad), jnp.arange(length // block_rows, dtype=jnp.int32)
    )
    return (query_grad.reshape(length, head_width), key_grad, value_grad)


def to_items(values, heads_local):
    length = values.shape[0]
    seq_count = values.shape[1]
    head_width = values.shape[2] // heads_local
    shaped = values.reshape(length, seq_count, heads_local, head_width).transpose(1, 2, 0, 3)
    return shaped.reshape(seq_count * heads_local, length, head_width)


def from_items(items, seq_count, heads_local):
    length = items.shape[1]
    head_width = items.shape[2]
    shaped = items.reshape(seq_count, heads_local, length, head_width).transpose(2, 0, 1, 3)
    return shaped.reshape(length, seq_count, heads_local * head_width)


def gather_project(values, weight):
    gathered = gather_axes(values, (("tensor_0", "tensor_1"), "tensor_2"), 0)
    projected = jnp.einsum("rsd,dc->rsc", gathered, weight, preferred_element_type=jnp.float32)
    return (projected, gathered)


def scatter_project(values, weight):

    def partial_term(first_row, row_count):
        return jnp.einsum("rsc,cd->rsd", values, weight, preferred_element_type=jnp.float32)

    return sum_in_two_steps(
        partial_term(
            jnp.int32(0), values.shape[0] // lax.axis_size(TENSOR) * lax.axis_size(TENSOR)
        ).astype(jnp.bfloat16),
        (("tensor_0", "tensor_1"), "tensor_2"),
        0,
    )


def scatter_back(gradient, weight):

    def partial_term(first_row, row_count):
        return jnp.einsum("rsc,dc->rsd", gradient, weight, preferred_element_type=jnp.float32)

    return sum_in_two_steps(
        partial_term(
            jnp.int32(0), gradient.shape[0] // lax.axis_size(TENSOR) * lax.axis_size(TENSOR)
        ).astype(jnp.bfloat16),
        (("tensor_0", "tensor_1"), "tensor_2"),
        0,
    )


def gather_grad(gradient):
    return gather_axes(gradient, (("tensor_0", "tensor_1"), "tensor_2"), 0)


def fold_grad(gradient, kept_rows):
    return jnp.einsum("rsd,rsc->dc", kept_rows, gradient, preferred_element_type=jnp.float32)


def fetch_forward(params, layer_index):
    w_qkv, b_qv, w_out, w_fc, b_fc, w_proj, norm_gains, shifts = params
    return (
        lax.all_gather(w_qkv[layer_index], "dp", axis=1, tiled=True),
        lax.all_gather(b_qv[layer_index], "dp", axis=2, tiled=True),
        lax.all_gather(w_out[layer_index], "dp", axis=1, tiled=True),
        lax.all_gather(w_fc[layer_index], "dp", axis=0, tiled=True),
        lax.all_gather(b_fc[layer_index], "dp", axis=1, tiled=True),
        *in_one_piece(
            (w_proj[layer_index], norm_gains[layer_index], shifts[layer_index]), "dp", 1, 0
        ),
    )


def on_device(
    tokens, segments, cotangent, w_qkv, b_qv, w_out, w_fc, b_fc, w_proj, norm_gains, shifts
):
    params = (w_qkv, b_qv, w_out, w_fc, b_fc, w_proj, norm_gains, shifts)
    heads_local = b_qv.shape[2]
    seq_count = tokens.shape[1]
    layer_total = w_qkv.shape[0]
    segment_items = jnp.repeat(segments, heads_local, axis=0)
    residual = tokens.astype(jnp.float32)
    kept_state = []
    for layer_index in range(layer_total):
        weights = fetch_forward(params, layer_index)
        qkv_w, qv_bias, out_w, fc_w, fc_bias, projection_weight, gain_pair, shift_set = weights
        columns = qkv_w.shape[2]
        attn_input = residual
        stacked = jnp.concatenate((qkv_w[0], qkv_w[1], qkv_w[2]), axis=1)
        normed = row_norm_values(residual, gain_pair[0], shift_set[0]).astype(jnp.bfloat16)
        projected, attn_rows = gather_project(normed, stacked)
        queries = (
            projected[:, :, :columns] + qv_bias[0].reshape(columns).astype(jnp.float32)
        ).astype(jnp.bfloat16)
        keys_all = projected[:, :, columns : 2 * columns].astype(jnp.bfloat16)
        values_all = (
            projected[:, :, 2 * columns :] + qv_bias[1].reshape(columns).astype(jnp.float32)
        ).astype(jnp.bfloat16)
        query_items = to_items(queries, heads_local)
        key_items = to_items(keys_all, heads_local)
        value_items = to_items(values_all, heads_local)
        mixed_items, logsum = lax.map(
            attention_entry, (query_items, key_items, value_items, segment_items)
        )
        mixed_heads = from_items(mixed_items.astype(jnp.bfloat16), seq_count, heads_local)
        attn_out = scatter_project(mixed_heads, out_w)
        residual = residual + attn_out + shift_set[2].astype(jnp.float32)
        mlp_input = residual
        normed_mlp = row_norm_values(residual, gain_pair[1], shift_set[1]).astype(jnp.bfloat16)
        mlp_rows = None
        projected_mlp, mlp_rows = gather_project(normed_mlp, fc_w)
        hidden_pre = projected_mlp + fc_bias.reshape(-1).astype(jnp.float32)
        hidden_activation = gelu_tanh(hidden_pre).astype(jnp.bfloat16)
        mlp_out = scatter_project(hidden_activation, projection_weight)
        residual = residual + mlp_out + shift_set[3].astype(jnp.float32)
        kept_state.append(
            (
                weights,
                attn_input,
                mlp_input,
                query_items,
                key_items,
                value_items,
                mixed_heads,
                logsum,
                hidden_pre,
                attn_rows,
                mlp_rows,
            )
        )
    output = residual.astype(jnp.bfloat16)
    gradient = cotangent.astype(jnp.float32)
    layer_grads = []
    for layer_index in reversed(range(layer_total)):
        (
            weights,
            attn_input,
            mlp_input,
            query_items,
            key_items,
            value_items,
            mixed_heads,
            logsum,
            hidden_pre,
            attn_rows,
            mlp_rows,
        ) = kept_state[layer_index]
        qkv_w, qv_bias, out_w, fc_w, fc_bias, projection_weight, gain_pair, shift_set = weights
        columns = qkv_w.shape[2]
        mlp_grad = gradient.astype(jnp.bfloat16)
        shift_mlp = jnp.sum(mlp_grad.astype(jnp.float32), axis=(0, 1))
        normed_value, norm_pull = jax.vjp(
            row_norm_values,
            mlp_input,
            gain_pair[1].astype(jnp.float32),
            shift_set[1].astype(jnp.float32),
        )
        normed_mlp = normed_value.astype(jnp.bfloat16)
        hidden_value, gelu_pull = jax.vjp(gelu_tanh, hidden_pre)
        hidden_activation = hidden_value.astype(jnp.bfloat16)
        complete_gradient = gather_grad(mlp_grad)
        hidden_grad = jnp.einsum(
            "pqu,zu->pqz", complete_gradient, projection_weight, preferred_element_type=jnp.float32
        )
        projection_gradient = jnp.einsum(
            "teo,ter->or", hidden_activation, complete_gradient, preferred_element_type=jnp.float32
        )
        (pre_grad,) = gelu_pull(hidden_grad)
        pre_low = pre_grad.astype(jnp.bfloat16)
        fc_bias_grad = jnp.sum(pre_low.astype(jnp.float32), axis=(0, 1)).reshape(fc_bias.shape)
        fc_grad = fold_grad(pre_low, mlp_rows)
        normed_grad = scatter_back(pre_low, fc_w)
        input_grad, gain_mlp, shift_norm_mlp = norm_pull(normed_grad)
        gradient = gradient + input_grad
        attn_grad = gradient.astype(jnp.bfloat16)
        shift_attn = jnp.sum(attn_grad.astype(jnp.float32), axis=(0, 1))
        normed_value, norm_pull = jax.vjp(
            row_norm_values,
            attn_input,
            gain_pair[0].astype(jnp.float32),
            shift_set[0].astype(jnp.float32),
        )
        complete_gradient = gather_grad(attn_grad)
        mixed_grad = jnp.einsum(
            "lsd,cd->lsc", complete_gradient, out_w, preferred_element_type=jnp.float32
        ).astype(jnp.bfloat16)
        out_grad = jnp.einsum(
            "lsc,lsd->cd", mixed_heads, complete_gradient, preferred_element_type=jnp.float32
        )
        grad_items = to_items(mixed_grad, heads_local)
        query_grad, key_grad, value_grad = lax.map(
            attend_back, (query_items, key_items, value_items, segment_items, logsum, grad_items)
        )
        query_low = from_items(query_grad.astype(jnp.bfloat16), seq_count, heads_local)
        key_low = from_items(key_grad.astype(jnp.bfloat16), seq_count, heads_local)
        value_low = from_items(value_grad.astype(jnp.bfloat16), seq_count, heads_local)
        qkv_grad = jnp.concatenate((query_low, key_low, value_low), axis=2)
        query_bias_grad = jnp.sum(query_low.astype(jnp.float32), axis=(0, 1)).reshape(
            qv_bias.shape[1:]
        )
        value_bias_grad = jnp.sum(value_low.astype(jnp.float32), axis=(0, 1)).reshape(
            qv_bias.shape[1:]
        )
        qv_bias_grad = jnp.stack((query_bias_grad, value_bias_grad))
        stacked = jnp.concatenate((qkv_w[0], qkv_w[1], qkv_w[2]), axis=1)
        stacked_grad = fold_grad(qkv_grad, attn_rows)
        qkv_w_grad = stacked_grad.reshape(stacked_grad.shape[0], 3, columns).transpose(1, 0, 2)
        normed_grad = scatter_back(qkv_grad, stacked)
        input_grad, gain_attn, shift_norm_attn = norm_pull(normed_grad)
        gradient = gradient + input_grad
        gains_grad = jnp.stack((gain_attn, gain_mlp))
        shifts_grad = jnp.stack((shift_norm_attn, shift_norm_mlp, shift_attn, shift_mlp))
        shard_grads = (
            lax.psum_scatter(
                qkv_w_grad.astype(jnp.bfloat16), "dp", scatter_dimension=1, tiled=True
            ).astype(jnp.float32),
            lax.psum_scatter(
                qv_bias_grad.astype(jnp.bfloat16), "dp", scatter_dimension=2, tiled=True
            ).astype(jnp.float32),
            lax.psum_scatter(
                out_grad.astype(jnp.bfloat16), "dp", scatter_dimension=1, tiled=True
            ).astype(jnp.float32),
            lax.psum_scatter(
                fc_grad.astype(jnp.bfloat16), "dp", scatter_dimension=0, tiled=True
            ).astype(jnp.float32),
            lax.psum_scatter(
                fc_bias_grad.astype(jnp.bfloat16), "dp", scatter_dimension=1, tiled=True
            ).astype(jnp.float32),
            *tuple(
                (
                    part.astype(jnp.float32)
                    for part in sent_together(
                        (
                            projection_gradient.astype(jnp.bfloat16),
                            gains_grad.astype(jnp.bfloat16),
                            shifts_grad.astype(jnp.bfloat16),
                        ),
                        "dp",
                        1,
                        0,
                    )
                )
            ),
        )
        norm_part = in_one((shard_grads[6], shard_grads[7]), TENSOR)
        layer_grads.append(
            (
                shard_grads[0],
                shard_grads[1],
                shard_grads[2],
                shard_grads[3],
                shard_grads[4],
                shard_grads[5],
                norm_part[0],
                norm_part[1],
            )
        )
    ordered = layer_grads[::-1]
    stacked_out = tuple(
        (jnp.stack([grads_one[component] for grads_one in ordered]) for component in range(8))
    )
    return (
        output,
        gradient,
        stacked_out[0],
        stacked_out[1],
        stacked_out[2],
        stacked_out[3],
        stacked_out[4],
        stacked_out[5],
        stacked_out[6],
        stacked_out[7],
    )


def solution(mesh):
    split = Mesh(
        mesh.devices.reshape(mesh.shape["dp"], 2, 4, 2), ("dp", "tensor_0", "tensor_1", "tensor_2")
    )
    placed = (
        P(TENSOR, "dp", None),
        P("dp", None),
        P(TENSOR, "dp", None),
        P(None, None, "dp", TENSOR),
        P(None, None, TENSOR, "dp"),
        P(None, TENSOR, "dp"),
        P(None, "dp", TENSOR),
        P(None, TENSOR, "dp"),
        P(None, TENSOR, "dp"),
        P(None, None, "dp"),
        P(None, None, "dp"),
    )
    return jax.shard_map(
        on_device,
        mesh=split,
        in_specs=placed,
        out_specs=(
            P(TENSOR, "dp", None),
            P(TENSOR, "dp", None),
            P(None, None, "dp", TENSOR),
            P(None, None, TENSOR, "dp"),
            P(None, TENSOR, "dp"),
            P(None, "dp", TENSOR),
            P(None, TENSOR, "dp"),
            P(None, TENSOR, "dp"),
            P(None, None, "dp"),
            P(None, None, "dp"),
        ),
        check_vma=False,
    )
```

profile of v0, /device:TPU:0, one launch (start us, length us, event | category | flops | bytes accessed | tf_op | source)
XLA Modules:
  0.0 1355.8 jit_solution(12972840692710857035)
XLA Ops:
  13.4 26.3 %all_gather.36 = bf16[262,1024]{1,0:T(8,128)(2,1)S(1)} all-gather(bf16[262,128]{1,0:T(8,128)(2,1)S(1)} %pad_maximum_fusion.2), channel_id=1, replica_groups=mesh['dp'=8,'tensor_0'=2,'tensor_1'=4,'tensor_2'=2] {'dp'}, dimensions={1}, use_global_device_ids=true | all-gather | bytes 603648 | tf_op jit(solution)/shard_map/all_gather | solution.py:55
  52.1 41.1 %all-gather.1 = bf16[1,2,1,64]{2,1,0,3:T(2,128)(2,1)S(1)} all-gather(bf16[1,2,1,8]{2,1,0,3:T(2,128)(2,1)S(1)} %copy.597), channel_id=3, replica_groups=mesh['dp'=8,'tensor_0'=2,'tensor_1'=4,'tensor_2'=2] {'dp'}, dimensions={3}, use_global_device_ids=true | all-gather | bytes 288 | tf_op jit(solution)/shard_map/all_gather | solution.py:240
  93.8 24.4 %all-gather.2 = bf16[1,64,1024]{2,1,0:T(8,128)(2,1)S(1)} all-gather(bf16[1,64,128]{2,1,0:T(8,128)(2,1)S(1)} %get-tuple-element.1011), channel_id=4, replica_groups=mesh['dp'=8,'tensor_0'=2,'tensor_1'=4,'tensor_2'=2] {'dp'}, dimensions={2}, use_global_device_ids=true | all-gather | bytes 147456 | tf_op jit(solution)/shard_map/all_gather | solution.py:241
  119.3 24.6 %all-gather = bf16[1,3,1024,64]{2,3,1,0:T(8,128)(2,1)S(1)} all-gather(bf16[1,3,128,64]{2,3,1,0:T(8,128)(2,1)S(1)} %get-tuple-element.1009), channel_id=2, replica_groups=mesh['dp'=8,'tensor_0'=2,'tensor_1'=4,'tensor_2'=2] {'dp'}, dimensions={2}, use_global_device_ids=true | all-gather | bytes 442368 | tf_op jit(solution)/shard_map/all_gather | solution.py:239
  156.2 16.6 %while.107 = (s32[]{:T(128)}, bf16[2,1024,64]{2,1,0:T(8,128)(2,1)S(1)}, f32[2,1024]{1,0:T(2,128)}, bf16[2,1024,64]{2,1,0:T(8,128)(2,1)S(1)}, s32[2,1024]{1,0:T(2...) while((s32[]{:T(128)}, ...), condition=%wide.region_7.8_spmd, body=%wide.region_2.7_spmd.sunk | while | flops 139984896 | bytes 8710612 | solution.py:278
  187.1 35.4 %all_to_all.174 = bf16[8,64,2,1024]{3,1,2,0:T(8,128)(2,1)S(1)} all-to-all(bf16[8,64,2,1024]{3,1,2,0:T(8,128)(2,1)S(1)} %copy.461), channel_id=1, replica_groups=mesh['dp'=8,'tensor_0'=2,'tensor_1'=4,'tensor_2'=2] {'tensor_0','tensor_1'}, dimensions={0} | all-to-all | bytes 4194304 | tf_op jit(solution)/shard_map/all_to_all | solution.py:49
  231.5 33.6 %all-reduce.5 = (bf16[256]{0:T(256)(128)(2,1)S(1)}, bf16[256]{0:T(256)(128)(2,1)}) all-reduce(bf16[256]{0:T(256)(128)(2,1)S(1)} %dynamic-update-slice, bf16[256]{0:T(256)(128)(2,1)S(1)} %dynamic-update-slice.1), channel_id=6, replica_groups=mesh['dp'=8,'tensor_0'=2,'tensor_1'=4,'tensor_2'=2] {'dp'}, use_global_device_ids=true, to_apply=%add | all-reduce | flops 512 | bytes 2048
  265.7 29.2 %all-gather.3 = bf16[1,1024,256]{2,1,0:T(8,128)(2,1)S(1)} all-gather(bf16[1,128,256]{2,1,0:T(8,128)(2,1)S(1)} %get-tuple-element.1005), channel_id=5, replica_groups=mesh['dp'=8,'tensor_0'=2,'tensor_1'=4,'tensor_2'=2] {'dp'}, dimensions={1}, use_global_device_ids=true | all-gather | bytes 589824 | tf_op jit(solution)/shard_map/all_gather | solution.py:242
  328.5 43.3 %all_gather.42 = bf16[262,1024]{1,0:T(8,128)(2,1)S(1)} all-gather(bf16[262,128]{1,0:T(8,128)(2,1)S(1)} %pad_maximum_fusion.3), channel_id=1, replica_groups=mesh['dp'=8,'tensor_0'=2,'tensor_1'=4,'tensor_2'=2] {'dp'}, dimensions={1}, use_global_device_ids=true | all-gather | bytes 603648 | tf_op jit(solution)/shard_map/all_gather | solution.py:55
  383.1 41.7 %all-gather.6 = bf16[1,2,1,64]{2,1,0,3:T(2,128)(2,1)S(1)} all-gather(bf16[1,2,1,8]{2,1,0,3:T(2,128)(2,1)S(1)} %copy.598), channel_id=8, replica_groups=mesh['dp'=8,'tensor_0'=2,'tensor_1'=4,'tensor_2'=2] {'dp'}, dimensions={3}, use_global_device_ids=true | all-gather | bytes 288 | tf_op jit(solution)/shard_map/all_gather | solution.py:240
  424.9 26.0 %all-gather.7 = bf16[1,64,1024]{2,1,0:T(8,128)(2,1)} all-gather(bf16[1,64,128]{2,1,0:T(8,128)(2,1)S(1)} %copy-done.87), channel_id=9, replica_groups=mesh['dp'=8,'tensor_0'=2,'tensor_1'=4,'tensor_2'=2] {'dp'}, dimensions={2}, use_global_device_ids=true | all-gather | bytes 147456 | tf_op jit(solution)/shard_map/all_gather | solution.py:241
  451.5 24.4 %all-gather.5 = bf16[1,3,1024,64]{2,3,1,0:T(8,128)(2,1)S(1)} all-gather(bf16[1,3,128,64]{2,3,1,0:T(8,128)(2,1)S(1)} %copy-done.70), channel_id=7, replica_groups=mesh['dp'=8,'tensor_0'=2,'tensor_1'=4,'tensor_2'=2] {'dp'}, dimensions={2}, use_global_device_ids=true | all-gather | bytes 442368 | tf_op jit(solution)/shard_map/all_gather | solution.py:239
  490.1 27.0 %while.109 = (s32[]{:T(128)}, bf16[2,1024,64]{2,1,0:T(8,128)(2,1)S(1)}, f32[2,1024]{1,0:T(2,128)}, bf16[2,1024,64]{2,1,0:T(8,128)(2,1)S(1)}, s32[2,1024]{1,0:T(2...) while((s32[]{:T(128)}, ...), condition=%wide.region_21.22_spmd, body=%wide.region_16.21_spmd.sunk | while | flops 139984896 | bytes 8710612 | solution.py:278
  490.8 10.6 while.115
  504.3 10.6 while.115
  545.5 18.4 %all-to-all-done.16 = bf16[8,64,2,1024]{3,1,2,0:T(8,128)(2,1)} async-done(((bf16[8,64,2,1024]{3,1,2,0:T(8,128)(2,1)}), bf16[8,64,2,1024]{3,1,2,0:T(8,128)(2,1)}, u32[]{:S(2)}, u32[]{:S(2)}) %all-to-all-start.16) | async-done | bytes 2097184 | tf_op jit(solution)/shard_map/all_to_all | solution.py:15
  571.8 23.6 %all-to-all-done.11 = bf16[8,64,2,1024]{3,1,2,0:T(8,128)(2,1)} async-done(((bf16[8,64,2,1024]{3,1,2,0:T(8,128)(2,1)}), bf16[8,64,2,1024]{3,1,2,0:T(8,128)(2,1)}, u32[]{:S(2)}, u32[]{:S(2)}) %all-to-all-start.11) | async-done | bytes 2097184 | tf_op jit(solution)/shard_map/all_to_all | solution.py:49
  616.2 48.2 %all-gather.8 = bf16[1,1024,256]{2,1,0:T(8,128)(2,1)} all-gather(bf16[1,128,256]{2,1,0:T(8,128)(2,1)S(1)} %copy-done.66), channel_id=10, replica_groups=mesh['dp'=8,'tensor_0'=2,'tensor_1'=4,'tensor_2'=2] {'dp'}, dimensions={1}, use_global_device_ids=true | all-gather | bytes 589824 | tf_op jit(solution)/shard_map/all_gather | solution.py:242
  725.2 18.6 %all-to-all-done.19 = bf16[8,64,2,1024]{3,1,2,0:T(8,128)(2,1)S(1)} async-done(((bf16[8,64,2,1024]{3,1,2,0:T(8,128)(2,1)}), bf16[8,64,2,1024]{3,1,2,0:T(8,128)(2,1)S(1)}, u32[]{:S(2)}, u32[]{:S(2)}) %all-to-all-start.19) | async-done | bytes 2097184 | tf_op jit(solution)/shard_map/all_to_all | solution.py:49
  750.5 24.8 %all-to-all-done.15 = bf16[8,64,2,1024]{3,1,2,0:T(8,128)(2,1)} async-done(((bf16[8,64,2,1024]{3,1,2,0:T(8,128)(2,1)}), bf16[8,64,2,1024]{3,1,2,0:T(8,128)(2,1)}, u32[]{:S(2)}, u32[]{:S(2)}) %all-to-all-start.15) | async-done | bytes 2097184 | tf_op jit(solution)/shard_map/all_to_all | solution.py:49
  786.2 26.6 %all-to-all-done.20 = bf16[8,64,2,1024]{3,1,2,0:T(8,128)(2,1)S(1)} async-done(((bf16[8,64,2,1024]{3,1,2,0:T(8,128)(2,1)}), bf16[8,64,2,1024]{3,1,2,0:T(8,128)(2,1)S(1)}, u32[]{:S(2)}, u32[]{:S(2)}) %all-to-all-start.20) | async-done | bytes 2097184 | tf_op jit(solution)/shard_map/all_to_all | solution.py:15
  825.7 27.1 %while.111 = (s32[]{:T(128)}, bf16[2,1024,64]{1,2,0:T(8,128)(2,1)}, bf16[2,1024,64]{1,2,0:T(8,128)(2,1)}, bf16[2,1024,64]{1,2,0:T(8,128)(2,1)}, bf16[2,1024,64]{...) while((s32[]{:T(128)}, bf16[2,1024,64]{1,2,0:T(8,128)(2,1)}, ...), condition=%wide.region_36.37_spmd, body=%wide.region_32.36_spmd.sunk | while | flops 342196224 | bytes 21406268 | solution.py:367
  868.2 33.2 %all_to_all.183 = bf16[8,64,2,1024]{3,1,2,0:T(8,128)(2,1)S(1)} all-to-all(bf16[8,64,2,1024]{3,1,2,0:T(8,128)(2,1)S(1)} %copy.506), channel_id=1, replica_groups=mesh['dp'=8,'tensor_0'=2,'tensor_1'=4,'tensor_2'=2] {'tensor_0','tensor_1'}, dimensions={0} | all-to-all | bytes 4194304 | tf_op jit(solution)/shard_map/all_to_all | solution.py:49
  919.0 16.8 %all-to-all-done.24 = bf16[8,64,2,1024]{3,1,2,0:T(8,128)(2,1)} async-done(((bf16[8,64,2,1024]{3,1,2,0:T(8,128)(2,1)}), bf16[8,64,2,1024]{3,1,2,0:T(8,128)(2,1)}, u32[]{:S(2)}, u32[]{:S(2)}) %all-to-all-start.24) | async-done | bytes 2097184 | tf_op jit(solution)/shard_map/all_to_all | solution.py:15
  986.5 10.8 all-to-all-done.27
  1026.7 27.2 %reduce-scatter.39.cloned.1.call-done = bf16[128,64]{1,0:T(8,128)(2,1)} async-done(((bf16[1024,64]{1,0:T(8,128)(2,1)}), bf16[128,64]{1,0:T(8,128)(2,1)}) %reduce-scatter.39.cloned.1.call-update) | async-done | bytes 16400
  1055.3 37.4 %reduce-scatter.35.cloned.1.call-done = bf16[128,192]{1,0:T(8,128)(2,1)} async-done(((bf16[1024,192]{1,0:T(8,128)(2,1)}), bf16[128,192]{1,0:T(8,128)(2,1)}) %reduce-scatter.35.cloned.1.call-update) | async-done | bytes 49168
  1115.1 26.9 %while.113 = (s32[]{:T(128)}, bf16[2,1024,64]{1,2,0:T(8,128)(2,1)}, bf16[2,1024,64]{1,2,0:T(8,128)(2,1)}, bf16[2,1024,64]{1,2,0:T(8,128)(2,1)}, bf16[2,1024,64]{...) while((s32[]{:T(128)}, bf16[2,1024,64]{1,2,0:T(8,128)(2,1)}, ...), condition=%wide.region_49.50_spmd, body=%wide.region_45.49_spmd.sunk | while | flops 342196224 | bytes 21406268 | solution.py:367
  1171.5 37.7 %reduce-scatter.29.cloned.1.call-done = bf16[128,256]{1,0:T(8,128)(2,1)} async-done(((bf16[1024,256]{1,0:T(8,128)(2,1)}), bf16[128,256]{1,0:T(8,128)(2,1)}) %reduce-scatter.29.cloned.1.call-update) | async-done | bytes 65552 | tf_op jit(solution)/shard_map/reduce_scatter | solution.py:399
  1221.1 16.6 %all-reduce.4 = (bf16[2,1,64]{2,1,0:T(2,128)(2,1)S(1)}, bf16[2,1,64]{2,1,0:T(2,128)(2,1)S(1)}) all-reduce(bf16[2,1,64]{2,1,0:T(2,128)(2,1)S(1)} %copy-done.122, bf16[2,1,64]{2,1,0:T(2,128)(2,1)S(1)} %pad_maximum_fusion.6), channel_id=15, replica_groups=mesh['dp'=8,'tensor_0'=2,'tensor_1'=4,'tensor_2'=2] {'dp'}, use_global_device_ids=true, to_apply=%region_61.62.clone | all-reduce | flops 256 | bytes 1024
  1252.9 37.4 %reduce-scatter.33.cloned.1.call-done = bf16[128,192]{1,0:T(8,128)(2,1)} async-done(((bf16[1024,192]{1,0:T(8,128)(2,1)}), bf16[128,192]{1,0:T(8,128)(2,1)}) %reduce-scatter.33.cloned.1.call-update) | async-done | bytes 49168
  1293.6 36.3 %reduce-scatter.45.cloned.1.call-done = bf16[128,262]{1,0:T(8,128)(2,1)} async-done(((bf16[1024,262]{1,0:T(8,128)(2,1)}), bf16[128,262]{1,0:T(8,128)(2,1)}) %reduce-scatter.45.cloned.1.call-update) | async-done | bytes 67088
  (853 shorter events, 616.3 us)
Async XLA Ops:
  40.4 183.5 %copy-start.83 = (f32[1,1024]{1,0:T(1,128)}, f32[1,1024]{1,0:T(1,128)S(1)}, u32[]{:S(2)}) copy-start(f32[1,1024]{1,0:T(1,128)S(1)} %get-tuple-element.991) | copy-start | bytes 12292
  43.8 100.1 %all-to-all-start = ((bf16[8,64,2,1024]{3,1,2,0:T(8,128)(2,1)}), bf16[8,64,2,1024]{3,1,2,0:T(8,128)(2,1)S(1)}, u32[]{:S(2)}, u32[]{:S(2)}) async-start(bf16[8,64,2,1024]{3,1,2,0:T(8,128)(2,1)} %broadcast_in_dim.131), calls=%async_computation | async-start | bytes 4194304 | tf_op jit(solution)/shard_map/all_to_all | solution.py:15
  223.6 149.2 %copy-start.11 = (f32[64,2,1024]{2,0,1:T(8,128)}, f32[64,2,1024]{2,0,1:T(8,128)S(1)}, u32[]{:S(2)}) copy-start(f32[64,2,1024]{2,0,1:T(8,128)S(1)} %get-tuple-element.964) | copy-start | bytes 1572868
  225.7 69.2 %all-to-all-start.4 = ((bf16[8,64,2,1024]{3,1,2,0:T(8,128)(2,1)}), bf16[8,64,2,1024]{3,1,2,0:T(8,128)(2,1)S(1)}, u32[]{:S(2)}, u32[]{:S(2)}) async-start(bf16[8,64,2,1024]{3,1,2,0:T(8,128)(2,1)} %broadcast_in_dim.133), calls=%async_computation.4 | async-start | bytes 4194304 | tf_op jit(solution)/shard_map/all_to_all | solution.py:15
  321.5 50.9 %all-to-all-start.7 = ((bf16[8,64,2,1024]{3,1,2,0:T(8,128)(2,1)}), bf16[8,64,2,1024]{3,1,2,0:T(8,128)(2,1)S(1)}, u32[]{:S(2)}, u32[]{:S(2)}) async-start(bf16[8,64,2,1024]{3,1,2,0:T(8,128)(2,1)} %copy.467), calls=%async_computation.7 | async-start | bytes 4194304 | tf_op jit(solution)/shard_map/all_to_all | solution.py:49
  373.0 234.2 %copy-start.2 = (f32[64,2,1024]{2,0,1:T(8,128)}, f32[64,2,1024]{2,0,1:T(8,128)S(1)}, u32[]{:S(2)}) copy-start(f32[64,2,1024]{2,0,1:T(8,128)S(1)} %get-tuple-element.962) | copy-start | bytes 1572868
  375.1 100.8 %all-to-all-start.8 = ((bf16[8,64,2,1024]{3,1,2,0:T(8,128)(2,1)}), bf16[8,64,2,1024]{3,1,2,0:T(8,128)(2,1)}, u32[]{:S(2)}, u32[]{:S(2)}) async-start(bf16[8,64,2,1024]{3,1,2,0:T(8,128)(2,1)} %broadcast_in_dim.135), calls=%async_computation.8 | async-start | bytes 4194304 | tf_op jit(solution)/shard_map/all_to_all | solution.py:15
  530.1 33.8 %all-to-all-start.16 = ((bf16[8,64,2,1024]{3,1,2,0:T(8,128)(2,1)}), bf16[8,64,2,1024]{3,1,2,0:T(8,128)(2,1)}, u32[]{:S(2)}, u32[]{:S(2)}) async-start(bf16[8,64,2,1024]{3,1,2,0:T(8,128)(2,1)} %broadcast_in_dim.139), calls=%async_computation.16 | async-start | bytes 4194304 | tf_op jit(solution)/shard_map/all_to_all | solution.py:15
  563.9 31.5 %all-to-all-start.11 = ((bf16[8,64,2,1024]{3,1,2,0:T(8,128)(2,1)}), bf16[8,64,2,1024]{3,1,2,0:T(8,128)(2,1)}, u32[]{:S(2)}, u32[]{:S(2)}) async-start(bf16[8,64,2,1024]{3,1,2,0:T(8,128)(2,1)} %copy.478), calls=%async_computation.11 | async-start | bytes 4194304 | tf_op jit(solution)/shard_map/all_to_all | solution.py:49
  599.6 10.1 all-to-all-start.17
  611.3 58.0 %all-to-all-start.12 = ((bf16[8,64,2,1024]{3,1,2,0:T(8,128)(2,1)}), bf16[8,64,2,1024]{3,1,2,0:T(8,128)(2,1)S(1)}, u32[]{:S(2)}, u32[]{:S(2)}) async-start(bf16[8,64,2,1024]{3,1,2,0:T(8,128)(2,1)} %broadcast_in_dim.137), calls=%async_computation.12 | async-start | bytes 4194304 | tf_op jit(solution)/shard_map/all_to_all | solution.py:15
  698.8 11.1 all-to-all-start.14
  709.8 34.0 %all-to-all-start.19 = ((bf16[8,64,2,1024]{3,1,2,0:T(8,128)(2,1)}), bf16[8,64,2,1024]{3,1,2,0:T(8,128)(2,1)S(1)}, u32[]{:S(2)}, u32[]{:S(2)}) async-start(bf16[8,64,2,1024]{3,1,2,0:T(8,128)(2,1)} %copy.493), calls=%async_computation.19 | async-start | bytes 4194304 | tf_op jit(solution)/shard_map/all_to_all | solution.py:49
  743.9 31.5 %all-to-all-start.15 = ((bf16[8,64,2,1024]{3,1,2,0:T(8,128)(2,1)}), bf16[8,64,2,1024]{3,1,2,0:T(8,128)(2,1)}, u32[]{:S(2)}, u32[]{:S(2)}) async-start(bf16[8,64,2,1024]{3,1,2,0:T(8,128)(2,1)} %copy.484), calls=%async_computation.15 | async-start | bytes 4194304 | tf_op jit(solution)/shard_map/all_to_all | solution.py:49
  781.5 31.4 %all-to-all-start.20 = ((bf16[8,64,2,1024]{3,1,2,0:T(8,128)(2,1)}), bf16[8,64,2,1024]{3,1,2,0:T(8,128)(2,1)S(1)}, u32[]{:S(2)}, u32[]{:S(2)}) async-start(bf16[8,64,2,1024]{3,1,2,0:T(8,128)(2,1)} %broadcast_in_dim.143), calls=%async_computation.20 | async-start | bytes 4194304 | tf_op jit(solution)/shard_map/all_to_all | solution.py:15
  903.8 100.4 %copy-start.34 = (f32[64,2,1024]{2,0,1:T(8,128)}, f32[64,2,1024]{2,0,1:T(8,128)S(1)}, u32[]{:S(2)}) copy-start(f32[64,2,1024]{2,0,1:T(8,128)S(1)} %get-tuple-element.950) | copy-start | bytes 1572868
  905.5 30.4 %all-to-all-start.24 = ((bf16[8,64,2,1024]{3,1,2,0:T(8,128)(2,1)}), bf16[8,64,2,1024]{3,1,2,0:T(8,128)(2,1)}, u32[]{:S(2)}, u32[]{:S(2)}) async-start(bf16[8,64,2,1024]{3,1,2,0:T(8,128)(2,1)} %broadcast_in_dim.147), calls=%async_computation.24 | async-start | bytes 4194304 | tf_op jit(solution)/shard_map/all_to_all | solution.py:15
  910.0 74.7 %reduce-scatter.47.cloned.1.call-start = ((), (), s32[]{:S(2)}) async-start(), calls=%async_computation.53 | async-start | bytes 884736
  966.0 31.2 %all-to-all-start.27 = ((bf16[8,64,2,1024]{3,1,2,0:T(8,128)(2,1)}), bf16[8,64,2,1024]{3,1,2,0:T(8,128)(2,1)S(1)}, u32[]{:S(2)}, u32[]{:S(2)}) async-start(bf16[8,64,2,1024]{3,1,2,0:T(8,128)(2,1)} %copy.512), calls=%async_computation.27 | async-start | bytes 4194304 | tf_op jit(solution)/shard_map/all_to_all | solution.py:49
  970.4 51.2 %reduce-scatter.43.cloned.1.call-start = ((), (), s32[]{:S(2)}) async-start(), calls=%async_computation.51 | async-start | bytes 73728
  971.2 82.6 %reduce-scatter.39.cloned.1.call-start = ((), (), s32[]{:S(2)}) async-start(), calls=%async_computation.49 | async-start | bytes 294912
  975.3 117.5 %reduce-scatter.35.cloned.1.call-start = ((), (), s32[]{:S(2)}) async-start(), calls=%async_computation.47 | async-start | bytes 589824
  998.0 12.3 all-to-all-start.33
  1012.0 90.1 %all-to-all-start.28 = ((bf16[8,64,2,1024]{3,1,2,0:T(8,128)(2,1)}), bf16[8,64,2,1024]{3,1,2,0:T(8,128)(2,1)S(1)}, u32[]{:S(2)}, u32[]{:S(2)}) async-start(bf16[8,64,2,1024]{3,1,2,0:T(8,128)(2,1)} %broadcast_in_dim.151), calls=%async_computation.28 | async-start | bytes 4194304 | tf_op jit(solution)/shard_map/all_to_all | solution.py:15
  1015.7 154.4 %reduce-scatter.41.cloned.1.call-start = ((), (), s32[]{:S(2)}) async-start(), calls=%async_computation.50 | async-start | bytes 73728
  1017.2 154.3 %reduce-scatter.31.cloned.1.call-start = ((), (), s32[]{:S(2)}) async-start(), calls=%async_computation.45 | async-start | bytes 589824 | tf_op jit(solution)/shard_map/reduce_scatter | solution.py:399
  1021.6 187.6 %reduce-scatter.29.cloned.1.call-start = ((), (), s32[]{:S(2)}) async-start(), calls=%async_computation.44 | async-start | bytes 589824 | tf_op jit(solution)/shard_map/reduce_scatter | solution.py:399
  1158.8 79.0 %all-to-all-start.31 = ((bf16[8,64,2,1024]{3,1,2,0:T(8,128)(2,1)}), bf16[8,64,2,1024]{3,1,2,0:T(8,128)(2,1)}, u32[]{:S(2)}, u32[]{:S(2)}) async-start(bf16[8,64,2,1024]{3,1,2,0:T(8,128)(2,1)} %copy.525), calls=%async_computation.31 | async-start | bytes 4194304 | tf_op jit(solution)/shard_map/all_to_all | solution.py:49
  1165.6 85.8 %reduce-scatter.37.cloned.1.call-start = ((), (), s32[]{:S(2)}) async-start(), calls=%async_computation.48 | async-start | bytes 294912
  1215.2 75.1 %reduce-scatter.33.cloned.1.call-start = ((), (), s32[]{:S(2)}) async-start(), calls=%async_computation.46 | async-start | bytes 589824
  1220.9 108.9 %reduce-scatter.45.cloned.1.call-start = ((), (), s32[]{:S(2)}) async-start(), calls=%async_computation.52 | async-start | bytes 884736
  1333.2 14.2 %all-to-all-start.32 = ((f32[16,1,768]{2,1,0:T(1,128)}), f32[16,1,768]{2,1,0:T(1,128)S(1)}, u32[]{:S(2)}, u32[]{:S(2)}) async-start(f32[16,1,768]{2,1,0:T(1,128)} %broadcast_in_dim.155), calls=%async_computation.34 | async-start | bytes 98304 | tf_op jit(solution)/shard_map/all_to_all | solution.py:15
  (137 other events, 1727.0 us)
Sparse Core Ops, SparseCore 0:
  919.1 41.0 reduce-scatter.46
  974.3 40.2 reduce-scatter.42
  1016.9 36.8 reduce-scatter.38
  1056.2 36.4 reduce-scatter.34
  1094.9 35.8 reduce-scatter.40
  1133.1 36.6 reduce-scatter.30
  1172.2 36.9 reduce-scatter.28
  1215.3 36.0 reduce-scatter.36
  1253.8 36.4 reduce-scatter.32
  1292.6 37.1 reduce-scatter.44
where the time goes:
time: 1370 us; the launch traced here: 1360 us
  blocking collectives  556 us (41%)
  waiting for transfers between devices  335 us (24%)
  local copies, waits for them, and re-layouts  166 us (12%)
  starting transfers between devices  102 us (7%)
  matrix products  91.1 us (7%)
  other arithmetic  75.2 us (5%)
  between operations  17.9 us (1%)
    unnamed x18, waiting for transfers between devices  145 us
    all_gather x2, blocking collectives, fetch_forward(): lax.all_gather(b_qv[layer_index], 'dp', axis=2, tiled=True)  82.8 us
    all_to_all x6, waiting for transfers between devices, sum_in_two_steps(): lax.all_to_all(own.astype(jnp.bfloat16), far, 0, 0, tiled=True)  77.8 us
    all_gather x2, blocking collectives, fetch_forward(): lax.all_gather(w_fc[layer_index], 'dp', axis=0, tiled=True)  77.4 us
    all_to_all x11, waiting for transfers between devices, copy_for_each(): lax.all_to_all(jnp.broadcast_to(value[None], (count, *value.shape)), axis...  74.6 us
    all_gather x2, blocking collectives, in_one_piece(): out, at, done = (lax.all_gather(both, axis, axis=dim, tiled=True), 0, [])  69.6 us
    all_to_all x2, blocking collectives, sum_in_two_steps(): lax.all_to_all(own.astype(jnp.bfloat16), far, 0, 0, tiled=True)  68.7 us
    all_to_all x11, starting transfers between devices, copy_for_each(): lax.all_to_all(jnp.broadcast_to(value[None], (count, *value.shape)), axis...  60.5 us
  transfers between devices with their start and end apart: 28, of which 16 were waited for; matrix products, arithmetic and copies ran while one was open for 13% of the time, Pallas kernels for 0%

commit v1 on v0

v1 whole, which is shorter than its diff:
```python
import jax
import jax.numpy as jnp
from jax import lax
from jax.experimental import pallas as pl
from jax.experimental.pallas import tpu as pltpu
from jax.sharding import Mesh
from jax.sharding import PartitionSpec as P

EPS = 1e-05
F32 = jnp.float32
BF16 = jnp.bfloat16
X = ("xl", "xh")
HD = 64
NT = (((1,), (1,)), ((), ()))
TN = (((0,), (0,)), ((), ()))


def swap(value, axis, mask):
    count = lax.axis_size(axis)
    return lax.ppermute(value, axis, [(i, i ^ mask) for i in range(count)])


def gather_plane(block):
    m, r, c = block.shape
    one, three, two = (swap(block, "y", k) for k in (1, 3, 2))
    ys = jnp.stack([block, one, two, three], axis=1)
    low, both, high = (swap(ys, X, k) for k in (2, 3, 1))
    own = jnp.stack([ys, low, high, both], axis=1).reshape(m, 2, 8, r, c)
    other = swap(own, "c", 1)
    return jnp.concatenate([own, other], axis=1)


def scatter_plane(own, other, send_type):
    m, _, _, r, c = own.shape
    both = own + swap(other.astype(send_type), "c", 1).astype(F32)
    parts = both.reshape(m, 4, 4, r, c)
    total = parts[:, 0]
    for k, mask in ((1, 2), (3, 3), (2, 1)):
        total = total + swap(parts[:, k].astype(send_type), X, mask).astype(F32)
    final = total[:, 0]
    for k in (1, 3, 2):
        final = final + swap(total[:, k].astype(send_type), "y", k).astype(F32)
    return final


def gather_tokens(own):
    t, n = own.shape
    got = {0: own}
    for k in (1, 3, 2):
        got[k] = swap(own, "z", k)
    return jnp.stack([got[k].reshape(2, t // 2, n) for k in range(4)], axis=1).reshape(4 * t, n)


def scatter_tokens(partial):
    t, n = partial.shape
    parts = partial.reshape(2, 4, t // 8, n)
    total = parts[:, 0].reshape(t // 4, n)
    for k in (1, 3, 2):
        total = total + swap(parts[:, k].reshape(t // 4, n).astype(BF16), "z", k).astype(F32)
    return total


def relative(value, d_own):
    for bit in (1, 2, 4):
        half = 128 * bit
        shape = value.shape
        cut = value.reshape(*shape[:-1], shape[-1] // (2 * half), 2, half)
        turned = jnp.concatenate([cut[..., 1:, :], cut[..., :1, :]], axis=-2).reshape(shape)
        value = jnp.where((d_own & bit) != 0, turned, value)
    return value


def norm_parts(values):
    center = values - jnp.mean(values, axis=-1, keepdims=True)
    spread = jnp.mean(center * center, axis=-1, keepdims=True)
    rstd = lax.rsqrt(spread + EPS)
    return center * rstd, rstd


def norm_rows(values, gain, shift):
    return (norm_parts(values)[0] * gain + shift).astype(BF16)


def norm_back(values, gain, grad):
    xhat, rstd = norm_parts(values)
    dxhat = grad * gain
    into = dxhat - jnp.mean(dxhat, axis=-1, keepdims=True)
    into = (into - xhat * jnp.mean(dxhat * xhat, axis=-1, keepdims=True)) * rstd
    return into, jnp.sum(grad * xhat, axis=0), jnp.sum(grad, axis=0)


def gelu_and_slope(pre):
    a, b = 0.7978845608028654, 0.044715
    square = pre * pre
    th = jnp.tanh(a * pre * (1.0 + b * square))
    value = 0.5 * pre * (1.0 + th)
    slope = 0.5 * (1.0 + th) + 0.5 * pre * (1.0 - th * th) * a * (1.0 + 3.0 * b * square)
    return value, slope


def head_keys(kv_ref, par_ref):
    half = kv_ref.shape[1] // 2
    return jnp.concatenate(
        [kv_ref[0, :half], par_ref[0, :half], kv_ref[0, half:], par_ref[0, half:]], axis=0
    )


def attend_kernel(kv_ref, par_ref, q_ref, bias_ref, mixed_ref, lse_ref):
    kv = head_keys(kv_ref, par_ref)
    count = q_ref.shape[1]
    half = count // 2
    for part in range(2):
        rows = slice(part * half, (part + 1) * half)
        seen = count * (part + 1)
        keys = kv[:seen]
        scores = lax.dot_general(q_ref[0, rows], keys, NT, preferred_element_type=F32)
        scores = scores + bias_ref[rows, :seen]
        highest = jnp.max(scores, axis=1, keepdims=True)
        raised = jnp.exp(scores - highest)
        totals = jnp.sum(raised, axis=1, keepdims=True)
        probs = (raised * (1.0 / totals)).astype(BF16)
        mixed = jnp.dot(probs, keys, preferred_element_type=F32)
        lane = lax.broadcasted_iota(jnp.int32, mixed.shape, 1)
        mixed_ref[0, rows] = jnp.where(lane >= HD, mixed, 0.0).astype(BF16)
        lse_ref[0, rows] = highest + jnp.log(totals)


def attend_back_kernel(
    kv_ref, par_ref, q_ref, bias_ref, lse_ref, dm_ref, dq_ref, own_ref, other_ref
):
    kv = head_keys(kv_ref, par_ref)
    count = q_ref.shape[1]
    half = count // 2
    sums = []
    for part in range(2):
        rows = slice(part * half, (part + 1) * half)
        seen = count * (part + 1)
        keys = kv[:seen]
        queries = q_ref[0, rows]
        grad = dm_ref[0, rows]
        scores = lax.dot_general(queries, keys, NT, preferred_element_type=F32)
        probs = jnp.exp(scores + bias_ref[rows, :seen] - lse_ref[0, rows])
        dprobs = lax.dot_general(grad, keys, NT, preferred_element_type=F32)
        inner = jnp.sum(probs * dprobs, axis=1, keepdims=True)
        dscores = (probs * (dprobs - inner)).astype(BF16)
        low = probs.astype(BF16)
        dq = jnp.dot(dscores, keys, preferred_element_type=F32) * 0.125
        lane = lax.broadcasted_iota(jnp.int32, dq.shape, 1)
        dq_ref[0, rows] = jnp.where(lane < HD, dq, 0.0).astype(BF16)
        sums.append(
            lax.dot_general(dscores, queries, TN, preferred_element_type=F32)
            + lax.dot_general(low, grad, TN, preferred_element_type=F32)
        )
    low_keys = sums[0] + sums[1][:count]
    own_ref[0, :half] = low_keys[:half]
    other_ref[0, :half] = low_keys[half:].astype(BF16)
    own_ref[0, half:] = sums[1][count : count + half]
    other_ref[0, half:] = sums[1][count + half :].astype(BF16)


def head_spec(rows, index, lanes=128, column=0):
    return pl.BlockSpec((1, rows, lanes), lambda t: (index(t), 0, column))


def same(t):
    return t


def across(t):
    return lax.rem(t + 2, 4)


def attend(qkvo, par, bias):
    heads, count, _ = qkvo.shape
    area = heads * count * 2 * count
    return pl.pallas_call(
        attend_kernel,
        grid=(heads,),
        in_specs=[
            head_spec(count, same),
            head_spec(count, across),
            head_spec(count, same, column=1),
            pl.BlockSpec(bias.shape, lambda t: (0, 0)),
        ],
        out_specs=[head_spec(count, same), head_spec(count, same, lanes=1)],
        out_shape=[
            jax.ShapeDtypeStruct((heads, count, 128), BF16),
            jax.ShapeDtypeStruct((heads, count, 1), F32),
        ],
        compiler_params=pltpu.CompilerParams(vmem_limit_bytes=40 << 20),
        cost_estimate=pl.CostEstimate(
            flops=area * 512, bytes_accessed=6 << 20, transcendentals=area
        ),
    )(qkvo, par, qkvo, bias)


def attend_back(qkvo, par, bias, lse, grad):
    heads, count, _ = qkvo.shape
    area = heads * count * 2 * count
    return pl.pallas_call(
        attend_back_kernel,
        grid=(heads,),
        in_specs=[
            head_spec(count, same),
            head_spec(count, across),
            head_spec(count, same, column=1),
            pl.BlockSpec(bias.shape, lambda t: (0, 0)),
            head_spec(count, same, lanes=1),
            head_spec(count, same),
        ],
        out_specs=[head_spec(count, same)] * 3,
        out_shape=[
            jax.ShapeDtypeStruct((heads, count, 128), BF16),
            jax.ShapeDtypeStruct((heads, count, 128), F32),
            jax.ShapeDtypeStruct((heads, count, 128), BF16),
        ],
        compiler_params=pltpu.CompilerParams(vmem_limit_bytes=40 << 20),
        cost_estimate=pl.CostEstimate(
            flops=area * 1280, bytes_accessed=8 << 20, transcendentals=area
        ),
    )(qkvo, par, qkvo, bias, lse, grad)


def into_blocks(rows, weight):
    return jnp.einsum("nd,tdk->tnk", rows, weight, preferred_element_type=F32)


def out_of_blocks(blocks, weight):
    return jnp.einsum("tnk,tdk->nd", blocks, weight, preferred_element_type=F32)


def weight_grad(rows, blocks):
    return jnp.einsum("nd,tnk->tdk", rows, blocks, preferred_element_type=F32)


def on_device(
    tokens, segments, cotangent, w_qkv, b_qv, w_out, w_fc, b_fc, w_proj, norm_gains, shifts
):
    layers = w_qkv.shape[0]
    xl, y, xh, z, core = (lax.axis_index(a) for a in ("xl", "y", "xh", "z", "c"))
    d_own = xl * 4 + y
    first = xh == 0
    block, _, width = tokens.shape
    to_own = jnp.arange(8, dtype=jnp.int32) ^ d_own

    def by_row(value):
        kept = jnp.where(first, value[:, 0], value[:, 1])
        sent = jnp.where(first, value[:, 1], value[:, 0])
        got = swap(sent, "xh", 1)
        both = jnp.concatenate(
            [jnp.where(first, kept, got), jnp.where(first, got, kept)], axis=0
        )
        return relative(both, d_own)

    def by_position(value):
        value = relative(value, d_own)
        lower, upper = value[:block], value[block:]
        kept = jnp.where(first, lower, upper)
        got = swap(jnp.where(first, upper, lower).astype(BF16), "xh", 1).astype(value.dtype)
        return jnp.stack([jnp.where(first, kept, got), jnp.where(first, got, kept)], axis=1)

    attn_blocks = jnp.concatenate(
        [w_qkv[:, 1], w_qkv[:, 2], w_qkv[:, 0], jnp.swapaxes(w_out, 1, 2)], axis=2
    )
    proj_blocks = jnp.swapaxes(w_proj, 1, 2)
    small = jnp.concatenate(
        [
            jnp.pad(
                jnp.concatenate([b_qv.reshape(layers, 1, -1), b_fc.reshape(layers, 1, -1)], axis=2),
                ((0, 0), (0, 0), (0, 128 - 48)),
            ),
            norm_gains,
            shifts,
            jnp.zeros((layers, 1, 128), BF16),
        ],
        axis=1,
    )
    small_all = gather_plane(small)
    attn_w, fc_w, proj_w = [], [], []
    for i in range(layers):
        for store, source in ((attn_w, attn_blocks), (fc_w, w_fc), (proj_w, proj_blocks)):
            store.append(gather_plane(source[i][None]).reshape(4, width, 256))

    gains = jnp.swapaxes(small_all[:, 0, :, 1:3], 1, 2).reshape(layers, 2, width).astype(F32)
    shift = jnp.swapaxes(small_all[:, 0, :, 3:7], 1, 2).reshape(layers, 4, width).astype(F32)
    biases = jnp.take(small_all[:, :, :, 0, :48], to_own, axis=2).astype(F32)
    q_bias = biases[..., :8].reshape(layers, 4, HD)
    v_bias = biases[..., 8:16].reshape(layers, 4, HD)
    fc_bias = biases[..., 16:].reshape(layers, 4, 256)
    none = jnp.zeros_like(q_bias)
    qkvo_bias = jnp.concatenate([none, v_bias, q_bias, none], axis=2)
    column = jnp.arange(256)
    scale = jnp.where(column < 2 * HD, 1.0, jnp.where(column < 3 * HD, 0.125, 0.0)).astype(F32)

    seg_row = jnp.where(first, segments[0], segments[1])
    position = jnp.arange(seg_row.shape[0], dtype=jnp.int32)

    def at_core(value, which):
        cut = value.reshape(2, 4, 2, block)
        cut = jnp.where(which == 0, cut[:, :, 0], cut[:, :, 1])
        for bit in (1, 2):
            cut = jnp.where(
                (z & bit) != 0, cut[:, jnp.array([k ^ bit for k in range(4)])], cut
            )
        return cut.reshape(2, 4 * block)

    own_pos, own_seg = at_core(position, core), at_core(seg_row, core)
    par_pos, par_seg = at_core(position, 1 - core), at_core(seg_row, 1 - core)
    q_pos, q_seg = own_pos.reshape(-1, 1), own_seg.reshape(-1, 1)
    k_pos = jnp.concatenate([own_pos, par_pos], axis=1).reshape(1, -1)
    k_seg = jnp.concatenate([own_seg, par_seg], axis=1).reshape(1, -1)
    bias = jnp.where((q_seg == k_seg) & (q_pos >= k_pos), 0.0, -1e30).astype(F32)

    own_tokens = by_row(tokens)
    all_tokens = gather_tokens(own_tokens)
    residual = own_tokens.astype(F32)
    own_cotangent = by_row(cotangent)
    all_cotangent = gather_tokens(own_cotangent)

    kept = []
    for i in range(layers):
        attn_input = residual
        if i == 0:
            attn_rows = norm_rows(all_tokens.astype(F32), gains[i, 0], shift[i, 0])
        else:
            attn_rows = gather_tokens(norm_rows(residual, gains[i, 0], shift[i, 0]))
        qkvo = (
            (into_blocks(attn_rows, attn_w[i]) + qkvo_bias[i][:, None, :]) * scale
        ).astype(BF16)
        par = swap(qkvo[:, :, :128], "c", 1)
        mixed, lse = attend(qkvo, par, bias)
        attn_out = scatter_tokens(out_of_blocks(mixed, attn_w[i][:, :, 128:]))
        residual = residual + attn_out + shift[i, 2]
        mlp_input = residual
        mlp_rows = gather_tokens(norm_rows(residual, gains[i, 1], shift[i, 1]))
        pre = into_blocks(mlp_rows, fc_w[i]) + fc_bias[i][:, None, :]
        hidden = gelu_and_slope(pre)[0].astype(BF16)
        mlp_out = scatter_tokens(out_of_blocks(hidden, proj_w[i]))
        residual = residual + mlp_out + shift[i, 3]
        kept.append(
            (attn_input, attn_rows, qkvo, par, mixed, lse, mlp_input, mlp_rows, pre, hidden)
        )
    output = by_position(residual.astype(BF16))

    gradient = own_cotangent.astype(F32)
    big, gain_grads, shift_grads, bias_grads = [], [], [], []
    for i in reversed(range(layers)):
        attn_input, attn_rows, qkvo, par, mixed, lse, mlp_input, mlp_rows, pre, hidden = kept[i]
        low = gradient.astype(BF16)
        shift_mlp = jnp.sum(low.astype(F32), axis=0)
        grad_rows = all_cotangent if i == layers - 1 else gather_tokens(low)
        d_hidden = into_blocks(grad_rows, proj_w[i])
        d_pre = (d_hidden * gelu_and_slope(pre)[1]).astype(BF16)
        d_normed = scatter_tokens(out_of_blocks(d_pre, fc_w[i]))
        proj_grad = weight_grad(grad_rows, hidden)
        fc_grad = weight_grad(mlp_rows, d_pre)
        fc_bias_grad = jnp.sum(d_pre.astype(F32), axis=1)
        into, gain_mlp, shift_norm_mlp = norm_back(mlp_input, gains[i, 1], d_normed)
        gradient = gradient + into
        low = gradient.astype(BF16)
        shift_attn = jnp.sum(low.astype(F32), axis=0)
        grad_rows = gather_tokens(low)
        d_mixed = into_blocks(grad_rows, attn_w[i][:, :, 128:])
        d_mixed = jnp.where(jnp.arange(128) >= HD, d_mixed, 0.0).astype(BF16)
        dq, own_dkv, other_dkv = attend_back(qkvo, par, bias, lse, d_mixed)
        from_core = jnp.concatenate([(got := swap(other_dkv, "c", 1))[2:], got[:2]], axis=0)
        dkv = (own_dkv + from_core.astype(F32)).astype(BF16)
        d_qkvo = jnp.concatenate([dkv, dq], axis=2)
        d_normed = scatter_tokens(out_of_blocks(d_qkvo, attn_w[i]))
        mixed_wide = jnp.concatenate([jnp.zeros_like(mixed), mixed], axis=2)
        attn_grad = weight_grad(attn_rows, d_qkvo) + weight_grad(grad_rows, mixed_wide)
        qkvo_bias_grad = jnp.sum(d_qkvo.astype(F32), axis=1)
        into, gain_attn, shift_norm_attn = norm_back(attn_input, gains[i, 0], d_normed)
        gradient = gradient + into
        gain_grads.append(jnp.stack([gain_attn, gain_mlp]))
        shift_grads.append(jnp.stack([shift_norm_attn, shift_norm_mlp, shift_attn, shift_mlp]))
        bias_grads.append(
            jnp.concatenate(
                [
                    qkvo_bias_grad[:, 128:192].reshape(4, 8, 8),
                    qkvo_bias_grad[:, 64:128].reshape(4, 8, 8),
                    fc_bias_grad.reshape(4, 8, 32),
                ],
                axis=2,
            )
        )
        shards = []
        for grad in (attn_grad, fc_grad, proj_grad):
            cut = grad.reshape(1, 4, 8, 128, 256)
            shards.append(scatter_plane(cut[:, :2], cut[:, 2:], BF16)[0])
        big.append(shards)
    g_tokens = by_position(gradient)

    big, gain_grads, shift_grads, bias_grads = (
        a[::-1] for a in (big, gain_grads, shift_grads, bias_grads)
    )
    vectors = jnp.concatenate([jnp.stack(gain_grads), jnp.stack(shift_grads)], axis=1)
    vectors = jnp.swapaxes(vectors.reshape(layers, 6, 8, 128), 1, 2)
    vectors = jnp.broadcast_to(vectors[:, None], (layers, 4, 8, 6, 128))
    bias_rows = jnp.take(jnp.stack(bias_grads), to_own, axis=2)
    bias_rows = jnp.pad(bias_rows, ((0, 0), (0, 0), (0, 0), (0, 80)))[:, :, :, None]
    packed = jnp.concatenate([bias_rows, vectors, jnp.zeros_like(bias_rows)], axis=3)
    mine = scatter_plane(packed[:, :2], packed[:, 2:], F32)
    over_z = mine
    for k in (1, 3, 2):
        over_z = over_z + swap(mine, "z", k)
    g_b_qv = mine[:, 0, :16].reshape(layers, 2, 1, 8)
    g_b_fc = mine[:, 0, 16:48].reshape(layers, 1, 32)
    g_norm_gains = over_z[:, 1:3]
    g_shifts = over_z[:, 3:7]
    attn_all = jnp.stack([b[0] for b in big])
    g_w_qkv = jnp.stack(
        [attn_all[:, :, 128:192], attn_all[:, :, :64], attn_all[:, :, 64:128]], axis=1
    )
    g_w_out = jnp.swapaxes(attn_all[:, :, 192:], 1, 2)
    g_w_fc = jnp.stack([b[1] for b in big])
    g_w_proj = jnp.stack([jnp.swapaxes(b[2], 0, 1) for b in big])
    return (
        output,
        g_tokens,
        g_w_qkv,
        g_b_qv,
        g_w_out,
        g_w_fc,
        g_b_fc,
        g_w_proj,
        g_norm_gains,
        g_shifts,
    )


def solution(mesh):
    split = Mesh(mesh.devices.reshape(2, 4, 2, 4, 2), ("xl", "y", "xh", "z", "c"))
    dp, tensor = ("xl", "y"), ("xh", "z", "c")
    rows = P(tensor, dp, None)
    weights = (
        P(None, None, dp, tensor),
        P(None, None, tensor, dp),
        P(None, tensor, dp),
        P(None, dp, tensor),
        P(None, tensor, dp),
        P(None, tensor, dp),
        P(None, None, dp),
        P(None, None, dp),
    )
    return jax.shard_map(
        on_device,
        mesh=split,
        in_specs=(rows, P(dp, None), rows, *weights),
        out_specs=(rows, rows, *weights),
        check_vma=False,
    )
```

time: 1370 us -> 662 us (0.48)
  blocking collectives: 556 us -> 0 us
  waiting for transfers between devices: 335 us -> 46.1 us
  starting transfers between devices: 102 us -> 215 us
  other arithmetic: 75.2 us -> 121 us
  matrix products: 91.1 us -> 61.2 us
  Pallas kernels: 0 us -> 26.6 us
    all_gather x10 -> x0, blocking collectives: 329 us -> none  [the longest x2 82.8 us: fetch_forward(): lax.all_gather(b_qv[layer_index], 'dp', axis=2, tiled=True)]
    ppermute x0 -> x157, starting transfers between devices: none -> 215 us  [swap(): return lax.ppermute(value, axis, [(i, i ^ mask) for i in range(count)])]
    all_to_all x16 -> x0, blocking collectives: 177 us -> none  [the longest x2 68.7 us: sum_in_two_steps(): lax.all_to_all(own.astype(jnp.bfloat16), far, 0, 0, tiled=True)]
    all_to_all x18 -> x0, waiting for transfers between devices: 152 us -> none  [the longest x6 77.8 us: sum_in_two_steps(): lax.all_to_all(own.astype(jnp.bfloat16), far, 0, 0, tiled=True)]
    unnamed x18 -> x0, waiting for transfers between devices: 145 us -> none
    all_to_all x18 -> x0, starting transfers between devices: 101 us -> none  [the longest x11 60.5 us: copy_for_each(): lax.all_to_all(jnp.broadcast_to(value[None], (count, *value.shape)), axis...]
    unnamed x2 -> x0, blocking collectives: 50.2 us -> none
    ppermute x0 -> x157, waiting for transfers between devices: none -> 46.1 us  [swap(): return lax.ppermute(value, axis, [(i, i ^ mask) for i in range(count)])]
  transfers between devices with their start and end apart: 28 -> 157, of which waited for: 16 -> 27; matrix products, arithmetic and copies ran while one was open for 13% -> 47% of each run, Pallas kernels for 0% -> 4%
where the time goes in v1:
time: 662 us; the launch traced here: 651 us
  starting transfers between devices  215 us (32%)
  local copies, waits for them, and re-layouts  176 us (27%)
  other arithmetic  121 us (18%)
  matrix products  61.2 us (9%)
  waiting for transfers between devices  46.1 us (7%)
  Pallas kernels  26.6 us (4%)
    ppermute x157, starting transfers between devices, swap(): return lax.ppermute(value, axis, [(i, i ^ mask) for i in range(count)])  215 us
    ppermute x157, waiting for transfers between devices, swap(): return lax.ppermute(value, axis, [(i, i ^ mask) for i in range(count)])  46.1 us
    unnamed x380, local copies, waits for them, and re-layouts  37.1 us
    dot_general x8, matrix products, into_blocks(): return jnp.einsum('nd,tdk->tnk', rows, weight, preferred_element_type=F32)  22.2 us
    another operation x14, other arithmetic, gather_plane(): own = jnp.stack([ys, low, high, both], axis=1).reshape(m, 2, 8, r, c)  21.3 us
    dot_general x8, matrix products, weight_grad(): return jnp.einsum('nd,tnk->tdk', rows, blocks, preferred_element_type=F32)  20.9 us
    dot_general x8, matrix products, out_of_blocks(): return jnp.einsum('tnk,tdk->nd', blocks, weight, preferred_element_type=F32)  18.1 us
    concatenate x8, local copies, waits for them, and re-layouts, gather_plane(): return jnp.concatenate([own, other], axis=1)  17.4 us
  transfers between devices with their start and end apart: 157, of which 27 were waited for; matrix products, arithmetic and copies ran while one was open for 47% of the time, Pallas kernels for 4%

profile of v1, /device:TPU:0, one launch (start us, length us, event | category | flops | bytes accessed | tf_op | source)
XLA Modules:
  0.0 650.5 jit_solution(13698105422889187503)
XLA Ops:
  11.1 4.1 collective-permute-start.2
  48.3 3.9 collective-permute-start.43
  54.8 3.9 collective-permute-start.57
  60.3 3.9 collective-permute-start.67
  96.9 3.6 collective-permute-start.9
  108.4 3.7 collective-permute-start.26
  132.6 3.3 collective-permute-start.36
  135.9 5.1 shard_map.258
  144.4 3.3 collective-permute-start.20
  164.0 3.4 collective-permute-start.30
  177.7 3.7 collective-permute-start.46
  183.9 3.2 multiply_convert_fusion.6
  249.2 3.7 collective-permute-start.70
  252.9 5.9 shard_map.259
  284.9 3.6 collective-permute-done.79
  289.6 4.0 collective-permute-done.80
  308.7 6.2 fusion.13
  330.5 3.6 fusion.30
  362.3 3.3 collective-permute-done.75
  388.6 7.9 %shard_map.260 = (bf16[4,512,128]{2,1,0:T(8,128)(2,1)S(1)}, f32[4,512,128]{2,1,0:T(8,128)S(1)}, bf16[4,512,128]{2,1,0:T(8,128)(2,1)S(1)}) custom-call(bf16[4,512,256]{2,1,0:T(8,128)(2,1)S(1)} %copy-done.2, bf16[4,512,128]{2,1,0:T(8,128)(2,1)} %collective-permute-done.52.par_ref, bf16[4,512,256]{2,1,0:T(8,128)(2,1)S(1)} %copy-done.2, ...), custom_call_target="tpu_custom_call" | custom-call | flops 2684354560 | bytes 8388608 | tf_op jit(solution)/shard_map/pallas_call | solution.py:200
  397.7 3.2 fusion.54
  415.3 3.4 convolution_add_fusion
  449.4 4.5 collective-permute-start.152
  459.7 3.5 collective-permute-start.138
  471.6 5.6 fusion.12
  484.7 3.6 fusion.32
  520.4 3.5 collective-permute-done.98
  529.7 3.3 fusion.56
  533.7 3.6 collective-permute-done.114
  537.9 4.0 collective-permute-start.117
  541.9 7.6 %shard_map.261 = (bf16[4,512,128]{2,1,0:T(8,128)(2,1)S(1)}, f32[4,512,128]{2,1,0:T(8,128)S(1)}, bf16[4,512,128]{2,1,0:T(8,128)(2,1)}) custom-call(bf16[4,512,256]{2,1,0:T(8,128)(2,1)S(1)} %fusion.18.kv_ref.q_ref, bf16[4,512,128]{2,1,0:T(8,128)(2,1)S(1)} %copy-done.14, bf16[4,512,256]{2,1,0:T(8,128)(2,1)S(1)} %fusion.18.kv_ref.q_ref, ...), custom_call_target="tpu_custom_call" | custom-call | flops 2684354560 | bytes 8388608 | tf_op jit(solution)/shard_map/pallas_call | solution.py:200
  587.2 3.2 collective-permute-start.145
  (1103 shorter events, 513.6 us)
Async XLA Ops:
  3.1 26.3 %collective-permute-start.11 = (bf16[2,8,128]{2,1,0:T(8,128)(2,1)S(1)}, bf16[2,8,128]{2,1,0:T(8,128)(2,1)S(1)}, u32[]{:S(2)}, u32[]{:S(2)}) collective-permute-start(bf16[2,8,128]{2,1,0:T(8,128)(2,1)S(1)} %maximum_maximum_fusion.2), channel_id=1, source_target_pairs={{0,16},{16,0},{32,48},{48,32},{1,17},{17,1},{33,49},{49,33},{2,18}... | collective-permute-start | bytes 12296 | tf_op jit(solution)/shard_map/ppermute | solution.py:20
  4.8 24.7 %collective-permute-start.12 = (bf16[2,8,128]{2,1,0:T(8,128)(2,1)S(1)}, bf16[2,8,128]{2,1,0:T(8,128)(2,1)S(1)}, u32[]{:S(2)}, u32[]{:S(2)}) collective-permute-start(bf16[2,8,128]{2,1,0:T(8,128)(2,1)S(1)} %maximum_maximum_fusion.2), channel_id=1, source_target_pairs={{0,32},{16,48},{32,0},{48,16},{1,33},{17,49},{33,1},{49,17},{2,34}... | collective-permute-start | bytes 12296 | tf_op jit(solution)/shard_map/ppermute | solution.py:20
  10.7 30.3 %collective-permute-start.1 = (bf16[1,128,256]{2,1,0:T(8,128)(2,1)}, bf16[1,128,256]{2,1,0:T(8,128)(2,1)}, u32[]{:S(2)}, u32[]{:S(2)}) collective-permute-start(bf16[1,128,256]{2,1,0:T(8,128)(2,1)} %get-tuple-element.276), channel_id=1, source_target_pairs={{0,16},{16,0},{32,48},{48,32},{1,17},{17,1},{33,49},{49,33},{2,18}... | collective-permute-start | bytes 196616 | tf_op jit(solution)/shard_map/ppermute | solution.py:20
  11.1 30.7 %collective-permute-start.2 = (bf16[1,128,256]{2,1,0:T(8,128)(2,1)}, bf16[1,128,256]{2,1,0:T(8,128)(2,1)}, u32[]{:S(2)}, u32[]{:S(2)}) collective-permute-start(bf16[1,128,256]{2,1,0:T(8,128)(2,1)} %get-tuple-element.276), channel_id=1, source_target_pairs={{0,32},{16,48},{32,0},{48,16},{1,33},{17,49},{33,1},{49,17},{2,34}... | collective-permute-start | bytes 196616 | tf_op jit(solution)/shard_map/ppermute | solution.py:20
  65.9 31.0 %collective-permute-start.77 = (bf16[64,1024]{1,0:T(8,128)(2,1)}, bf16[64,1024]{1,0:T(8,128)(2,1)}, u32[]{:S(2)}, u32[]{:S(2)}) collective-permute-start(bf16[64,1024]{1,0:T(8,128)(2,1)} %select_bitcast_fusion), channel_id=1, source_target_pairs={{0,8},{8,0},{1,9},{9,1},{2,10},{10,2},{3,11},{11,3},{4,12},{12,4},... | collective-permute-start | bytes 393224 | tf_op jit(solution)/shard_map/ppermute | solution.py:20
  71.1 36.3 %collective-permute-start.4 = (bf16[1,4,128,256]{3,2,1,0:T(8,128)(2,1)}, bf16[1,4,128,256]{3,2,1,0:T(8,128)(2,1)}, u32[]{:S(2)}, u32[]{:S(2)}) collective-permute-start(bf16[1,4,128,256]{3,2,1,0:T(8,128)(2,1)} %get-tuple-element.261), channel_id=1, source_target_pairs={{0,64},{8,72},{64,0},{72,8},{1,65},{9,73},{65,1},{73,9},{2,66},{10... | collective-permute-start | bytes 786440 | tf_op jit(solution)/shard_map/ppermute | solution.py:20
  71.8 36.7 %collective-permute-start.5 = (bf16[1,4,128,256]{3,2,1,0:T(8,128)(2,1)}, bf16[1,4,128,256]{3,2,1,0:T(8,128)(2,1)}, u32[]{:S(2)}, u32[]{:S(2)}) collective-permute-start(bf16[1,4,128,256]{3,2,1,0:T(8,128)(2,1)} %get-tuple-element.261), channel_id=1, source_target_pairs={{0,8},{8,0},{64,72},{72,64},{1,9},{9,1},{65,73},{73,65},{2,10},{10... | collective-permute-start | bytes 786440 | tf_op jit(solution)/shard_map/ppermute | solution.py:20
  76.5 31.9 %collective-permute-start.6 = (bf16[1,4,128,256]{3,2,1,0:T(8,128)(2,1)}, bf16[1,4,128,256]{3,2,1,0:T(8,128)(2,1)}, u32[]{:S(2)}, u32[]{:S(2)}) collective-permute-start(bf16[1,4,128,256]{3,2,1,0:T(8,128)(2,1)} %get-tuple-element.261), channel_id=1, source_target_pairs={{0,72},{8,64},{64,8},{72,0},{1,73},{9,65},{65,9},{73,1},{2,74},{10... | collective-permute-start | bytes 786440 | tf_op jit(solution)/shard_map/ppermute | solution.py:20
  108.4 33.9 %collective-permute-start.25 = (bf16[1,4,128,256]{3,2,1,0:T(8,128)(2,1)}, bf16[1,4,128,256]{3,2,1,0:T(8,128)(2,1)}, u32[]{:S(2)}, u32[]{:S(2)}) collective-permute-start(bf16[1,4,128,256]{3,2,1,0:T(8,128)(2,1)} %get-tuple-element.249), channel_id=1, source_target_pairs={{0,64},{8,72},{64,0},{72,8},{1,65},{9,73},{65,1},{73,9},{2,66},{10... | collective-permute-start | bytes 786440 | tf_op jit(solution)/shard_map/ppermute | solution.py:20
  108.4 35.9 %collective-permute-start.26 = (bf16[1,4,128,256]{3,2,1,0:T(8,128)(2,1)}, bf16[1,4,128,256]{3,2,1,0:T(8,128)(2,1)}, u32[]{:S(2)}, u32[]{:S(2)}) collective-permute-start(bf16[1,4,128,256]{3,2,1,0:T(8,128)(2,1)} %get-tuple-element.249), channel_id=1, source_target_pairs={{0,8},{8,0},{64,72},{72,64},{1,9},{9,1},{65,73},{73,65},{2,10},{10... | collective-permute-start | bytes 786440 | tf_op jit(solution)/shard_map/ppermute | solution.py:20
  116.3 28.1 %collective-permute-start.27 = (bf16[1,4,128,256]{3,2,1,0:T(8,128)(2,1)}, bf16[1,4,128,256]{3,2,1,0:T(8,128)(2,1)}, u32[]{:S(2)}, u32[]{:S(2)}) collective-permute-start(bf16[1,4,128,256]{3,2,1,0:T(8,128)(2,1)} %get-tuple-element.249), channel_id=1, source_target_pairs={{0,72},{8,64},{64,8},{72,0},{1,73},{9,65},{65,9},{73,1},{2,74},{10... | collective-permute-start | bytes 786440 | tf_op jit(solution)/shard_map/ppermute | solution.py:20
  117.3 30.4 %collective-permute-start.35 = (bf16[1,4,128,256]{2,3,1,0:T(8,128)(2,1)}, bf16[1,4,128,256]{2,3,1,0:T(8,128)(2,1)}, u32[]{:S(2)}, u32[]{:S(2)}) collective-permute-start(bf16[1,4,128,256]{2,3,1,0:T(8,128)(2,1)} %get-tuple-element.251), channel_id=1, source_target_pairs={{0,64},{8,72},{64,0},{72,8},{1,65},{9,73},{65,1},{73,9},{2,66},{10... | collective-permute-start | bytes 786440 | tf_op jit(solution)/shard_map/ppermute | solution.py:20
  158.4 30.9 %collective-permute-start.38 = (bf16[1,2,8,128,256]{4,3,2,1,0:T(8,128)(2,1)}, bf16[1,2,8,128,256]{4,3,2,1,0:T(8,128)(2,1)}, u32[]{:S(2)}, u32[]{:S(2)}) collective-permute-start(bf16[1,2,8,128,256]{4,3,2,1,0:T(8,128)(2,1)} %copy.717), channel_id=1, source_target_pairs={{0,1},{1,0},{2,3},{3,2},{4,5},{5,4},{6,7},{7,6},{8,9},{9,8},{10,11... | collective-permute-start | bytes 3145736 | tf_op jit(solution)/shard_map/ppermute | solution.py:20
  198.7 61.4 %collective-permute-start.59 = (bf16[1,4,128,256]{3,2,1,0:T(8,128)(2,1)}, bf16[1,4,128,256]{3,2,1,0:T(8,128)(2,1)}, u32[]{:S(2)}, u32[]{:S(2)}) collective-permute-start(bf16[1,4,128,256]{3,2,1,0:T(8,128)(2,1)} %get-tuple-element.243), channel_id=1, source_target_pairs={{0,64},{8,72},{64,0},{72,8},{1,65},{9,73},{65,1},{73,9},{2,66},{10... | collective-permute-start | bytes 786440 | tf_op jit(solution)/shard_map/ppermute | solution.py:20
  219.4 43.0 %collective-permute-start.60 = (bf16[1,4,128,256]{3,2,1,0:T(8,128)(2,1)}, bf16[1,4,128,256]{3,2,1,0:T(8,128)(2,1)}, u32[]{:S(2)}, u32[]{:S(2)}) collective-permute-start(bf16[1,4,128,256]{3,2,1,0:T(8,128)(2,1)} %get-tuple-element.243), channel_id=1, source_target_pairs={{0,8},{8,0},{64,72},{72,64},{1,9},{9,1},{65,73},{73,65},{2,10},{10... | collective-permute-start | bytes 786440 | tf_op jit(solution)/shard_map/ppermute | solution.py:20
  223.2 39.2 %collective-permute-start.61 = (bf16[1,4,128,256]{3,2,1,0:T(8,128)(2,1)}, bf16[1,4,128,256]{3,2,1,0:T(8,128)(2,1)}, u32[]{:S(2)}, u32[]{:S(2)}) collective-permute-start(bf16[1,4,128,256]{3,2,1,0:T(8,128)(2,1)} %get-tuple-element.243), channel_id=1, source_target_pairs={{0,72},{8,64},{64,8},{72,0},{1,73},{9,65},{65,9},{73,1},{2,74},{10... | collective-permute-start | bytes 786440 | tf_op jit(solution)/shard_map/ppermute | solution.py:20
  224.7 39.0 %collective-permute-start.69 = (bf16[1,4,128,256]{2,3,1,0:T(8,128)(2,1)}, bf16[1,4,128,256]{2,3,1,0:T(8,128)(2,1)}, u32[]{:S(2)}, u32[]{:S(2)}) collective-permute-start(bf16[1,4,128,256]{2,3,1,0:T(8,128)(2,1)} %get-tuple-element.245), channel_id=1, source_target_pairs={{0,64},{8,72},{64,0},{72,8},{1,65},{9,73},{65,1},{73,9},{2,66},{10... | collective-permute-start | bytes 786440 | tf_op jit(solution)/shard_map/ppermute | solution.py:20
  281.9 26.6 %collective-permute-start.72 = (bf16[1,2,8,128,256]{4,3,2,1,0:T(8,128)(2,1)}, bf16[1,2,8,128,256]{4,3,2,1,0:T(8,128)(2,1)}, u32[]{:S(2)}, u32[]{:S(2)}) collective-permute-start(bf16[1,2,8,128,256]{4,3,2,1,0:T(8,128)(2,1)} %copy.735), channel_id=1, source_target_pairs={{0,1},{1,0},{2,3},{3,2},{4,5},{5,4},{6,7},{7,6},{8,9},{9,8},{10,11... | collective-permute-start | bytes 3145736 | tf_op jit(solution)/shard_map/ppermute | solution.py:20
  336.8 25.5 %collective-permute-start.73 = (bf16[128,1024]{1,0:T(8,128)(2,1)}, bf16[128,1024]{1,0:T(8,128)(2,1)}, u32[]{:S(2)}, u32[]{:S(2)}) collective-permute-start(bf16[128,1024]{1,0:T(8,128)(2,1)} %bitcast.190), channel_id=1, source_target_pairs={{0,2},{2,0},{4,6},{6,4},{1,3},{3,1},{5,7},{7,5},{8,10},{10,8},{12,... | collective-permute-start | bytes 786440 | tf_op jit(solution)/shard_map/ppermute | solution.py:20
  336.9 25.5 %collective-permute-start.74 = (bf16[128,1024]{1,0:T(8,128)(2,1)}, bf16[128,1024]{1,0:T(8,128)(2,1)}, u32[]{:S(2)}, u32[]{:S(2)}) collective-permute-start(bf16[128,1024]{1,0:T(8,128)(2,1)} %bitcast.191), channel_id=1, source_target_pairs={{0,6},{2,4},{4,2},{6,0},{1,7},{3,5},{5,3},{7,1},{8,14},{10,12},{12... | collective-permute-start | bytes 786440 | tf_op jit(solution)/shard_map/ppermute | solution.py:20
  359.7 48.9 %collective-permute-start.147 = (bf16[1,2,8,128,256]{3,2,4,1,0:T(8,128)(2,1)}, bf16[1,2,8,128,256]{3,2,4,1,0:T(8,128)(2,1)}, u32[]{:S(2)}, u32[]{:S(2)}) collective-permute-start(bf16[1,2,8,128,256]{3,2,4,1,0:T(8,128)(2,1)} %slice.1297), channel_id=1, source_target_pairs={{0,1},{1,0},{2,3},{3,2},{4,5},{5,4},{6,7},{7,6},{8,9},{9,8},{10,11... | collective-permute-start | bytes 3145736 | tf_op jit(solution)/shard_map/ppermute | solution.py:20
  359.7 59.0 %collective-permute-start.133 = (bf16[1,2,8,128,256]{3,2,4,1,0:T(8,128)(2,1)}, bf16[1,2,8,128,256]{3,2,4,1,0:T(8,128)(2,1)}, u32[]{:S(2)}, u32[]{:S(2)}) collective-permute-start(bf16[1,2,8,128,256]{3,2,4,1,0:T(8,128)(2,1)} %slice.1299), channel_id=1, source_target_pairs={{0,1},{1,0},{2,3},{3,2},{4,5},{5,4},{6,7},{7,6},{8,9},{9,8},{10,11... | collective-permute-start | bytes 3145736 | tf_op jit(solution)/shard_map/ppermute | solution.py:20
  404.1 29.4 %collective-permute-start.88 = (bf16[128,1024]{1,0:T(8,128)(2,1)}, bf16[128,1024]{1,0:T(8,128)(2,1)}, u32[]{:S(2)}, u32[]{:S(2)}) collective-permute-start(bf16[128,1024]{1,0:T(8,128)(2,1)} %bitcast.237), channel_id=1, source_target_pairs={{0,2},{2,0},{4,6},{6,4},{1,3},{3,1},{5,7},{7,5},{8,10},{10,8},{12,... | collective-permute-start | bytes 786440 | tf_op jit(solution)/shard_map/ppermute | solution.py:20
  404.1 32.0 %collective-permute-start.89 = (bf16[128,1024]{1,0:T(8,128)(2,1)}, bf16[128,1024]{1,0:T(8,128)(2,1)}, u32[]{:S(2)}, u32[]{:S(2)}) collective-permute-start(bf16[128,1024]{1,0:T(8,128)(2,1)} %bitcast.238), channel_id=1, source_target_pairs={{0,6},{2,4},{4,2},{6,0},{1,7},{3,5},{5,3},{7,1},{8,14},{10,12},{12... | collective-permute-start | bytes 786440 | tf_op jit(solution)/shard_map/ppermute | solution.py:20
  405.4 31.1 %collective-permute-start.90 = (bf16[128,1024]{1,0:T(8,128)(2,1)}, bf16[128,1024]{1,0:T(8,128)(2,1)}, u32[]{:S(2)}, u32[]{:S(2)}) collective-permute-start(bf16[128,1024]{1,0:T(8,128)(2,1)} %bitcast.239), channel_id=1, source_target_pairs={{0,4},{2,6},{4,0},{6,2},{1,5},{3,7},{5,1},{7,3},{8,12},{10,14},{12... | collective-permute-start | bytes 786440 | tf_op jit(solution)/shard_map/ppermute | solution.py:20
  412.6 28.3 %collective-permute-start.148 = (bf16[1,4,128,256]{2,3,1,0:T(8,128)(2,1)}, bf16[1,4,128,256]{2,3,1,0:T(8,128)(2,1)}, u32[]{:S(2)}, u32[]{:S(2)}) collective-permute-start(bf16[1,4,128,256]{2,3,1,0:T(8,128)(2,1)} %get-tuple-element.152), channel_id=1, source_target_pairs={{0,64},{8,72},{64,0},{72,8},{1,65},{9,73},{65,1},{73,9},{2,66},{10... | collective-permute-start | bytes 786440 | tf_op jit(solution)/shard_map/ppermute | solution.py:20
  418.7 24.7 %collective-permute-start.149 = (bf16[1,4,128,256]{2,3,1,0:T(8,128)(2,1)}, bf16[1,4,128,256]{2,3,1,0:T(8,128)(2,1)}, u32[]{:S(2)}, u32[]{:S(2)}) collective-permute-start(bf16[1,4,128,256]{2,3,1,0:T(8,128)(2,1)} %get-tuple-element.154), channel_id=1, source_target_pairs={{0,72},{8,64},{64,8},{72,0},{1,73},{9,65},{65,9},{73,1},{2,74},{10... | collective-permute-start | bytes 786440 | tf_op jit(solution)/shard_map/ppermute | solution.py:20
  443.4 25.6 %collective-permute-start.91 = (bf16[128,1024]{1,0:T(8,128)(2,1)S(1)}, bf16[128,1024]{1,0:T(8,128)(2,1)S(1)}, u32[]{:S(2)}, u32[]{:S(2)}) collective-permute-start(bf16[128,1024]{1,0:T(8,128)(2,1)S(1)} %get-tuple-element.122), channel_id=1, source_target_pairs={{0,2},{2,0},{4,6},{6,4},{1,3},{3,1},{5,7},{7,5},{8,10},{10,8},{12,... | collective-permute-start | bytes 786440 | tf_op jit(solution)/shard_map/ppermute | solution.py:20
  466.2 46.5 %collective-permute-start.112 = (bf16[1,2,8,128,256]{3,2,4,1,0:T(8,128)(2,1)}, bf16[1,2,8,128,256]{3,2,4,1,0:T(8,128)(2,1)}, u32[]{:S(2)}, u32[]{:S(2)}) collective-permute-start(bf16[1,2,8,128,256]{3,2,4,1,0:T(8,128)(2,1)} %slice.1301), channel_id=1, source_target_pairs={{0,1},{1,0},{2,3},{3,2},{4,5},{5,4},{6,7},{7,6},{8,9},{9,8},{10,11... | collective-permute-start | bytes 3145736 | tf_op jit(solution)/shard_map/ppermute | solution.py:20
  500.9 48.8 %collective-permute-start.140 = (bf16[1,2,8,128,256]{3,2,4,1,0:T(8,128)(2,1)S(1)}, bf16[1,2,8,128,256]{3,2,4,1,0:T(8,128)(2,1)S(1)}, u32[]{:S(2)}, u32[]{:S(2)}) collective-permute-start(bf16[1,2,8,128,256]{3,2,4,1,0:T(8,128)(2,1)S(1)} %slice.1298), channel_id=1, source_target_pairs={{0,1},{1,0},{2,3},{3,2},{4,5},{5,4},{6,7},{7,6},{8,9},{9,8},{10,11... | collective-permute-start | bytes 3145736 | tf_op jit(solution)/shard_map/ppermute | solution.py:20
  504.8 52.1 %collective-permute-start.126 = (bf16[1,2,8,128,256]{3,2,4,1,0:T(8,128)(2,1)S(1)}, bf16[1,2,8,128,256]{3,2,4,1,0:T(8,128)(2,1)S(1)}, u32[]{:S(2)}, u32[]{:S(2)}) collective-permute-start(bf16[1,2,8,128,256]{3,2,4,1,0:T(8,128)(2,1)S(1)} %slice.1300), channel_id=1, source_target_pairs={{0,1},{1,0},{2,3},{3,2},{4,5},{5,4},{6,7},{7,6},{8,9},{9,8},{10,11... | collective-permute-start | bytes 3145736 | tf_op jit(solution)/shard_map/ppermute | solution.py:20
  583.5 42.7 %collective-permute-start.105 = (bf16[1,2,8,128,256]{3,2,4,1,0:T(8,128)(2,1)}, bf16[1,2,8,128,256]{3,2,4,1,0:T(8,128)(2,1)S(1)}, u32[]{:S(2)}, u32[]{:S(2)}) collective-permute-start(bf16[1,2,8,128,256]{3,2,4,1,0:T(8,128)(2,1)} %slice.1302), channel_id=1, source_target_pairs={{0,1},{1,0},{2,3},{3,2},{4,5},{5,4},{6,7},{7,6},{8,9},{9,8},{10,11... | collective-permute-start | bytes 3145736 | tf_op jit(solution)/shard_map/ppermute | solution.py:20
  (306 other events, 2714.0 us)

commit v2 on v1

v2 whole, which is shorter than its diff:
```python
import functools

import jax
import jax.numpy as jnp
from jax import lax
from jax.experimental import pallas as pl
from jax.experimental.pallas import tpu as pltpu
from jax.sharding import Mesh
from jax.sharding import PartitionSpec as P

EPS = 1e-05
F32 = jnp.float32
BF16 = jnp.bfloat16
X = ("xl", "xh")
PLANE = ("xl", "y", "xh", "c")
HD = 64
OWN = 128
SEEN = 512
WIDTH = 1024
VMEM = 20 << 20
NT = (((1,), (1,)), ((), ()))
TN = (((0,), (0,)), ((), ()))


def swap(value, axis, mask):
    count = lax.axis_size(axis)
    return lax.ppermute(value, axis, [(i, i ^ mask) for i in range(count)])


def over_z(value):
    two, one, three = (swap(value, "z", k) for k in (2, 1, 3))
    return value, one, two, three


def exchanged(parts):
    two, one, three = (swap(parts[k], "z", k) for k in (2, 1, 3))
    return parts[0], one, two, three


def tied(*values):
    return lax.optimization_barrier(values)


def swaps_x(parts):
    return [swap(part, X, mask) for part, mask in zip(parts, (2, 1, 3))]


def swaps_y(parts):
    one, three, two = (swap(parts[k - 1], "y", k) for k in (1, 3, 2))
    return one, two, three


def call(kernel, name, grid, ins, outs, scratch=(), flops=0, exps=0, prefetch=None):
    arrays = [a for a, _, _ in ins]
    in_specs = [pl.BlockSpec(block, index) for _, block, index in ins]
    out_specs = [pl.BlockSpec(block, index) for _, _, block, index in outs]
    shapes = [jax.ShapeDtypeStruct(shape, kind) for shape, kind, _, _ in outs]
    moved = sum(a.size * a.dtype.itemsize for a in arrays)
    moved += sum(s.size * s.dtype.itemsize for s in shapes)
    keys = dict(
        out_shape=shapes,
        name=name,
        compiler_params=pltpu.CompilerParams(vmem_limit_bytes=VMEM),
        cost_estimate=pl.CostEstimate(flops=flops, bytes_accessed=moved, transcendentals=exps),
    )
    if prefetch is None:
        return pl.pallas_call(
            kernel,
            grid=grid,
            in_specs=in_specs,
            out_specs=out_specs,
            scratch_shapes=list(scratch),
            **keys,
        )(*arrays)
    spec = pltpu.PrefetchScalarGridSpec(
        num_scalar_prefetch=1,
        grid=grid,
        in_specs=in_specs,
        out_specs=out_specs,
        scratch_shapes=list(scratch),
    )
    return pl.pallas_call(kernel, grid_spec=spec, **keys)(prefetch, *arrays)


def whole(array):
    return (array, array.shape, lambda *_: (0,) * array.ndim)


def weight_of(store, lanes=256, column=0):
    array, row = store
    return (array, (8, 4, 128, lanes), lambda *_: (0, 0, row, column))


def out_whole(shape, kind):
    return (shape, kind, shape, lambda *_: (0,) * len(shape))


def out_parts():
    return [out_whole((OWN, WIDTH), BF16)] * 4


def matrix(ref, t):
    return ref[:, t].reshape(8 * ref.shape[2], ref.shape[3])


def turned_product(blocks, ref, emit):
    left = jnp.concatenate(blocks, axis=1)
    for d in range(4):
        pieces = [
            ref[2 * d : 2 * d + 2, t].reshape(2 * ref.shape[2], ref.shape[3]) for t in range(4)
        ]
        right = jnp.concatenate(pieces, axis=1)
        value = lax.dot_general(left, right, NT, preferred_element_type=F32)
        emit(slice(d * 256, (d + 1) * 256), value)


def into_parts(parts):
    def emit(columns, value):
        for k, part in enumerate(parts):
            part[:, columns] = value[k * OWN : (k + 1) * OWN].astype(BF16)

    return emit


def xhat_of(values):
    center = values - jnp.mean(values, axis=-1, keepdims=True)
    rstd = lax.rsqrt(jnp.mean(center * center, axis=-1, keepdims=True) + EPS)
    return center * rstd, rstd


def fill_rows(sources, rows_ref, gain_ref=None, shift_ref=None):
    for k, source in enumerate(sources):
        value = source[...]
        if gain_ref is not None:
            value = xhat_of(value.astype(F32))[0] * gain_ref[0:1] + shift_ref[0:1]
            value = value.astype(BF16)
        rows_ref[k * OWN : (k + 1) * OWN] = value


def project_kernel(normalize, *refs):
    sources, refs = refs[:4], refs[4:]
    gain_ref, shift_ref = None, None
    if normalize:
        (gain_ref, shift_ref), refs = refs[:2], refs[2:]
    w_ref, bias_ref, scale_ref, rows_ref, q_ref, kv_ref = refs
    fill_rows(sources, rows_ref, gain_ref, shift_ref)
    for t in range(4):
        value = jnp.dot(rows_ref[...], matrix(w_ref, t), preferred_element_type=F32)
        value = ((value + bias_ref[t, 0:1]) * scale_ref[0:1]).astype(BF16)
        q_ref[t] = value[:, 128:]
        kv_ref[t] = value[:, :128]


def project(sources, norm, store, bias, scale):
    ins = [whole(s) for s in sources] + [whole(n) for n in norm]
    ins += [weight_of(store), whole(bias), whole(scale)]
    return call(
        functools.partial(project_kernel, len(norm) > 0),
        "project",
        (1,),
        ins,
        [out_whole((SEEN, WIDTH), BF16)] + [out_whole((4, SEEN, 128), BF16)] * 2,
        flops=2 * SEEN * WIDTH * 1024,
    )


def half_rows(value, part):
    step = OWN // 2
    return jnp.concatenate(
        [value[k * OWN + part * step : k * OWN + (part + 1) * step] for k in range(4)], axis=0
    )


def store_half(ref, t, part, value):
    step = OWN // 2
    for k in range(4):
        ref[t, k * OWN + part * step : k * OWN + (part + 1) * step] = value[
            k * step : (k + 1) * step
        ]


def head_keys(kv, par):
    return jnp.concatenate(
        [half_rows(kv, 0), half_rows(par, 0), half_rows(kv, 1), half_rows(par, 1)], axis=0
    )


def attend_kernel(kv_ref, par_ref, q_ref, bias_ref, w_ref, mixed_ref, lse_ref, *parts):
    half = SEEN // 2
    for t in range(4):
        kv = head_keys(kv_ref[t], par_ref[t])
        queries = q_ref[t]
        for part in range(2):
            rows = slice(part * half, (part + 1) * half)
            seen = SEEN * (part + 1)
            keys = kv[:seen]
            scores = lax.dot_general(
                half_rows(queries, part), keys, NT, preferred_element_type=F32
            )
            scores = scores + bias_ref[rows, :seen]
            highest = jnp.max(scores, axis=1, keepdims=True)
            raised = jnp.exp(scores - highest)
            totals = jnp.sum(raised, axis=1, keepdims=True)
            probs = (raised * (1.0 / totals)).astype(BF16)
            mixed = jnp.dot(probs, keys, preferred_element_type=F32)
            lane = lax.broadcasted_iota(jnp.int32, mixed.shape, 1)
            store_half(mixed_ref, t, part, jnp.where(lane >= HD, mixed, 0.0).astype(BF16))
            lse_ref[t, rows] = highest + jnp.log(totals)
    turned_product([mixed_ref[t] for t in range(4)], w_ref, into_parts(parts))


AREA = 4 * SEEN * 768


def attend(queries, kv, par, bias, store):
    return call(
        attend_kernel,
        "attend",
        (1,),
        [whole(kv), whole(par), whole(queries), whole(bias), weight_of(store, 128, 1)],
        [
            out_whole((4, SEEN, 128), BF16),
            out_whole((4, SEEN, 1), F32),
            *out_parts(),
        ],
        flops=AREA * 3700,
        exps=AREA,
    )


def attend_back_kernel(g0, g1, g2, g3, w_ref, kv_ref, par_ref, q_ref, bias_ref, lse_ref, *outs):
    rows_ref, dq_ref, own_ref, other_ref = outs
    fill_rows((g0, g1, g2, g3), rows_ref)
    half = SEEN // 2
    for t in range(4):
        d_mixed = jnp.dot(rows_ref[...], matrix(w_ref, t), preferred_element_type=F32)
        lane = lax.broadcasted_iota(jnp.int32, d_mixed.shape, 1)
        d_mixed = jnp.where(lane >= HD, d_mixed, 0.0).astype(BF16)
        kv = head_keys(kv_ref[t], par_ref[t])
        all_queries = q_ref[t]
        sums = []
        for part in range(2):
            rows = slice(part * half, (part + 1) * half)
            seen = SEEN * (part + 1)
            keys = kv[:seen]
            queries = half_rows(all_queries, part)
            grad = half_rows(d_mixed, part)
            scores = lax.dot_general(queries, keys, NT, preferred_element_type=F32)
            probs = jnp.exp(scores + bias_ref[rows, :seen] - lse_ref[t, rows])
            dprobs = lax.dot_general(grad, keys, NT, preferred_element_type=F32)
            inner = jnp.sum(probs * dprobs, axis=1, keepdims=True)
            dscores = (probs * (dprobs - inner)).astype(BF16)
            low = probs.astype(BF16)
            dq = jnp.dot(dscores, keys, preferred_element_type=F32) * 0.125
            lane = lax.broadcasted_iota(jnp.int32, dq.shape, 1)
            store_half(dq_ref, t, part, jnp.where(lane < HD, dq, 0.0).astype(BF16))
            sums.append(
                lax.dot_general(dscores, queries, TN, preferred_element_type=F32)
                + lax.dot_general(low, grad, TN, preferred_element_type=F32)
            )
        lower = sums[0] + sums[1][:SEEN]
        upper = sums[1][SEEN:]
        for part, value in enumerate((lower, upper)):
            store_half(own_ref, t, part, value[:half])
            store_half(other_ref, t, part, value[half:].astype(BF16))


def attend_back(sources, store, queries, kv, par, bias, lse):
    return call(
        attend_back_kernel,
        "attend_back",
        (1,),
        [whole(s) for s in sources]
        + [weight_of(store, 128, 1)]
        + [whole(a) for a in (kv, par, queries, bias, lse)],
        [
            out_whole((SEEN, WIDTH), BF16),
            out_whole((4, SEEN, 128), BF16),
            out_whole((4, SEEN, 128), F32),
            out_whole((4, SEEN, 128), BF16),
        ],
        flops=AREA * 6200,
        exps=AREA,
    )


def rejoin_kernel(norm_sums, own_ref, got_ref, dq_ref, w_ref, *refs):
    tokens, refs = refs[: 4 * norm_sums], refs[4 * norm_sums :]
    d_ref, sum_ref, p0, p1, p2, p3, *rest = refs
    for t in range(4):
        dkv = (own_ref[t] + got_ref[t].astype(F32)).astype(BF16)
        value = jnp.concatenate([dkv, dq_ref[t]], axis=1)
        d_ref[t] = value
        sums = jnp.sum(value.astype(F32), axis=0, keepdims=True)
        sum_ref[t] = jnp.broadcast_to(sums, sum_ref.shape[1:])
    blocks = [d_ref[t] for t in range(4)]
    emit = into_parts((p0, p1, p2, p3))
    if not norm_sums:
        turned_product(blocks, w_ref, emit)
        return
    norm_ref, xhat_ref = rest
    for k in range(4):
        xhat_ref[k * OWN : (k + 1) * OWN] = xhat_of(tokens[k][...].astype(F32))[0]
    norm_ref[...] = jnp.zeros_like(norm_ref)

    def emit_sums(columns, value):
        emit(columns, value)
        norm_ref[0:1, columns] = jnp.sum(value * xhat_ref[:, columns], axis=0, keepdims=True)
        norm_ref[1:2, columns] = jnp.sum(value, axis=0, keepdims=True)

    turned_product(blocks, w_ref, emit_sums)


def rejoin(own, got, dq, store, tokens=()):
    outs = [out_whole((4, SEEN, 256), BF16), out_whole((4, 8, 256), F32), *out_parts()]
    scratch = []
    if tokens:
        outs.append(out_whole((8, WIDTH), F32))
        scratch.append(pltpu.VMEM((SEEN, WIDTH), F32))
    return call(
        functools.partial(rejoin_kernel, len(tokens) > 0),
        "rejoin",
        (1,),
        [whole(own), whole(got), whole(dq), weight_of(store)] + [whole(t) for t in tokens],
        outs,
        scratch,
        flops=2 * SEEN * WIDTH * 1024,
    )


def gelu_parts(pre):
    a, b = 0.7978845608028654, 0.044715
    square = pre * pre
    return square, jnp.tanh(a * pre * (1.0 + b * square)), a, b


def feed_kernel(x0, x1, x2, x3, fc_ref, proj_ref, bias_ref, rows_ref, pre_ref, hid_ref, *parts):
    fill_rows((x0, x1, x2, x3), rows_ref)
    blocks = []
    for t in range(4):
        pre = jnp.dot(rows_ref[...], matrix(fc_ref, t), preferred_element_type=F32)
        pre = pre + bias_ref[t, 0:1]
        pre_ref[t] = pre
        _, th, _, _ = gelu_parts(pre)
        hidden = (0.5 * pre * (1.0 + th)).astype(BF16)
        hid_ref[t] = hidden
        blocks.append(hidden)
    turned_product(blocks, proj_ref, into_parts(parts))


def feed(sources, fc, proj, bias):
    return call(
        feed_kernel,
        "feed",
        (1,),
        [whole(s) for s in sources] + [weight_of(fc), weight_of(proj), whole(bias)],
        [
            out_whole((SEEN, WIDTH), BF16),
            out_whole((4, SEEN, 256), F32),
            out_whole((4, SEEN, 256), BF16),
            *out_parts(),
        ],
        flops=8 * SEEN * WIDTH * 1024,
        exps=SEEN * 1024,
    )


def feed_back_kernel(g0, g1, g2, g3, fc_ref, proj_ref, pre_ref, rows_ref, d_ref, sum_ref, *parts):
    fill_rows((g0, g1, g2, g3), rows_ref)
    blocks = []
    for t in range(4):
        d_hidden = jnp.dot(rows_ref[...], matrix(proj_ref, t), preferred_element_type=F32)
        pre = pre_ref[t]
        square, th, a, b = gelu_parts(pre)
        slope = 0.5 * (1.0 + th) + 0.5 * pre * (1.0 - th * th) * a * (1.0 + 3.0 * b * square)
        d_pre = (d_hidden * slope).astype(BF16)
        d_ref[t] = d_pre
        sums = jnp.sum(d_pre.astype(F32), axis=0, keepdims=True)
        sum_ref[t] = jnp.broadcast_to(sums, sum_ref.shape[1:])
        blocks.append(d_pre)
    turned_product(blocks, fc_ref, into_parts(parts))


def feed_back(sources, fc, proj, pre):
    return call(
        feed_back_kernel,
        "feed_back",
        (1,),
        [whole(s) for s in sources] + [weight_of(fc), weight_of(proj), whole(pre)],
        [
            out_whole((SEEN, WIDTH), BF16),
            out_whole((4, SEEN, 256), BF16),
            out_whole((4, 8, 256), F32),
            *out_parts(),
        ],
        flops=8 * SEEN * WIDTH * 1024,
        exps=SEEN * 1024,
    )


def small_rows(d, t, refs):
    fc0, fc1, qkvo0, qkvo1, attn0, feed0, attn1, feed1, last = refs
    lanes = slice(d * 128, (d + 1) * 128)

    def pair(one, first, two, second):
        return jnp.concatenate(
            [one[first : first + 1, lanes], two[second : second + 1, lanes]], axis=1
        )

    rows = [fc0[t, 0:1], fc1[t, 0:1], qkvo0[t, 0:1], qkvo1[t, 0:1]]
    for attn, feed, after in ((attn0, feed0, attn1), (attn1, feed1, last)):
        rows += [
            pair(attn, 0, feed, 0),
            pair(attn, 1, feed, 1),
            pair(feed, 2, after, 2),
        ]
    return rows


def weight_grad_kernel(attention, extra, me_ref, a_ref, ab_ref, b_ref, bb_ref, *refs):
    own_ref, other_ref = refs[-2:]
    left, right = a_ref[...].T, b_ref[...].T
    for out, core in ((own_ref, 0), (other_ref, 1)):
        for x in range(2):
            t = (x ^ me_ref[1]) * 2 + (core ^ me_ref[2])
            one = jnp.dot(left, ab_ref[t], preferred_element_type=F32)
            two = jnp.dot(right, bb_ref[t], preferred_element_type=F32)
            for d in range(8):
                to = d ^ me_ref[0]
                rows = slice(d * 128, (d + 1) * 128)
                if attention:
                    out[x, to, :128, :128] = one[rows, :128].astype(BF16)
                    out[x, to, :128, 128:] = (one[rows, 128:] + two[rows]).astype(BF16)
                else:
                    out[x, to, :128] = one[rows].astype(BF16)
                    out[x, to, 128:] = two[rows].astype(BF16)
                if extra:
                    small = small_rows(d, t, refs[:-2])
                    small.append(jnp.zeros((16 - len(small), 256), F32))
                    out[x, to, 128:] = jnp.concatenate(small, axis=0).astype(BF16)


def weight_grads(attention, me, a, a_blocks, b, b_blocks, extra=()):
    rows = (128 if attention else 256) + (16 if extra else 0)
    arrays = [a, a_blocks, b, b_blocks, *extra]
    own, other = call(
        functools.partial(weight_grad_kernel, attention, len(extra) > 0),
        "weight_grads",
        (1,),
        [whole(array) for array in arrays],
        [out_whole((2, 8, rows, 256), BF16)] * 2,
        flops=7 * SEEN * WIDTH * 1024,
        prefetch=me,
    )
    return own.reshape(4, 4, rows, 256), other.reshape(4, 4, rows, 256)


def after_core_kernel(own_ref, got_ref, keep_ref, *sends):
    keep_ref[0] = own_ref[0, 0].astype(F32) + got_ref[0, 0].astype(F32)
    for k, send in enumerate(sends):
        send[0] = (own_ref[k + 1, 0].astype(F32) + got_ref[k + 1, 0].astype(F32)).astype(BF16)


def after_core(own, got):
    rows = own.shape[2]

    def at(y):
        return (0, y, 0, 0)

    def to(y):
        return (y, 0, 0)

    shape, block = (4, rows, 256), (1, rows, 256)
    keep, *sends = call(
        after_core_kernel,
        "after_core",
        (4,),
        [(own, (4, 1, rows, 256), at), (got, (4, 1, rows, 256), at)],
        [(shape, F32, block, to)] + [(shape, BF16, block, to)] * 3,
        flops=own.size,
    )
    return keep, sends


def after_x_kernel(keep_ref, one, two, three, out_ref, *sends):
    for y in range(4):
        value = keep_ref[y] + one[y].astype(F32) + two[y].astype(F32) + three[y].astype(F32)
        if y == 0:
            out_ref[...] = value
        else:
            sends[y - 1][...] = value.astype(BF16)


def after_x(keep, got):
    shape = keep.shape[1:]
    keep, *sends = call(
        after_x_kernel,
        "after_x",
        (1,),
        [whole(keep)] + [whole(g) for g in got],
        [out_whole(shape, F32)] + [out_whole(shape, BF16)] * 3,
        flops=keep.size * 3,
    )
    return keep, sends


def finish_feed_kernel(*refs):
    fc_ref, proj_ref = refs[-2:]
    for i in range(2):
        value = total_of(refs[4 * i : 4 * i + 4])
        fc_ref[i] = value[:128]
        proj_ref[i] = value[128:].T


def finish_feed(groups):
    return call(
        finish_feed_kernel,
        "finish_feed",
        (1,),
        [whole(a) for group in groups for a in group],
        [out_whole((2, 128, 256), F32), out_whole((2, 256, 128), F32)],
        flops=1 << 19,
    )


def finish_attention_kernel(*refs):
    qkv_ref, out_ref, small_ref = refs[-3:]
    for i in range(2):
        value = total_of(refs[4 * i : 4 * i + 4])
        qkv_ref[i, 0] = value[:128, 128:192]
        qkv_ref[i, 1] = value[:128, :64]
        qkv_ref[i, 2] = value[:128, 64:128]
        out_ref[i] = value[:128, 128:].T[64:]
        if i == 0:
            small_ref[...] = value[128:]


def finish_attention(groups):
    return call(
        finish_attention_kernel,
        "finish_attention",
        (1,),
        [whole(a) for group in groups for a in group],
        [
            out_whole((2, 3, 128, 64), F32),
            out_whole((2, 64, 128), F32),
            out_whole((16, 256), F32),
        ],
        flops=1 << 19,
    )


def pack_kernel(qkv_ref, wo_ref, fc_ref, proj_ref, bq_ref, bf_ref, gain_ref, shift_ref, *outs):
    early_ref, late_ref, last_ref = outs

    def attention(i):
        pieces = [qkv_ref[i, 1], qkv_ref[i, 2], qkv_ref[i, 0], wo_ref[i].T]
        return jnp.concatenate(pieces, axis=1)

    early_ref[:128] = attention(0)
    rows = []
    for i in range(2):
        none = jnp.zeros((1, 80), BF16)
        rows.append(jnp.concatenate([bq_ref[i, 0], bq_ref[i, 1], bf_ref[i], none], axis=1))
        rows += [gain_ref[i], shift_ref[i], jnp.zeros((1, 128), BF16)]
    small = jnp.concatenate([r.astype(F32) for r in rows], axis=0)
    small = jnp.concatenate([small, jnp.zeros_like(small)], axis=1)
    early_ref[128:] = small.astype(BF16)
    late_ref[:128] = fc_ref[0]
    late_ref[128:256] = proj_ref[0].T
    late_ref[256:] = attention(1)
    last_ref[:128] = fc_ref[1]
    last_ref[128:] = proj_ref[1].T


def pack(*arrays):
    return call(
        pack_kernel,
        "pack",
        (1,),
        [whole(a) for a in arrays],
        [
            out_whole((144, 256), BF16),
            out_whole((384, 256), BF16),
            out_whole((256, 256), BF16),
        ],
    )


def merge_kernel(me_ref, own_ref, other_ref, out_ref):
    for d in range(8):
        for ref, core in ((own_ref, 0), (other_ref, 1)):
            for x in range(2):
                t = (x ^ me_ref[1]) * 2 + (core ^ me_ref[2])
                out_ref[d, t] = ref[x, d ^ me_ref[0]]


def merge(me, own, other):
    return call(
        merge_kernel,
        "merge",
        (1,),
        [whole(own), whole(other)],
        [out_whole((8, 4, *own.shape[2:]), BF16)],
        prefetch=me,
    )[0]


def total_of(parts):
    value = parts[0][...].astype(F32)
    for part in parts[1:]:
        value = value + part[...].astype(F32)
    return value


def residual_kernel(p0, p1, p2, p3, x_ref, bias_ref, gain_ref, shift_ref, next_ref, norm_ref):
    value = x_ref[...].astype(F32) + total_of((p0, p1, p2, p3)) + bias_ref[0:1]
    next_ref[...] = value
    norm_ref[...] = (xhat_of(value)[0] * gain_ref[0:1] + shift_ref[0:1]).astype(BF16)


def add_and_norm(parts, values, bias, gain, shift):
    return call(
        residual_kernel,
        "add_and_norm",
        (1,),
        [whole(p) for p in parts] + [whole(values), whole(bias), whole(gain), whole(shift)],
        [out_whole((OWN, WIDTH), F32), out_whole((OWN, WIDTH), BF16)],
        flops=OWN * WIDTH * 16,
    )


def norm_back_kernel(p0, p1, p2, p3, x_ref, gain_ref, g_ref, out_ref, low_ref, sum_ref):
    grad = total_of((p0, p1, p2, p3))
    xhat, rstd = xhat_of(x_ref[...].astype(F32))
    dxhat = grad * gain_ref[0:1]
    into = dxhat - jnp.mean(dxhat, axis=-1, keepdims=True)
    into = (into - xhat * jnp.mean(dxhat * xhat, axis=-1, keepdims=True)) * rstd
    value = g_ref[...].astype(F32) + into
    out_ref[...] = value
    low = value.astype(BF16)
    low_ref[...] = low
    sum_ref[...] = jnp.zeros_like(sum_ref)
    sum_ref[0:1] = jnp.sum(grad * xhat, axis=0, keepdims=True)
    sum_ref[1:2] = jnp.sum(grad, axis=0, keepdims=True)
    sum_ref[2:3] = jnp.sum(low.astype(F32), axis=0, keepdims=True)


def norm_back(parts, values, gain, grad):
    return call(
        norm_back_kernel,
        "norm_back",
        (1,),
        [whole(p) for p in parts] + [whole(values), whole(gain), whole(grad)],
        [
            out_whole((OWN, WIDTH), F32),
            out_whole((OWN, WIDTH), BF16),
            out_whole((8, WIDTH), F32),
        ],
        flops=OWN * WIDTH * 32,
    )


def on_device(
    tokens, segments, cotangent, w_qkv, b_qv, w_out, w_fc, b_fc, w_proj, norm_gains, shifts
):
    layers = w_qkv.shape[0]
    xl, y, xh, z, core = (lax.axis_index(a) for a in ("xl", "y", "xh", "z", "c"))
    d_own = xl * 4 + y
    me = jnp.stack([d_own, xh, core]).astype(jnp.int32)
    first = xh == 0
    block = tokens.shape[0]

    def by_row(value):
        kept = jnp.where(first, value[:, 0], value[:, 1])
        got = swap(jnp.where(first, value[:, 1], value[:, 0]), "xh", 1)
        return jnp.concatenate(
            [jnp.where(first, kept, got), jnp.where(first, got, kept)], axis=0
        )

    def by_position(value):
        lower, upper = value[:block], value[block:]
        kept = jnp.where(first, lower, upper)
        got = swap(jnp.where(first, upper, lower).astype(BF16), "xh", 1).astype(value.dtype)
        return jnp.stack([jnp.where(first, kept, got), jnp.where(first, got, kept)], axis=1)

    own_tokens = by_row(tokens)

    early, late, last = pack(w_qkv, w_out, w_fc, w_proj, b_qv, b_fc, norm_gains, shifts)
    one, three, two = (swap(early, "y", k) for k in (1, 3, 2))
    early = jnp.stack([early, one, two, three])
    early, own_tokens, late = tied(early, own_tokens, late)
    all_tokens = over_z(own_tokens)
    low, high, both = swaps_x([early] * 3)
    low, high, both, all_tokens = tied(low, high, both, all_tokens)
    early = jnp.stack([early, low, high, both]).reshape(2, 8, *early.shape[1:])
    early = merge(me, early, swap(early, "c", 1))
    late = lax.all_gather(late, PLANE, axis=0, tiled=False).reshape(8, 4, *late.shape)
    last = lax.all_gather(last, PLANE, axis=0, tiled=False).reshape(8, 4, *last.shape)
    attn_w = [(early, 0), (late, 2)]
    fc_w = [(late, 0), (last, 0)]
    proj_w = [(late, 1), (last, 1)]

    small_all = early[:, :, 128:, :128].reshape(8, 4, layers, 8, 128).transpose(2, 1, 3, 0, 4)
    rows = small_all[:, 0, 1:7].reshape(layers, 6, 1, WIDTH).astype(F32)
    rows = jnp.broadcast_to(rows, (layers, 6, 8, WIDTH))
    gains = [[rows[i, k] for k in range(2)] for i in range(layers)]
    shift = [[rows[i, 2 + k] for k in range(4)] for i in range(layers)]
    biases = small_all[:, :, 0].astype(F32)
    q_bias = biases[..., :8].reshape(layers, 4, HD)
    v_bias = biases[..., 8:16].reshape(layers, 4, HD)
    fc_bias = biases[..., 16:48].reshape(layers, 4, 1, 256)
    fc_bias = jnp.broadcast_to(fc_bias, (layers, 4, 8, 256))
    none = jnp.zeros_like(q_bias)
    qkvo_bias = jnp.concatenate([none, v_bias, q_bias, none], axis=2)[:, :, None]
    qkvo_bias = jnp.broadcast_to(qkvo_bias, (layers, 4, 8, 256))
    column = jnp.arange(256)
    scale = jnp.where(column < 2 * HD, 1.0, jnp.where(column < 3 * HD, 0.125, 0.0))
    scale = jnp.broadcast_to(scale.astype(F32), (8, 256))

    seg_row = jnp.where(first, segments[0], segments[1])
    position = jnp.arange(seg_row.shape[0], dtype=jnp.int32)

    def at_core(value, which):
        cut = value.reshape(2, 4, 2, block)
        cut = jnp.where(which == 0, cut[:, :, 0], cut[:, :, 1])
        for bit in (1, 2):
            turned = jnp.stack([cut[:, k ^ bit] for k in range(4)], axis=1)
            cut = jnp.where((z & bit) != 0, turned, cut)
        return cut.reshape(2, 4 * block)

    own_pos, own_seg = at_core(position, core), at_core(seg_row, core)
    par_pos, par_seg = at_core(position, 1 - core), at_core(seg_row, 1 - core)
    q_pos, q_seg = own_pos.reshape(-1, 1), own_seg.reshape(-1, 1)
    k_pos = jnp.concatenate([own_pos, par_pos], axis=1).reshape(1, -1)
    k_seg = jnp.concatenate([own_seg, par_seg], axis=1).reshape(1, -1)
    bias = jnp.where((q_seg == k_seg) & (q_pos >= k_pos), 0.0, -1e30).astype(F32)

    kept = []
    residual, normed = own_tokens, None
    low = by_row(cotangent)
    for i in range(layers):
        attn_input = residual
        if i == 0:
            sources, norm = all_tokens, (gains[i][0], shift[i][0])
        else:
            sources, norm = over_z(normed), ()
        attn_rows, queries, kv = project(sources, norm, attn_w[i], qkvo_bias[i], scale)
        par = swap(kv, "c", 1)
        if i == 0:
            _, *cotangents = over_z(low)
        mixed, lse, *parts = attend(queries, kv, par, bias, attn_w[i])
        if i == 0:
            parts, cotangents[1] = tied(parts, cotangents[1])
        else:
            parts, cotangents = tied(parts, cotangents)
        residual, normed = add_and_norm(
            exchanged(parts), residual, shift[i][2], gains[i][1], shift[i][1]
        )
        mlp_input = residual
        mlp_rows, pre, hidden, *parts = feed(over_z(normed), fc_w[i], proj_w[i], fc_bias[i])
        after = min(i + 1, layers - 1)
        if i == layers - 1:
            last_parts = exchanged(parts)
        else:
            residual, normed = add_and_norm(
                exchanged(parts), residual, shift[i][3], gains[after][0], shift[after][0]
            )
        kept.append(
            (attn_input, attn_rows, queries, kv, par, mixed, lse, mlp_input, mlp_rows, pre, hidden)
        )
    gradient = low
    sums = jnp.sum(low.astype(F32), axis=0, keepdims=True)
    last_sums = jnp.concatenate([jnp.zeros((2, WIDTH), F32), sums, jnp.zeros((5, WIDTH), F32)])
    feed_shards, attn_shards = [None] * layers, [None] * layers
    small_sums = [None] * layers
    attn_x = None
    for i in reversed(range(layers)):
        (attn_input, attn_rows, queries, kv, par, mixed, lse, mlp_input, mlp_rows, pre, hidden) = (
            kept[i]
        )
        if i == layers - 1:
            sources = (low, *cotangents)
        else:
            got = swaps_x(attn_x[1])
            sources, got = tied(over_z(low), got)
            done = after_x(attn_x[0], got)
            attn_shards[i + 1] = (done[0], *swaps_y(done[1]))
        grad_rows, d_pre, fc_sum, *parts = feed_back(sources, fc_w[i], proj_w[i], pre)
        feed_grads = weight_grads(False, me, mlp_rows, d_pre, grad_rows, hidden)
        feed_x = after_core(feed_grads[0], swap(feed_grads[1], "c", 1))
        parts, feed_x = tied(exchanged(parts), feed_x)
        if i < layers - 1:
            parts, attn_shards[i + 1] = tied(parts, attn_shards[i + 1])
        gradient, low, feed_sums = norm_back(parts, mlp_input, gains[i][1], gradient)
        got = swaps_x(feed_x[1])
        grad_rows, dq, own_dkv, other_dkv = attend_back(
            over_z(low), attn_w[i], queries, kv, par, bias, lse
        )
        other_dkv, got, last_parts = tied(other_dkv, got, last_parts)
        if i == layers - 1:
            last, _ = add_and_norm(last_parts, residual, shift[i][3], gains[i][0], shift[i][0])
            output = by_position(last.astype(BF16))
        got_dkv = swap(other_dkv, "c", 1)
        done = after_x(feed_x[0], got)
        feed_shards[i] = (done[0], *swaps_y(done[1]))
        d_qkvo, qkvo_sum, *parts = rejoin(
            own_dkv, got_dkv, dq, attn_w[i], all_tokens if i == 0 else ()
        )
        small_sums[i] = [fc_sum, qkvo_sum, feed_sums]
        if i > 0:
            attn_grads = weight_grads(True, me, attn_rows, d_qkvo, grad_rows, mixed)
            attn_x = after_core(attn_grads[0], swap(attn_grads[1], "c", 1))
            parts, attn_x, feed_shards[i] = tied(exchanged(parts), attn_x, feed_shards[i])
            gradient, low, sums = norm_back(parts, attn_input, gains[i][0], gradient)
            small_sums[i].append(sums)
        else:
            small_sums[i].append(parts.pop())
    (fc0, qkvo0, feed0, attn0), (fc1, qkvo1, feed1, attn1) = small_sums
    extra = (fc0, fc1, qkvo0, qkvo1, attn0, feed0, attn1, feed1, last_sums)
    attn_grads = weight_grads(True, me, attn_rows, d_qkvo, grad_rows, mixed, extra)
    attn_x = after_core(attn_grads[0], swap(attn_grads[1], "c", 1))
    parts, attn_x = tied(exchanged(parts), attn_x)
    got = swaps_x(attn_x[1])
    gradient, _, _ = norm_back(parts, attn_input, gains[0][0], gradient)
    done = after_x(attn_x[0], got)
    attn_shards[0] = (done[0], *swaps_y(done[1]))
    g_tokens = by_position(gradient)
    g_w_fc, g_w_proj = finish_feed(feed_shards)
    g_w_qkv, g_w_out, mine = finish_attention(attn_shards)
    everywhere = sum(over_z(mine))
    g_b_fc = lax.dynamic_slice_in_dim(mine[:2], d_own * 32, 32, 1).reshape(layers, 1, 32)
    bias_sums = jnp.stack([mine[2:4, 128:192], mine[2:4, 64:128]], axis=1)
    g_b_qv = lax.dynamic_slice_in_dim(bias_sums, d_own * 8, 8, 2).reshape(layers, 2, 1, 8)
    vectors = everywhere[4:10].reshape(layers, 3, 2, 128)
    g_norm_gains = vectors[:, 0]
    g_shifts = jnp.concatenate([vectors[:, 1], vectors[:, 2]], axis=1)
    return (
        output,
        g_tokens,
        g_w_qkv,
        g_b_qv,
        g_w_out,
        g_w_fc,
        g_b_fc,
        g_w_proj,
        g_norm_gains,
        g_shifts,
    )


def solution(mesh):
    split = Mesh(mesh.devices.reshape(2, 4, 2, 4, 2), ("xl", "y", "xh", "z", "c"))
    dp, tensor = ("xl", "y"), ("xh", "z", "c")
    rows = P(tensor, dp, None)
    weights = (
        P(None, None, dp, tensor),
        P(None, None, tensor, dp),
        P(None, tensor, dp),
        P(None, dp, tensor),
        P(None, tensor, dp),
        P(None, tensor, dp),
        P(None, None, dp),
        P(None, None, dp),
    )
    return jax.shard_map(
        on_device,
        mesh=split,
        in_specs=(rows, P(dp, None), rows, *weights),
        out_specs=(rows, rows, *weights),
        check_vma=False,
    )
```

time: 662 us -> 477 us (0.72)
  waiting for transfers between devices: 46.1 us -> 193 us
  local copies, waits for them, and re-layouts: 176 us -> 46.2 us
  other arithmetic: 121 us -> 7.54 us
  starting transfers between devices: 215 us -> 132 us
  matrix products: 61.2 us -> 0 us
  Pallas kernels: 26.6 us -> 75.2 us
  between operations: 4.6 us -> 16.1 us
    ppermute x157 -> x94, waiting for transfers between devices: 46.1 us -> 192 us  [swap(): return lax.ppermute(value, axis, [(i, i ^ mask) for i in range(count)])]
    ppermute x157 -> x94, starting transfers between devices: 215 us -> 132 us  [swap(): return lax.ppermute(value, axis, [(i, i ^ mask) for i in range(count)])]
    dot_general x24 -> x0, matrix products: 61.2 us -> none  [the longest x8 22.2 us: into_blocks(): return jnp.einsum('nd,tdk->tnk', rows, weight, preferred_element_type=F32)]
    pallas_call x4 -> x36, Pallas kernels: 26.6 us -> 75.2 us  [the longest x31 61.6 us: call(): pl.pallas_call(kernel, grid=grid, in_specs=in_specs, out_specs=out_specs,...]
    another operation x47 -> x11, other arithmetic: 41.6 us -> 1.32 us  [the longest x1 1.11 us: on_device(): early = jnp.stack([early, low, high, both]).reshape(2, 8, *early.shape[1:])]
    reshape x44 -> x3, local copies, waits for them, and re-layouts: 36.6 us -> 0.13 us  [the longest x2 0.12 us: on_device(): early[:, :, 128:, :128].reshape(8, 4, layers, 8, 128)]
    reduce_sum x22 -> x1, other arithmetic: 30.8 us -> 0.05 us  [on_device(): sums = jnp.sum(low.astype(F32), axis=0, keepdims=True)]
    slice x53 -> x11, local copies, waits for them, and re-layouts: 27 us -> 1.36 us  [the longest x1 0.68 us: on_device(): fc_bias[i]]
  transfers between devices with their start and end apart: 157 -> 96, of which waited for: 27 -> 52; matrix products, arithmetic and copies ran while one was open for 47% -> 4% of each run, Pallas kernels for 4% -> 10%
where the time goes in v2:
time: 477 us; the launch traced here: 470 us
  waiting for transfers between devices  193 us (40%)
  starting transfers between devices  132 us (28%)
  Pallas kernels  75.2 us (16%)
  local copies, waits for them, and re-layouts  46.2 us (10%)
  between operations  16.1 us (3%)
  other arithmetic  7.54 us (2%)
    ppermute x94, waiting for transfers between devices, swap(): return lax.ppermute(value, axis, [(i, i ^ mask) for i in range(count)])  192 us
    ppermute x94, starting transfers between devices, swap(): return lax.ppermute(value, axis, [(i, i ^ mask) for i in range(count)])  132 us
    pallas_call x31, Pallas kernels, call(): pl.pallas_call(kernel, grid=grid, in_specs=in_specs, out_specs=out_specs,...  61.6 us
    unnamed x255, local copies, waits for them, and re-layouts  37 us
    pallas_call x5, Pallas kernels, call(): return pl.pallas_call(kernel, grid_spec=spec, **keys)(prefetch, *arrays)  13.6 us
  transfers between devices with their start and end apart: 96, of which 52 were waited for; matrix products, arithmetic and copies ran while one was open for 4% of the time, Pallas kernels for 10%

profile of v2, /device:TPU:0, one launch (start us, length us, event | category | flops | bytes accessed | tf_op | source)
XLA Modules:
  0.0 470.1 jit_solution(8730953934196946944)
XLA Ops:
  29.9 4.2 collective-permute-start.10
  39.1 4.3 collective-permute-done.10.refs_3_
  49.8 11.4 %collective-permute-done.5 = bf16[4,144,256]{2,1,0:T(8,128)(2,1)} collective-permute-done((bf16[4,144,256]{2,1,0:T(8,128)(2,1)S(1)}, bf16[4,144,256]{2,1,0:T(8,128)(2,1)}, u32[]{:S(2)}, u32[]{:S(2)}) %collective-permute-start.5) | collective-permute-done | bytes 294944 | tf_op jit(solution)/shard_map/ppermute | solution.py:27
  79.4 4.8 %collective-permute-start.13 = (bf16[128,1024]{1,0:T(8,128)(2,1)S(1)}, bf16[128,1024]{1,0:T(8,128)(2,1)S(1)}, u32[]{:S(2)}, u32[]{:S(2)}) collective-permute-start(bf16[128,1024]{1,0:T(8,128)(2,1)S(1)} %pad_maximum_fusion.3.g0.g_ref), channel_id=1, source_target_pairs={{0,4},{2,6},{4,0},{6,2},{1,5},{3,7},{5,1},{7,3},{8,12},{10,14},{12... | collective-permute-start | bytes 786440 | tf_op jit(solution)/shard_map/ppermute | solution.py:27
  84.2 5.0 %attend.2 = (bf16[4,512,128]{2,1,0:T(8,128)(2,1)S(1)}, f32[4,512,1]{2,1,0:T(8,128)S(1)}, bf16[128,1024]{1,0:T(8,128)(2,1)S(1)}, bf16[128,1024]{1,0:T(8,128)(2,1)...) custom-call(bf16[4,512,128]{2,1,0:T(8,128)(2,1)S(1)} %get-tuple-element.238.kv_ref, ...), custom_call_target="tpu_custom_call" | custom-call | flops 5819596800 | bytes 7610368 | tf_op jit(solution)/shard_map/attend/pallas_call | solution.py:67
  95.7 4.5 collective-permute-done.14.p1
  100.2 5.7 %collective-permute-done.15.p2 = bf16[128,1024]{1,0:T(8,128)(2,1)S(1)} collective-permute-done((bf16[128,1024]{1,0:T(8,128)(2,1)S(1)}, bf16[128,1024]{1,0:T(8,128)(2,1)S(1)}, u32[]{:S(2)}, u32[]{:S(2)}) %collective-permute-start.15) | collective-permute-done | bytes 262176 | tf_op jit(solution)/shard_map/ppermute | solution.py:27
  114.4 8.8 %collective-permute-done.19.x3 = bf16[128,1024]{1,0:T(8,128)(2,1)} collective-permute-done((bf16[128,1024]{1,0:T(8,128)(2,1)}, bf16[128,1024]{1,0:T(8,128)(2,1)}, u32[]{:S(2)}, u32[]{:S(2)}) %collective-permute-start.19) | collective-permute-done | bytes 262176 | tf_op jit(solution)/shard_map/ppermute | solution.py:27
  126.7 3.8 feed.2
  136.6 3.6 collective-permute-done.20.p1
  140.2 3.7 collective-permute-done.21.p2
  151.1 9.3 %collective-permute-done.25.refs_3_ = bf16[128,1024]{1,0:T(8,128)(2,1)S(1)} collective-permute-done((bf16[128,1024]{1,0:T(8,128)(2,1)S(1)}, bf16[128,1024]{1,0:T(8,128)(2,1)S(1)}, u32[]{:S(2)}, u32[]{:S(2)}) %collective-permute-start.25) | collective-permute-done | bytes 262176 | tf_op jit(solution)/shard_map/ppermute | solution.py:27
  165.3 5.0 %attend.3 = (bf16[4,512,128]{2,1,0:T(8,128)(2,1)S(1)}, f32[4,512,1]{2,1,0:T(8,128)S(1)}, bf16[128,1024]{1,0:T(8,128)(2,1)S(1)}, bf16[128,1024]{1,0:T(8,128)(2,1)...) custom-call(bf16[4,512,128]{2,1,0:T(8,128)(2,1)S(1)} %get-tuple-element.256.kv_ref, ...), custom_call_target="tpu_custom_call" | custom-call | flops 5819596800 | bytes 11542528 | tf_op jit(solution)/shard_map/attend/pallas_call | solution.py:67
  179.3 4.5 collective-permute-done.29.p1
  183.8 5.7 %collective-permute-done.30.p2 = bf16[128,1024]{1,0:T(8,128)(2,1)S(1)} collective-permute-done((bf16[128,1024]{1,0:T(8,128)(2,1)S(1)}, bf16[128,1024]{1,0:T(8,128)(2,1)S(1)}, u32[]{:S(2)}, u32[]{:S(2)}) %collective-permute-start.30) | collective-permute-done | bytes 262176 | tf_op jit(solution)/shard_map/ppermute | solution.py:27
  198.4 8.4 %collective-permute-done.34.x3 = bf16[128,1024]{1,0:T(8,128)(2,1)} collective-permute-done((bf16[128,1024]{1,0:T(8,128)(2,1)}, bf16[128,1024]{1,0:T(8,128)(2,1)}, u32[]{:S(2)}, u32[]{:S(2)}) %collective-permute-start.34) | collective-permute-done | bytes 262176 | tf_op jit(solution)/shard_map/ppermute | solution.py:27
  209.7 3.8 feed.3
  226.3 3.5 collective-permute-done.35.p1
  229.9 6.5 %collective-permute-done.36.p2 = bf16[128,1024]{1,0:T(8,128)(2,1)S(1)} collective-permute-done((bf16[128,1024]{1,0:T(8,128)(2,1)S(1)}, bf16[128,1024]{1,0:T(8,128)(2,1)S(1)}, u32[]{:S(2)}, u32[]{:S(2)}) %collective-permute-start.36) | collective-permute-done | bytes 262176 | tf_op jit(solution)/shard_map/ppermute | solution.py:27
  246.0 14.9 %collective-permute-done.41.g3 = bf16[128,1024]{1,0:T(8,128)(2,1)S(1)} collective-permute-done((bf16[128,1024]{1,0:T(8,128)(2,1)S(1)}, bf16[128,1024]{1,0:T(8,128)(2,1)S(1)}, u32[]{:S(2)}, u32[]{:S(2)}) %collective-permute-start.41) | collective-permute-done | bytes 262176 | tf_op jit(solution)/shard_map/ppermute | solution.py:27
  265.8 8.4 %attend_back.2 = (bf16[512,1024]{1,0:T(8,128)(2,1)S(1)}, bf16[4,512,128]{2,1,0:T(8,128)(2,1)S(1)}, f32[4,512,128]{2,1,0:T(8,128)S(1)}, bf16[4,512,128]{2,1,0:T(8,128)(2,1)S(1)}) custom-call(bf16[128,1024]{1,0:T(8,128)(2,1)S(1)} %get-tuple-element.293.g0, bf16[128,1024]{1,0:T(8,128)(2,1)S(1)} %collective-permute-done.39.g1, ...), custom_call_target="tpu_custom_call" | custom-call | flops 9751756800 | bytes 14163968 | tf_op jit(solution)/shard_map/attend_back/pallas_call | solution.py:67
  288.8 5.3 %collective-permute-start.51 = (bf16[128,1024]{1,0:T(8,128)(2,1)S(1)}, bf16[128,1024]{1,0:T(8,128)(2,1)S(1)}, u32[]{:S(2)}, u32[]{:S(2)}) collective-permute-start(bf16[128,1024]{1,0:T(8,128)(2,1)S(1)} %get-tuple-element.313), channel_id=1, source_target_pairs={{0,4},{2,6},{4,0},{6,2},{1,5},{3,7},{5,1},{7,3},{8,12},{10,14},{12... | collective-permute-start | bytes 786440 | tf_op jit(solution)/shard_map/ppermute | solution.py:27
  310.3 3.6 collective-permute-start.57
  316.0 7.4 %collective-permute-done.59.g3 = bf16[128,1024]{1,0:T(8,128)(2,1)S(1)} collective-permute-done((bf16[128,1024]{1,0:T(8,128)(2,1)S(1)}, bf16[128,1024]{1,0:T(8,128)(2,1)S(1)}, u32[]{:S(2)}, u32[]{:S(2)}) %collective-permute-start.59) | collective-permute-done | bytes 262176 | tf_op jit(solution)/shard_map/ppermute | solution.py:27
  325.6 6.4 %collective-permute-done.62.three = bf16[4,128,256]{2,1,0:T(8,128)(2,1)S(1)} collective-permute-done((bf16[4,128,256]{2,1,0:T(8,128)(2,1)S(1)}, bf16[4,128,256]{2,1,0:T(8,128)(2,1)S(1)}, u32[]{:S(2)}, u32[]{:S(2)}) %collective-permute-start.62) | collective-permute-done | bytes 262176 | tf_op jit(solution)/shard_map/ppermute | solution.py:27
  364.8 6.2 %collective-permute-done.72.g3 = bf16[128,1024]{1,0:T(8,128)(2,1)S(1)} collective-permute-done((bf16[128,1024]{1,0:T(8,128)(2,1)S(1)}, bf16[128,1024]{1,0:T(8,128)(2,1)S(1)}, u32[]{:S(2)}, u32[]{:S(2)}) %collective-permute-start.72) | collective-permute-done | bytes 262176 | tf_op jit(solution)/shard_map/ppermute | solution.py:27
  373.2 8.4 %attend_back.3 = (bf16[512,1024]{1,0:T(8,128)(2,1)S(1)}, bf16[4,512,128]{2,1,0:T(8,128)(2,1)S(1)}, f32[4,512,128]{2,1,0:T(8,128)S(1)}, bf16[4,512,128]{2,1,0:T(8,128)(2,1)S(1)}) custom-call(bf16[128,1024]{1,0:T(8,128)(2,1)S(1)} %get-tuple-element.378.g0, bf16[128,1024]{1,0:T(8,128)(2,1)S(1)} %collective-permute-done.70.g1, ...), custom_call_target="tpu_custom_call" | custom-call | flops 9751756800 | bytes 10231808 | tf_op jit(solution)/shard_map/attend_back/pallas_call | solution.py:67
  386.6 8.2 %collective-permute-done.75.three = bf16[4,256,256]{2,1,0:T(8,128)(2,1)S(1)} collective-permute-done((bf16[4,256,256]{2,1,0:T(8,128)(2,1)S(1)}, bf16[4,256,256]{2,1,0:T(8,128)(2,1)S(1)}, u32[]{:S(2)}, u32[]{:S(2)}) %collective-permute-start.75) | collective-permute-done | bytes 524320 | tf_op jit(solution)/shard_map/ppermute | solution.py:27
  399.3 4.0 weight_grads.7
  403.7 4.6 collective-permute-start.78
  433.9 5.1 %collective-permute-done.82.one = bf16[4,144,256]{2,1,0:T(8,128)(2,1)S(1)} collective-permute-done((bf16[4,144,256]{2,1,0:T(8,128)(2,1)S(1)}, bf16[4,144,256]{2,1,0:T(8,128)(2,1)S(1)}, u32[]{:S(2)}, u32[]{:S(2)}) %collective-permute-start.82) | collective-permute-done | bytes 294944 | tf_op jit(solution)/shard_map/ppermute | solution.py:27
  439.0 5.5 %collective-permute-done.83.two = bf16[4,144,256]{2,1,0:T(8,128)(2,1)S(1)} collective-permute-done((bf16[4,144,256]{2,1,0:T(8,128)(2,1)S(1)}, bf16[4,144,256]{2,1,0:T(8,128)(2,1)S(1)}, u32[]{:S(2)}, u32[]{:S(2)}) %collective-permute-start.83) | collective-permute-done | bytes 294944 | tf_op jit(solution)/shard_map/ppermute | solution.py:27
  (572 shorter events, 259.6 us)
Async XLA Ops:
  7.2 116.6 %all-gather.5.cloned.1.call-start = ((), (), s32[]{:S(2)}) async-start(), calls=%async_computation | async-start | bytes 6488064 | tf_op jit(solution)/shard_map/all_gather | solution.py:698
  26.9 171.5 %all-gather.7.cloned.1.call-start = ((), (), s32[]{:S(2)}) async-start(), calls=%async_computation.1 | async-start | bytes 4325376 | tf_op jit(solution)/shard_map/all_gather | solution.py:699
  34.6 15.2 %collective-permute-start.8 = (bf16[128,1024]{1,0:T(8,128)(2,1)S(1)}, bf16[128,1024]{1,0:T(8,128)(2,1)S(1)}, u32[]{:S(2)}, u32[]{:S(2)}) collective-permute-start(bf16[128,1024]{1,0:T(8,128)(2,1)S(1)} %pad_maximum_fusion.4.refs_0_.x_ref), channel_id=1, source_target_pairs={{0,2},{2,0},{4,6},{6,4},{1,3},{3,1},{5,7},{7,5},{8,10},{10,8},{12,... | collective-permute-start | bytes 786440 | tf_op jit(solution)/shard_map/ppermute | solution.py:27
  35.5 14.3 %collective-permute-start.7 = (bf16[4,144,256]{2,1,0:T(8,128)(2,1)S(1)}, bf16[4,144,256]{2,1,0:T(8,128)(2,1)S(1)}, u32[]{:S(2)}, u32[]{:S(2)}) collective-permute-start(bf16[4,144,256]{2,1,0:T(8,128)(2,1)S(1)} %pad_maximum_fusion.2), channel_id=1, source_target_pairs={{0,72},{8,64},{64,8},{72,0},{1,73},{9,65},{65,9},{73,1},{2,74},{10... | collective-permute-start | bytes 884744 | tf_op jit(solution)/shard_map/ppermute | solution.py:27
  44.1 17.1 %collective-permute-start.5 = (bf16[4,144,256]{2,1,0:T(8,128)(2,1)S(1)}, bf16[4,144,256]{2,1,0:T(8,128)(2,1)}, u32[]{:S(2)}, u32[]{:S(2)}) collective-permute-start(bf16[4,144,256]{2,1,0:T(8,128)(2,1)S(1)} %pad_maximum_fusion.2), channel_id=1, source_target_pairs={{0,64},{8,72},{64,0},{72,8},{1,65},{9,73},{65,1},{73,9},{2,66},{10... | collective-permute-start | bytes 884744 | tf_op jit(solution)/shard_map/ppermute | solution.py:27
  47.1 30.4 %collective-permute-start = (bf16[64,1024]{1,0:T(8,128)(2,1)}, bf16[64,1024]{1,0:T(8,128)(2,1)}, u32[]{:S(2)}, u32[]{:S(2)}) collective-permute-start(bf16[64,1024]{1,0:T(8,128)(2,1)} %select_bitcast_fusion.3), channel_id=1, source_target_pairs={{0,8},{8,0},{1,9},{9,1},{2,10},{10,2},{3,11},{11,3},{4,12},{12,4},... | collective-permute-start | bytes 393224 | tf_op jit(solution)/shard_map/ppermute | solution.py:27
  94.2 14.2 %collective-permute-start.16 = (bf16[128,1024]{1,0:T(8,128)(2,1)S(1)}, bf16[128,1024]{1,0:T(8,128)(2,1)S(1)}, u32[]{:S(2)}, u32[]{:S(2)}) collective-permute-start(bf16[128,1024]{1,0:T(8,128)(2,1)S(1)} %get-tuple-element.247), channel_id=1, source_target_pairs={{0,6},{2,4},{4,2},{6,0},{1,7},{3,5},{5,3},{7,1},{8,14},{10,12},{12... | collective-permute-start | bytes 786440 | tf_op jit(solution)/shard_map/ppermute | solution.py:27
  177.8 14.2 %collective-permute-start.31 = (bf16[128,1024]{1,0:T(8,128)(2,1)S(1)}, bf16[128,1024]{1,0:T(8,128)(2,1)S(1)}, u32[]{:S(2)}, u32[]{:S(2)}) collective-permute-start(bf16[128,1024]{1,0:T(8,128)(2,1)S(1)} %get-tuple-element.270), channel_id=1, source_target_pairs={{0,6},{2,4},{4,2},{6,0},{1,7},{3,5},{5,3},{7,1},{8,14},{10,12},{12... | collective-permute-start | bytes 786440 | tf_op jit(solution)/shard_map/ppermute | solution.py:27
  220.8 15.6 %collective-permute-start.36 = (bf16[128,1024]{1,0:T(8,128)(2,1)S(1)}, bf16[128,1024]{1,0:T(8,128)(2,1)S(1)}, u32[]{:S(2)}, u32[]{:S(2)}) collective-permute-start(bf16[128,1024]{1,0:T(8,128)(2,1)S(1)} %get-tuple-element.276), channel_id=1, source_target_pairs={{0,4},{2,6},{4,0},{6,2},{1,5},{3,7},{5,1},{7,3},{8,12},{10,14},{12... | collective-permute-start | bytes 786440 | tf_op jit(solution)/shard_map/ppermute | solution.py:27
  223.6 14.9 %collective-permute-start.37 = (bf16[128,1024]{1,0:T(8,128)(2,1)S(1)}, bf16[128,1024]{1,0:T(8,128)(2,1)S(1)}, u32[]{:S(2)}, u32[]{:S(2)}) collective-permute-start(bf16[128,1024]{1,0:T(8,128)(2,1)S(1)} %get-tuple-element.277), channel_id=1, source_target_pairs={{0,6},{2,4},{4,2},{6,0},{1,7},{3,5},{5,3},{7,1},{8,14},{10,12},{12... | collective-permute-start | bytes 786440 | tf_op jit(solution)/shard_map/ppermute | solution.py:27
  225.4 19.1 %collective-permute-start.45 = (bf16[128,1024]{1,0:T(8,128)(2,1)S(1)}, bf16[128,1024]{1,0:T(8,128)(2,1)S(1)}, u32[]{:S(2)}, u32[]{:S(2)}) collective-permute-start(bf16[128,1024]{1,0:T(8,128)(2,1)S(1)} %get-tuple-element.300), channel_id=1, source_target_pairs={{0,2},{2,0},{4,6},{6,4},{1,3},{3,1},{5,7},{7,5},{8,10},{10,8},{12,... | collective-permute-start | bytes 786440 | tf_op jit(solution)/shard_map/ppermute | solution.py:27
  239.2 21.7 %collective-permute-start.41 = (bf16[128,1024]{1,0:T(8,128)(2,1)S(1)}, bf16[128,1024]{1,0:T(8,128)(2,1)S(1)}, u32[]{:S(2)}, u32[]{:S(2)}) collective-permute-start(bf16[128,1024]{1,0:T(8,128)(2,1)S(1)} %get-tuple-element.293.g0), channel_id=1, source_target_pairs={{0,6},{2,4},{4,2},{6,0},{1,7},{3,5},{5,3},{7,1},{8,14},{10,12},{12... | collective-permute-start | bytes 786440 | tf_op jit(solution)/shard_map/ppermute | solution.py:27
  241.1 19.8 %collective-permute-start.40 = (bf16[128,1024]{1,0:T(8,128)(2,1)S(1)}, bf16[128,1024]{1,0:T(8,128)(2,1)S(1)}, u32[]{:S(2)}, u32[]{:S(2)}) collective-permute-start(bf16[128,1024]{1,0:T(8,128)(2,1)S(1)} %get-tuple-element.293.g0), channel_id=1, source_target_pairs={{0,4},{2,6},{4,0},{6,2},{1,5},{3,7},{5,1},{7,3},{8,12},{10,14},{12... | collective-permute-start | bytes 786440 | tf_op jit(solution)/shard_map/ppermute | solution.py:27
  241.1 21.3 %collective-permute-start.39 = (bf16[128,1024]{1,0:T(8,128)(2,1)S(1)}, bf16[128,1024]{1,0:T(8,128)(2,1)S(1)}, u32[]{:S(2)}, u32[]{:S(2)}) collective-permute-start(bf16[128,1024]{1,0:T(8,128)(2,1)S(1)} %get-tuple-element.293.g0), channel_id=1, source_target_pairs={{0,2},{2,0},{4,6},{6,4},{1,3},{3,1},{5,7},{7,5},{8,10},{10,8},{12,... | collective-permute-start | bytes 786440 | tf_op jit(solution)/shard_map/ppermute | solution.py:27
  243.3 30.9 %collective-permute-start.46 = (bf16[128,1024]{1,0:T(8,128)(2,1)S(1)}, bf16[128,1024]{1,0:T(8,128)(2,1)S(1)}, u32[]{:S(2)}, u32[]{:S(2)}) collective-permute-start(bf16[128,1024]{1,0:T(8,128)(2,1)S(1)} %get-tuple-element.301), channel_id=1, source_target_pairs={{0,4},{2,6},{4,0},{6,2},{1,5},{3,7},{5,1},{7,3},{8,12},{10,14},{12... | collective-permute-start | bytes 786440 | tf_op jit(solution)/shard_map/ppermute | solution.py:27
  244.6 29.6 %collective-permute-start.47 = (bf16[128,1024]{1,0:T(8,128)(2,1)S(1)}, bf16[128,1024]{1,0:T(8,128)(2,1)S(1)}, u32[]{:S(2)}, u32[]{:S(2)}) collective-permute-start(bf16[128,1024]{1,0:T(8,128)(2,1)S(1)} %get-tuple-element.302), channel_id=1, source_target_pairs={{0,6},{2,4},{4,2},{6,0},{1,7},{3,5},{5,3},{7,1},{8,14},{10,12},{12... | collective-permute-start | bytes 786440 | tf_op jit(solution)/shard_map/ppermute | solution.py:27
  260.9 16.9 %collective-permute-start.43 = (bf16[4,256,256]{2,1,0:T(8,128)(2,1)S(1)}, bf16[4,256,256]{2,1,0:T(8,128)(2,1)S(1)}, u32[]{:S(2)}, u32[]{:S(2)}) collective-permute-start(bf16[4,256,256]{2,1,0:T(8,128)(2,1)S(1)} %get-tuple-element.297), channel_id=1, source_target_pairs={{0,8},{8,0},{64,72},{72,64},{1,9},{9,1},{65,73},{73,65},{2,10},{10... | collective-permute-start | bytes 1572872 | tf_op jit(solution)/shard_map/ppermute | solution.py:27
  262.3 18.1 %collective-permute-start.44 = (bf16[4,256,256]{2,1,0:T(8,128)(2,1)S(1)}, bf16[4,256,256]{2,1,0:T(8,128)(2,1)S(1)}, u32[]{:S(2)}, u32[]{:S(2)}) collective-permute-start(bf16[4,256,256]{2,1,0:T(8,128)(2,1)S(1)} %get-tuple-element.298), channel_id=1, source_target_pairs={{0,72},{8,64},{64,8},{72,0},{1,73},{9,65},{65,9},{73,1},{2,74},{10... | collective-permute-start | bytes 1572872 | tf_op jit(solution)/shard_map/ppermute | solution.py:27
  288.8 15.1 %collective-permute-start.50 = (bf16[128,1024]{1,0:T(8,128)(2,1)S(1)}, bf16[128,1024]{1,0:T(8,128)(2,1)S(1)}, u32[]{:S(2)}, u32[]{:S(2)}) collective-permute-start(bf16[128,1024]{1,0:T(8,128)(2,1)S(1)} %get-tuple-element.312), channel_id=1, source_target_pairs={{0,2},{2,0},{4,6},{6,4},{1,3},{3,1},{5,7},{7,5},{8,10},{10,8},{12,... | collective-permute-start | bytes 786440 | tf_op jit(solution)/shard_map/ppermute | solution.py:27
  288.8 17.3 %collective-permute-start.51 = (bf16[128,1024]{1,0:T(8,128)(2,1)S(1)}, bf16[128,1024]{1,0:T(8,128)(2,1)S(1)}, u32[]{:S(2)}, u32[]{:S(2)}) collective-permute-start(bf16[128,1024]{1,0:T(8,128)(2,1)S(1)} %get-tuple-element.313), channel_id=1, source_target_pairs={{0,4},{2,6},{4,0},{6,2},{1,5},{3,7},{5,1},{7,3},{8,12},{10,14},{12... | collective-permute-start | bytes 786440 | tf_op jit(solution)/shard_map/ppermute | solution.py:27
  294.1 14.9 %collective-permute-start.52 = (bf16[128,1024]{1,0:T(8,128)(2,1)S(1)}, bf16[128,1024]{1,0:T(8,128)(2,1)S(1)}, u32[]{:S(2)}, u32[]{:S(2)}) collective-permute-start(bf16[128,1024]{1,0:T(8,128)(2,1)S(1)} %get-tuple-element.314), channel_id=1, source_target_pairs={{0,6},{2,4},{4,2},{6,0},{1,7},{3,5},{5,3},{7,1},{8,14},{10,12},{12... | collective-permute-start | bytes 786440 | tf_op jit(solution)/shard_map/ppermute | solution.py:27
  310.1 14.0 %collective-permute-start.58 = (bf16[128,1024]{1,0:T(8,128)(2,1)S(1)}, bf16[128,1024]{1,0:T(8,128)(2,1)S(1)}, u32[]{:S(2)}, u32[]{:S(2)}) collective-permute-start(bf16[128,1024]{1,0:T(8,128)(2,1)S(1)} %get-tuple-element.342.g0), channel_id=1, source_target_pairs={{0,4},{2,6},{4,0},{6,2},{1,5},{3,7},{5,1},{7,3},{8,12},{10,14},{12... | collective-permute-start | bytes 786440 | tf_op jit(solution)/shard_map/ppermute | solution.py:27
  340.0 15.2 %collective-permute-start.65 = (bf16[128,1024]{1,0:T(8,128)(2,1)S(1)}, bf16[128,1024]{1,0:T(8,128)(2,1)S(1)}, u32[]{:S(2)}, u32[]{:S(2)}) collective-permute-start(bf16[128,1024]{1,0:T(8,128)(2,1)S(1)} %get-tuple-element.350), channel_id=1, source_target_pairs={{0,6},{2,4},{4,2},{6,0},{1,7},{3,5},{5,3},{7,1},{8,14},{10,12},{12... | collective-permute-start | bytes 786440 | tf_op jit(solution)/shard_map/ppermute | solution.py:27
  361.4 20.1 %collective-permute-start.73 = (bf16[4,256,256]{2,1,0:T(8,128)(2,1)S(1)}, bf16[4,256,256]{2,1,0:T(8,128)(2,1)S(1)}, u32[]{:S(2)}, u32[]{:S(2)}) collective-permute-start(bf16[4,256,256]{2,1,0:T(8,128)(2,1)S(1)} %get-tuple-element.382), channel_id=1, source_target_pairs={{0,64},{8,72},{64,0},{72,8},{1,65},{9,73},{65,1},{73,9},{2,66},{10... | collective-permute-start | bytes 1572872 | tf_op jit(solution)/shard_map/ppermute | solution.py:27
  361.4 24.4 %collective-permute-start.74 = (bf16[4,256,256]{2,1,0:T(8,128)(2,1)S(1)}, bf16[4,256,256]{2,1,0:T(8,128)(2,1)S(1)}, u32[]{:S(2)}, u32[]{:S(2)}) collective-permute-start(bf16[4,256,256]{2,1,0:T(8,128)(2,1)S(1)} %get-tuple-element.383), channel_id=1, source_target_pairs={{0,8},{8,0},{64,72},{72,64},{1,9},{9,1},{65,73},{73,65},{2,10},{10... | collective-permute-start | bytes 1572872 | tf_op jit(solution)/shard_map/ppermute | solution.py:27
  371.0 23.8 %collective-permute-start.75 = (bf16[4,256,256]{2,1,0:T(8,128)(2,1)S(1)}, bf16[4,256,256]{2,1,0:T(8,128)(2,1)S(1)}, u32[]{:S(2)}, u32[]{:S(2)}) collective-permute-start(bf16[4,256,256]{2,1,0:T(8,128)(2,1)S(1)} %get-tuple-element.384), channel_id=1, source_target_pairs={{0,72},{8,64},{64,8},{72,0},{1,73},{9,65},{65,9},{73,1},{2,74},{10... | collective-permute-start | bytes 1572872 | tf_op jit(solution)/shard_map/ppermute | solution.py:27
  403.7 17.2 %collective-permute-start.78 = (bf16[128,1024]{1,0:T(8,128)(2,1)}, bf16[128,1024]{1,0:T(8,128)(2,1)}, u32[]{:S(2)}, u32[]{:S(2)}) collective-permute-start(bf16[128,1024]{1,0:T(8,128)(2,1)} %get-tuple-element.389), channel_id=1, source_target_pairs={{0,4},{2,6},{4,0},{6,2},{1,5},{3,7},{5,1},{7,3},{8,12},{10,14},{12... | collective-permute-start | bytes 786440 | tf_op jit(solution)/shard_map/ppermute | solution.py:27
  408.3 15.2 %collective-permute-start.79 = (bf16[128,1024]{1,0:T(8,128)(2,1)}, bf16[128,1024]{1,0:T(8,128)(2,1)}, u32[]{:S(2)}, u32[]{:S(2)}) collective-permute-start(bf16[128,1024]{1,0:T(8,128)(2,1)} %get-tuple-element.390), channel_id=1, source_target_pairs={{0,6},{2,4},{4,2},{6,0},{1,7},{3,5},{5,3},{7,1},{8,14},{10,12},{12... | collective-permute-start | bytes 786440 | tf_op jit(solution)/shard_map/ppermute | solution.py:27
  412.9 15.5 %collective-permute-start.88 = (bf16[256,256]{1,0:T(8,128)(2,1)S(1)}, bf16[256,256]{1,0:T(8,128)(2,1)S(1)}, u32[]{:S(2)}, u32[]{:S(2)}) collective-permute-start(bf16[256,256]{1,0:T(8,128)(2,1)S(1)} %get-tuple-element.435), channel_id=1, source_target_pairs={{0,16},{16,0},{32,48},{48,32},{1,17},{17,1},{33,49},{49,33},{2,18}... | collective-permute-start | bytes 393224 | tf_op jit(solution)/shard_map/ppermute | solution.py:27
  414.7 15.0 %collective-permute-start.89 = (bf16[256,256]{1,0:T(8,128)(2,1)S(1)}, bf16[256,256]{1,0:T(8,128)(2,1)S(1)}, u32[]{:S(2)}, u32[]{:S(2)}) collective-permute-start(bf16[256,256]{1,0:T(8,128)(2,1)S(1)} %get-tuple-element.436), channel_id=1, source_target_pairs={{0,32},{16,48},{32,0},{48,16},{1,33},{17,49},{33,1},{49,17},{2,34}... | collective-permute-start | bytes 393224 | tf_op jit(solution)/shard_map/ppermute | solution.py:27
  428.4 16.1 %collective-permute-start.83 = (bf16[4,144,256]{2,1,0:T(8,128)(2,1)S(1)}, bf16[4,144,256]{2,1,0:T(8,128)(2,1)S(1)}, u32[]{:S(2)}, u32[]{:S(2)}) collective-permute-start(bf16[4,144,256]{2,1,0:T(8,128)(2,1)S(1)} %get-tuple-element.417), channel_id=1, source_target_pairs={{0,8},{8,0},{64,72},{72,64},{1,9},{9,1},{65,73},{73,65},{2,10},{10... | collective-permute-start | bytes 884744 | tf_op jit(solution)/shard_map/ppermute | solution.py:27
  429.7 15.8 %collective-permute-start.84 = (bf16[4,144,256]{2,1,0:T(8,128)(2,1)S(1)}, bf16[4,144,256]{2,1,0:T(8,128)(2,1)S(1)}, u32[]{:S(2)}, u32[]{:S(2)}) collective-permute-start(bf16[4,144,256]{2,1,0:T(8,128)(2,1)S(1)} %get-tuple-element.418), channel_id=1, source_target_pairs={{0,72},{8,64},{64,8},{72,0},{1,73},{9,65},{65,9},{73,1},{2,74},{10... | collective-permute-start | bytes 884744 | tf_op jit(solution)/shard_map/ppermute | solution.py:27
  (187 other events, 2375.7 us)
Sparse Core Ops, SparseCore 0:
  27.0 73.9 all-gather.4
  102.7 59.0 all-gather.6

commit v3 on v2

--- a/solution.py
+++ b/solution.py
@@ -50,7 +50,7 @@
     return one, two, three
 
 
-def call(kernel, name, grid, ins, outs, scratch=(), flops=0, exps=0, prefetch=None):
+def call(kernel, name, grid, ins, outs, scratch=(), flops=0, exps=0, prefetch=None, vmem=VMEM):
     arrays = [a for a, _, _ in ins]
     in_specs = [pl.BlockSpec(block, index) for _, block, index in ins]
     out_specs = [pl.BlockSpec(block, index) for _, _, block, index in outs]
@@ -60,8 +60,10 @@
     keys = dict(
         out_shape=shapes,
         name=name,
-        compiler_params=pltpu.CompilerParams(vmem_limit_bytes=VMEM),
-        cost_estimate=pl.CostEstimate(flops=flops, bytes_accessed=moved, transcendentals=exps),
+        compiler_params=pltpu.CompilerParams(vmem_limit_bytes=vmem),
+        cost_estimate=pl.CostEstimate(
+            flops=flops // 10, bytes_accessed=moved // 10, transcendentals=exps // 10
+        ),
     )
     if prefetch is None:
         return pl.pallas_call(
@@ -584,6 +586,7 @@
             out_whole((384, 256), BF16),
             out_whole((256, 256), BF16),
         ],
+        vmem=56 << 20,
     )
 
 
@@ -671,12 +674,12 @@
     first = xh == 0
     block = tokens.shape[0]
 
-    def by_row(value):
-        kept = jnp.where(first, value[:, 0], value[:, 1])
-        got = swap(jnp.where(first, value[:, 1], value[:, 0]), "xh", 1)
-        return jnp.concatenate(
-            [jnp.where(first, kept, got), jnp.where(first, got, kept)], axis=0
-        )
+    def by_row(values):
+        both = jnp.stack(values)
+        kept = jnp.where(first, both[:, :, 0], both[:, :, 1])
+        got = swap(jnp.where(first, both[:, :, 1], both[:, :, 0]), "xh", 1)
+        lower, upper = jnp.where(first, kept, got), jnp.where(first, got, kept)
+        return [jnp.concatenate([lower[k], upper[k]], axis=0) for k in range(len(values))]
 
     def by_position(value):
         lower, upper = value[:block], value[block:]
@@ -684,16 +687,15 @@
         got = swap(jnp.where(first, upper, lower).astype(BF16), "xh", 1).astype(value.dtype)
         return jnp.stack([jnp.where(first, kept, got), jnp.where(first, got, kept)], axis=1)
 
-    own_tokens = by_row(tokens)
-
     early, late, last = pack(w_qkv, w_out, w_fc, w_proj, b_qv, b_fc, norm_gains, shifts)
     one, three, two = (swap(early, "y", k) for k in (1, 3, 2))
     early = jnp.stack([early, one, two, three])
-    early, own_tokens, late = tied(early, own_tokens, late)
+    early, tokens, cotangent = tied(early, tokens, cotangent)
+    others = swaps_x([early] * 3)
+    own_tokens, low = by_row([tokens, cotangent])
     all_tokens = over_z(own_tokens)
-    low, high, both = swaps_x([early] * 3)
-    low, high, both, all_tokens = tied(low, high, both, all_tokens)
-    early = jnp.stack([early, low, high, both]).reshape(2, 8, *early.shape[1:])
+    others, all_tokens = tied(others, all_tokens)
+    early = jnp.stack([early, *others]).reshape(2, 8, *early.shape[1:])
     early = merge(me, early, swap(early, "c", 1))
     late = lax.all_gather(late, PLANE, axis=0, tiled=False).reshape(8, 4, *late.shape)
     last = lax.all_gather(last, PLANE, axis=0, tiled=False).reshape(8, 4, *last.shape)
@@ -738,7 +740,6 @@
 
     kept = []
     residual, normed = own_tokens, None
-    low = by_row(cotangent)
     for i in range(layers):
         attn_input = residual
         if i == 0:

time: 477 us -> 470 us (0.985)
  waiting for transfers between devices: 193 us -> 175 us
  starting transfers between devices: 132 us -> 146 us
    ppermute x94 -> x93, waiting for transfers between devices: 192 us -> 175 us  [swap(): return lax.ppermute(value, axis, [(i, i ^ mask) for i in range(count)])]
    ppermute x94 -> x93, starting transfers between devices: 132 us -> 146 us  [swap(): return lax.ppermute(value, axis, [(i, i ^ mask) for i in range(count)])]
    unnamed x255 -> x229, local copies, waits for them, and re-layouts: 37 us -> 36.3 us
  transfers between devices with their start and end apart: 96 -> 95, of which waited for: 52 -> 57; matrix products, arithmetic and copies ran while one was open for 4% -> 3% of each run, Pallas kernels for 10% -> 10%
where the time goes in v3:
time: 470 us; the launch traced here: 465 us
  waiting for transfers between devices  175 us (37%)
  starting transfers between devices  146 us (31%)
  Pallas kernels  78.1 us (17%)
  local copies, waits for them, and re-layouts  44.5 us (9%)
  between operations  15.9 us (3%)
  other arithmetic  5.38 us (1%)
    ppermute x93, waiting for transfers between devices, swap(): return lax.ppermute(value, axis, [(i, i ^ mask) for i in range(count)])  175 us
    ppermute x93, starting transfers between devices, swap(): return lax.ppermute(value, axis, [(i, i ^ mask) for i in range(count)])  146 us
    pallas_call x31, Pallas kernels, call(): pl.pallas_call(kernel, grid=grid, in_specs=in_specs, out_specs=out_specs,...  64.4 us
    unnamed x229, local copies, waits for them, and re-layouts  36.3 us
    pallas_call x5, Pallas kernels, call(): return pl.pallas_call(kernel, grid_spec=spec, **keys)(prefetch, *arrays)  13.6 us
  transfers between devices with their start and end apart: 95, of which 57 were waited for; matrix products, arithmetic and copies ran while one was open for 3% of the time, Pallas kernels for 10%

profile of v3, /device:TPU:0, one launch (start us, length us, event | category | flops | bytes accessed | tf_op | source)
XLA Modules:
  0.0 465.1 jit_solution(15070320714634070474)
XLA Ops:
  31.5 7.0 %collective-permute-done.3 = bf16[2,64,1024]{2,1,0:T(8,128)(2,1)S(1)} collective-permute-done((bf16[2,64,1024]{2,1,0:T(8,128)(2,1)S(1)}, bf16[2,64,1024]{2,1,0:T(8,128)(2,1)S(1)}, u32[]{:S(2)}, u32[]{:S(2)}) %collective-permute-start.3) | collective-permute-done | bytes 262176 | tf_op jit(solution)/shard_map/ppermute | solution.py:27
  40.0 3.8 collective-permute-start.9
  48.0 4.4 collective-permute-done.4
  74.1 5.0 %attend.2 = (bf16[4,512,128]{2,1,0:T(8,128)(2,1)S(1)}, f32[4,512,1]{2,1,0:T(8,128)S(1)}, bf16[128,1024]{1,0:T(8,128)(2,1)S(1)}, bf16[128,1024]{1,0:T(8,128)(2,1)...) custom-call(bf16[4,512,128]{2,1,0:T(8,128)(2,1)S(1)} %get-tuple-element.238.kv_ref, ...), custom_call_target="tpu_custom_call" | custom-call | flops 581959680 | bytes 761036 | tf_op jit(solution)/shard_map/attend/pallas_call | solution.py:69
  81.6 9.0 %collective-permute-start.13 = (bf16[128,1024]{1,0:T(8,128)(2,1)S(1)}, bf16[128,1024]{1,0:T(8,128)(2,1)S(1)}, u32[]{:S(2)}, u32[]{:S(2)}) collective-permute-start(bf16[128,1024]{1,0:T(8,128)(2,1)S(1)} %get-tuple-element.245), channel_id=1, source_target_pairs={{0,2},{2,0},{4,6},{6,4},{1,3},{3,1},{5,7},{7,5},{8,10},{10,8},{12,... | collective-permute-start | bytes 786440 | tf_op jit(solution)/shard_map/ppermute | solution.py:27
  90.6 3.8 collective-permute-start.14
  94.8 4.5 collective-permute-done.13.p1
  99.3 6.5 %collective-permute-done.14.p2 = bf16[128,1024]{1,0:T(8,128)(2,1)S(1)} collective-permute-done((bf16[128,1024]{1,0:T(8,128)(2,1)S(1)}, bf16[128,1024]{1,0:T(8,128)(2,1)S(1)}, u32[]{:S(2)}, u32[]{:S(2)}) %collective-permute-start.14) | collective-permute-done | bytes 262176 | tf_op jit(solution)/shard_map/ppermute | solution.py:27
  115.1 8.8 %collective-permute-done.18.x3 = bf16[128,1024]{1,0:T(8,128)(2,1)} collective-permute-done((bf16[128,1024]{1,0:T(8,128)(2,1)}, bf16[128,1024]{1,0:T(8,128)(2,1)}, u32[]{:S(2)}, u32[]{:S(2)}) %collective-permute-start.18) | collective-permute-done | bytes 262176 | tf_op jit(solution)/shard_map/ppermute | solution.py:27
  127.5 3.8 feed.2
  137.3 4.5 collective-permute-done.19.p1
  152.6 9.2 %collective-permute-done.24.refs_3_ = bf16[128,1024]{1,0:T(8,128)(2,1)S(1)} collective-permute-done((bf16[128,1024]{1,0:T(8,128)(2,1)S(1)}, bf16[128,1024]{1,0:T(8,128)(2,1)S(1)}, u32[]{:S(2)}, u32[]{:S(2)}) %collective-permute-start.24) | collective-permute-done | bytes 262176 | tf_op jit(solution)/shard_map/ppermute | solution.py:27
  167.3 5.1 %attend.3 = (bf16[4,512,128]{2,1,0:T(8,128)(2,1)S(1)}, f32[4,512,1]{2,1,0:T(8,128)S(1)}, bf16[128,1024]{1,0:T(8,128)(2,1)S(1)}, bf16[128,1024]{1,0:T(8,128)(2,1)...) custom-call(bf16[4,512,128]{2,1,0:T(8,128)(2,1)S(1)} %get-tuple-element.256.kv_ref, ...), custom_call_target="tpu_custom_call" | custom-call | flops 581959680 | bytes 1154252 | tf_op jit(solution)/shard_map/attend/pallas_call | solution.py:69
  181.4 4.5 collective-permute-done.28.p1
  185.9 6.0 %collective-permute-done.29.p2 = bf16[128,1024]{1,0:T(8,128)(2,1)S(1)} collective-permute-done((bf16[128,1024]{1,0:T(8,128)(2,1)S(1)}, bf16[128,1024]{1,0:T(8,128)(2,1)S(1)}, u32[]{:S(2)}, u32[]{:S(2)}) %collective-permute-start.29) | collective-permute-done | bytes 262176 | tf_op jit(solution)/shard_map/ppermute | solution.py:27
  201.3 8.8 %collective-permute-done.33.x3 = bf16[128,1024]{1,0:T(8,128)(2,1)} collective-permute-done((bf16[128,1024]{1,0:T(8,128)(2,1)}, bf16[128,1024]{1,0:T(8,128)(2,1)}, u32[]{:S(2)}, u32[]{:S(2)}) %collective-permute-start.33) | collective-permute-done | bytes 262176 | tf_op jit(solution)/shard_map/ppermute | solution.py:27
  212.9 3.8 feed.3
  229.6 3.5 collective-permute-done.34.p1
  233.1 5.8 %collective-permute-done.35.p2 = bf16[128,1024]{1,0:T(8,128)(2,1)S(1)} collective-permute-done((bf16[128,1024]{1,0:T(8,128)(2,1)S(1)}, bf16[128,1024]{1,0:T(8,128)(2,1)S(1)}, u32[]{:S(2)}, u32[]{:S(2)}) %collective-permute-start.35) | collective-permute-done | bytes 262176 | tf_op jit(solution)/shard_map/ppermute | solution.py:27
  246.0 6.6 %collective-permute-start.41 = (bf16[4,256,256]{2,1,0:T(8,128)(2,1)S(1)}, bf16[4,256,256]{2,1,0:T(8,128)(2,1)S(1)}, u32[]{:S(2)}, u32[]{:S(2)}) collective-permute-start(bf16[4,256,256]{2,1,0:T(8,128)(2,1)S(1)} %get-tuple-element.296), channel_id=1, source_target_pairs={{0,64},{8,72},{64,0},{72,8},{1,65},{9,73},{65,1},{73,9},{2,66},{10... | collective-permute-start | bytes 1572872 | tf_op jit(solution)/shard_map/ppermute | solution.py:27
  260.2 8.4 %attend_back.2 = (bf16[512,1024]{1,0:T(8,128)(2,1)S(1)}, bf16[4,512,128]{2,1,0:T(8,128)(2,1)S(1)}, f32[4,512,128]{2,1,0:T(8,128)S(1)}, bf16[4,512,128]{2,1,0:T(8,128)(2,1)S(1)}) custom-call(bf16[128,1024]{1,0:T(8,128)(2,1)S(1)} %get-tuple-element.293.g0, bf16[128,1024]{1,0:T(8,128)(2,1)S(1)} %collective-permute-done.38.g1, ...), custom_call_target="tpu_custom_call" | custom-call | flops 975175680 | bytes 1416396 | tf_op jit(solution)/shard_map/attend_back/pallas_call | solution.py:69
  271.3 3.5 collective-permute-done.42.two
  274.8 5.4 %collective-permute-done.43.three = bf16[4,256,256]{2,1,0:T(8,128)(2,1)S(1)} collective-permute-done((bf16[4,256,256]{2,1,0:T(8,128)(2,1)S(1)}, bf16[4,256,256]{2,1,0:T(8,128)(2,1)S(1)}, u32[]{:S(2)}, u32[]{:S(2)}) %collective-permute-start.43) | collective-permute-done | bytes 524320 | tf_op jit(solution)/shard_map/ppermute | solution.py:27
  287.3 5.2 %collective-permute-start.50 = (bf16[128,1024]{1,0:T(8,128)(2,1)S(1)}, bf16[128,1024]{1,0:T(8,128)(2,1)S(1)}, u32[]{:S(2)}, u32[]{:S(2)}) collective-permute-start(bf16[128,1024]{1,0:T(8,128)(2,1)S(1)} %get-tuple-element.313), channel_id=1, source_target_pairs={{0,4},{2,6},{4,0},{6,2},{1,5},{3,7},{5,1},{7,3},{8,12},{10,14},{12... | collective-permute-start | bytes 786440 | tf_op jit(solution)/shard_map/ppermute | solution.py:27
  312.1 4.2 collective-permute-start.59
  317.3 4.6 collective-permute-done.58.g3
  323.5 4.0 collective-permute-done.60.two
  327.5 5.5 %collective-permute-done.61.three = bf16[4,128,256]{2,1,0:T(8,128)(2,1)S(1)} collective-permute-done((bf16[4,128,256]{2,1,0:T(8,128)(2,1)S(1)}, bf16[4,128,256]{2,1,0:T(8,128)(2,1)S(1)}, u32[]{:S(2)}, u32[]{:S(2)}) %collective-permute-start.61) | collective-permute-done | bytes 262176 | tf_op jit(solution)/shard_map/ppermute | solution.py:27
  367.8 7.3 %collective-permute-done.70.g2 = bf16[128,1024]{1,0:T(8,128)(2,1)S(1)} collective-permute-done((bf16[128,1024]{1,0:T(8,128)(2,1)S(1)}, bf16[128,1024]{1,0:T(8,128)(2,1)S(1)}, u32[]{:S(2)}, u32[]{:S(2)}) %collective-permute-start.70) | collective-permute-done | bytes 262176 | tf_op jit(solution)/shard_map/ppermute | solution.py:27
  375.8 8.4 %attend_back.3 = (bf16[512,1024]{1,0:T(8,128)(2,1)S(1)}, bf16[4,512,128]{2,1,0:T(8,128)(2,1)S(1)}, f32[4,512,128]{2,1,0:T(8,128)S(1)}, bf16[4,512,128]{2,1,0:T(8,128)(2,1)S(1)}) custom-call(bf16[128,1024]{1,0:T(8,128)(2,1)S(1)} %get-tuple-element.378.g0, bf16[128,1024]{1,0:T(8,128)(2,1)S(1)} %collective-permute-done.69.g1, ...), custom_call_target="tpu_custom_call" | custom-call | flops 975175680 | bytes 1023180 | tf_op jit(solution)/shard_map/attend_back/pallas_call | solution.py:69
  393.0 4.0 weight_grads.7
  431.0 5.7 %collective-permute-done.82.two = bf16[4,144,256]{2,1,0:T(8,128)(2,1)S(1)} collective-permute-done((bf16[4,144,256]{2,1,0:T(8,128)(2,1)S(1)}, bf16[4,144,256]{2,1,0:T(8,128)(2,1)S(1)}, u32[]{:S(2)}, u32[]{:S(2)}) %collective-permute-start.82) | collective-permute-done | bytes 294944 | tf_op jit(solution)/shard_map/ppermute | solution.py:27
  (541 shorter events, 268.7 us)
Async XLA Ops:
  7.2 117.4 %all-gather.5.cloned.1.call-start = ((), (), s32[]{:S(2)}) async-start(), calls=%async_computation | async-start | bytes 6488064 | tf_op jit(solution)/shard_map/all_gather | solution.py:700
  13.5 187.8 %all-gather.7.cloned.1.call-start = ((), (), s32[]{:S(2)}) async-start(), calls=%async_computation.1 | async-start | bytes 4325376 | tf_op jit(solution)/shard_map/all_gather | solution.py:701
  24.1 14.5 %collective-permute-start.3 = (bf16[2,64,1024]{2,1,0:T(8,128)(2,1)S(1)}, bf16[2,64,1024]{2,1,0:T(8,128)(2,1)S(1)}, u32[]{:S(2)}, u32[]{:S(2)}) collective-permute-start(bf16[2,64,1024]{2,1,0:T(8,128)(2,1)S(1)} %select_bitcast_fusion), channel_id=1, source_target_pairs={{0,8},{8,0},{1,9},{9,1},{2,10},{10,2},{3,11},{11,3},{4,12},{12,4},... | collective-permute-start | bytes 786440 | tf_op jit(solution)/shard_map/ppermute | solution.py:27
  27.4 17.0 %collective-permute-start.6 = (bf16[4,144,256]{2,1,0:T(8,128)(2,1)S(1)}, bf16[4,144,256]{2,1,0:T(8,128)(2,1)S(1)}, u32[]{:S(2)}, u32[]{:S(2)}) collective-permute-start(bf16[4,144,256]{2,1,0:T(8,128)(2,1)S(1)} %pad_maximum_fusion.2), channel_id=1, source_target_pairs={{0,72},{8,64},{64,8},{72,0},{1,73},{9,65},{65,9},{73,1},{2,74},{10... | collective-permute-start | bytes 884744 | tf_op jit(solution)/shard_map/ppermute | solution.py:27
  28.6 19.4 %collective-permute-start.5 = (bf16[4,144,256]{2,1,0:T(8,128)(2,1)S(1)}, bf16[4,144,256]{2,1,0:T(8,128)(2,1)S(1)}, u32[]{:S(2)}, u32[]{:S(2)}) collective-permute-start(bf16[4,144,256]{2,1,0:T(8,128)(2,1)S(1)} %pad_maximum_fusion.2), channel_id=1, source_target_pairs={{0,8},{8,0},{64,72},{72,64},{1,9},{9,1},{65,73},{73,65},{2,10},{10... | collective-permute-start | bytes 884744 | tf_op jit(solution)/shard_map/ppermute | solution.py:27
  30.1 22.2 %collective-permute-start.4 = (bf16[4,144,256]{2,1,0:T(8,128)(2,1)S(1)}, bf16[4,144,256]{2,1,0:T(8,128)(2,1)S(1)}, u32[]{:S(2)}, u32[]{:S(2)}) collective-permute-start(bf16[4,144,256]{2,1,0:T(8,128)(2,1)S(1)} %pad_maximum_fusion.2), channel_id=1, source_target_pairs={{0,64},{8,72},{64,0},{72,8},{1,65},{9,73},{65,1},{73,9},{2,66},{10... | collective-permute-start | bytes 884744 | tf_op jit(solution)/shard_map/ppermute | solution.py:27
  81.6 17.8 %collective-permute-start.13 = (bf16[128,1024]{1,0:T(8,128)(2,1)S(1)}, bf16[128,1024]{1,0:T(8,128)(2,1)S(1)}, u32[]{:S(2)}, u32[]{:S(2)}) collective-permute-start(bf16[128,1024]{1,0:T(8,128)(2,1)S(1)} %get-tuple-element.245), channel_id=1, source_target_pairs={{0,2},{2,0},{4,6},{6,4},{1,3},{3,1},{5,7},{7,5},{8,10},{10,8},{12,... | collective-permute-start | bytes 786440 | tf_op jit(solution)/shard_map/ppermute | solution.py:27
  90.6 15.3 %collective-permute-start.14 = (bf16[128,1024]{1,0:T(8,128)(2,1)S(1)}, bf16[128,1024]{1,0:T(8,128)(2,1)S(1)}, u32[]{:S(2)}, u32[]{:S(2)}) collective-permute-start(bf16[128,1024]{1,0:T(8,128)(2,1)S(1)} %get-tuple-element.246), channel_id=1, source_target_pairs={{0,4},{2,6},{4,0},{6,2},{1,5},{3,7},{5,1},{7,3},{8,12},{10,14},{12... | collective-permute-start | bytes 786440 | tf_op jit(solution)/shard_map/ppermute | solution.py:27
  177.0 15.0 %collective-permute-start.29 = (bf16[128,1024]{1,0:T(8,128)(2,1)S(1)}, bf16[128,1024]{1,0:T(8,128)(2,1)S(1)}, u32[]{:S(2)}, u32[]{:S(2)}) collective-permute-start(bf16[128,1024]{1,0:T(8,128)(2,1)S(1)} %get-tuple-element.269), channel_id=1, source_target_pairs={{0,4},{2,6},{4,0},{6,2},{1,5},{3,7},{5,1},{7,3},{8,12},{10,14},{12... | collective-permute-start | bytes 786440 | tf_op jit(solution)/shard_map/ppermute | solution.py:27
  224.0 14.9 %collective-permute-start.35 = (bf16[128,1024]{1,0:T(8,128)(2,1)S(1)}, bf16[128,1024]{1,0:T(8,128)(2,1)S(1)}, u32[]{:S(2)}, u32[]{:S(2)}) collective-permute-start(bf16[128,1024]{1,0:T(8,128)(2,1)S(1)} %get-tuple-element.276), channel_id=1, source_target_pairs={{0,4},{2,6},{4,0},{6,2},{1,5},{3,7},{5,1},{7,3},{8,12},{10,14},{12... | collective-permute-start | bytes 786440 | tf_op jit(solution)/shard_map/ppermute | solution.py:27
  226.1 14.9 %collective-permute-start.36 = (bf16[128,1024]{1,0:T(8,128)(2,1)S(1)}, bf16[128,1024]{1,0:T(8,128)(2,1)S(1)}, u32[]{:S(2)}, u32[]{:S(2)}) collective-permute-start(bf16[128,1024]{1,0:T(8,128)(2,1)S(1)} %get-tuple-element.277), channel_id=1, source_target_pairs={{0,6},{2,4},{4,2},{6,0},{1,7},{3,5},{5,3},{7,1},{8,14},{10,12},{12... | collective-permute-start | bytes 786440 | tf_op jit(solution)/shard_map/ppermute | solution.py:27
  228.7 23.9 %collective-permute-start.44 = (bf16[128,1024]{1,0:T(8,128)(2,1)S(1)}, bf16[128,1024]{1,0:T(8,128)(2,1)S(1)}, u32[]{:S(2)}, u32[]{:S(2)}) collective-permute-start(bf16[128,1024]{1,0:T(8,128)(2,1)S(1)} %get-tuple-element.300), channel_id=1, source_target_pairs={{0,2},{2,0},{4,6},{6,4},{1,3},{3,1},{5,7},{7,5},{8,10},{10,8},{12,... | collective-permute-start | bytes 786440 | tf_op jit(solution)/shard_map/ppermute | solution.py:27
  241.6 14.1 %collective-permute-start.40 = (bf16[128,1024]{1,0:T(8,128)(2,1)S(1)}, bf16[128,1024]{1,0:T(8,128)(2,1)S(1)}, u32[]{:S(2)}, u32[]{:S(2)}) collective-permute-start(bf16[128,1024]{1,0:T(8,128)(2,1)S(1)} %get-tuple-element.293.g0), channel_id=1, source_target_pairs={{0,6},{2,4},{4,2},{6,0},{1,7},{3,5},{5,3},{7,1},{8,14},{10,12},{12... | collective-permute-start | bytes 786440 | tf_op jit(solution)/shard_map/ppermute | solution.py:27
  246.0 25.4 %collective-permute-start.41 = (bf16[4,256,256]{2,1,0:T(8,128)(2,1)S(1)}, bf16[4,256,256]{2,1,0:T(8,128)(2,1)S(1)}, u32[]{:S(2)}, u32[]{:S(2)}) collective-permute-start(bf16[4,256,256]{2,1,0:T(8,128)(2,1)S(1)} %get-tuple-element.296), channel_id=1, source_target_pairs={{0,64},{8,72},{64,0},{72,8},{1,65},{9,73},{65,1},{73,9},{2,66},{10... | collective-permute-start | bytes 1572872 | tf_op jit(solution)/shard_map/ppermute | solution.py:27
  253.3 21.5 %collective-permute-start.42 = (bf16[4,256,256]{2,1,0:T(8,128)(2,1)S(1)}, bf16[4,256,256]{2,1,0:T(8,128)(2,1)S(1)}, u32[]{:S(2)}, u32[]{:S(2)}) collective-permute-start(bf16[4,256,256]{2,1,0:T(8,128)(2,1)S(1)} %get-tuple-element.297), channel_id=1, source_target_pairs={{0,8},{8,0},{64,72},{72,64},{1,9},{9,1},{65,73},{73,65},{2,10},{10... | collective-permute-start | bytes 1572872 | tf_op jit(solution)/shard_map/ppermute | solution.py:27
  255.8 24.4 %collective-permute-start.43 = (bf16[4,256,256]{2,1,0:T(8,128)(2,1)S(1)}, bf16[4,256,256]{2,1,0:T(8,128)(2,1)S(1)}, u32[]{:S(2)}, u32[]{:S(2)}) collective-permute-start(bf16[4,256,256]{2,1,0:T(8,128)(2,1)S(1)} %get-tuple-element.298), channel_id=1, source_target_pairs={{0,72},{8,64},{64,8},{72,0},{1,73},{9,65},{65,9},{73,1},{2,74},{10... | collective-permute-start | bytes 1572872 | tf_op jit(solution)/shard_map/ppermute | solution.py:27
  287.2 15.1 %collective-permute-start.49 = (bf16[128,1024]{1,0:T(8,128)(2,1)S(1)}, bf16[128,1024]{1,0:T(8,128)(2,1)S(1)}, u32[]{:S(2)}, u32[]{:S(2)}) collective-permute-start(bf16[128,1024]{1,0:T(8,128)(2,1)S(1)} %get-tuple-element.312), channel_id=1, source_target_pairs={{0,2},{2,0},{4,6},{6,4},{1,3},{3,1},{5,7},{7,5},{8,10},{10,8},{12,... | collective-permute-start | bytes 786440 | tf_op jit(solution)/shard_map/ppermute | solution.py:27
  287.3 17.4 %collective-permute-start.50 = (bf16[128,1024]{1,0:T(8,128)(2,1)S(1)}, bf16[128,1024]{1,0:T(8,128)(2,1)S(1)}, u32[]{:S(2)}, u32[]{:S(2)}) collective-permute-start(bf16[128,1024]{1,0:T(8,128)(2,1)S(1)} %get-tuple-element.313), channel_id=1, source_target_pairs={{0,4},{2,6},{4,0},{6,2},{1,5},{3,7},{5,1},{7,3},{8,12},{10,14},{12... | collective-permute-start | bytes 786440 | tf_op jit(solution)/shard_map/ppermute | solution.py:27
  292.4 14.8 %collective-permute-start.51 = (bf16[128,1024]{1,0:T(8,128)(2,1)S(1)}, bf16[128,1024]{1,0:T(8,128)(2,1)S(1)}, u32[]{:S(2)}, u32[]{:S(2)}) collective-permute-start(bf16[128,1024]{1,0:T(8,128)(2,1)S(1)} %get-tuple-element.314), channel_id=1, source_target_pairs={{0,6},{2,4},{4,2},{6,0},{1,7},{3,5},{5,3},{7,1},{8,14},{10,12},{12... | collective-permute-start | bytes 786440 | tf_op jit(solution)/shard_map/ppermute | solution.py:27
  308.3 15.1 %collective-permute-start.57 = (bf16[128,1024]{1,0:T(8,128)(2,1)S(1)}, bf16[128,1024]{1,0:T(8,128)(2,1)S(1)}, u32[]{:S(2)}, u32[]{:S(2)}) collective-permute-start(bf16[128,1024]{1,0:T(8,128)(2,1)S(1)} %get-tuple-element.342.g0), channel_id=1, source_target_pairs={{0,4},{2,6},{4,0},{6,2},{1,5},{3,7},{5,1},{7,3},{8,12},{10,14},{12... | collective-permute-start | bytes 786440 | tf_op jit(solution)/shard_map/ppermute | solution.py:27
  308.6 14.7 %collective-permute-start.56 = (bf16[128,1024]{1,0:T(8,128)(2,1)S(1)}, bf16[128,1024]{1,0:T(8,128)(2,1)S(1)}, u32[]{:S(2)}, u32[]{:S(2)}) collective-permute-start(bf16[128,1024]{1,0:T(8,128)(2,1)S(1)} %get-tuple-element.342.g0), channel_id=1, source_target_pairs={{0,2},{2,0},{4,6},{6,4},{1,3},{3,1},{5,7},{7,5},{8,10},{10,8},{12,... | collective-permute-start | bytes 786440 | tf_op jit(solution)/shard_map/ppermute | solution.py:27
  339.6 14.5 %collective-permute-start.63 = (bf16[128,1024]{1,0:T(8,128)(2,1)S(1)}, bf16[128,1024]{1,0:T(8,128)(2,1)S(1)}, u32[]{:S(2)}, u32[]{:S(2)}) collective-permute-start(bf16[128,1024]{1,0:T(8,128)(2,1)S(1)} %get-tuple-element.349), channel_id=1, source_target_pairs={{0,4},{2,6},{4,0},{6,2},{1,5},{3,7},{5,1},{7,3},{8,12},{10,14},{12... | collective-permute-start | bytes 786440 | tf_op jit(solution)/shard_map/ppermute | solution.py:27
  341.5 14.9 %collective-permute-start.64 = (bf16[128,1024]{1,0:T(8,128)(2,1)S(1)}, bf16[128,1024]{1,0:T(8,128)(2,1)S(1)}, u32[]{:S(2)}, u32[]{:S(2)}) collective-permute-start(bf16[128,1024]{1,0:T(8,128)(2,1)S(1)} %get-tuple-element.350), channel_id=1, source_target_pairs={{0,6},{2,4},{4,2},{6,0},{1,7},{3,5},{5,3},{7,1},{8,14},{10,12},{12... | collective-permute-start | bytes 786440 | tf_op jit(solution)/shard_map/ppermute | solution.py:27
  360.0 24.2 %collective-permute-start.72 = (bf16[4,256,256]{2,1,0:T(8,128)(2,1)S(1)}, bf16[4,256,256]{2,1,0:T(8,128)(2,1)S(1)}, u32[]{:S(2)}, u32[]{:S(2)}) collective-permute-start(bf16[4,256,256]{2,1,0:T(8,128)(2,1)S(1)} %get-tuple-element.382), channel_id=1, source_target_pairs={{0,64},{8,72},{64,0},{72,8},{1,65},{9,73},{65,1},{73,9},{2,66},{10... | collective-permute-start | bytes 1572872 | tf_op jit(solution)/shard_map/ppermute | solution.py:27
  361.1 23.9 %collective-permute-start.73 = (bf16[4,256,256]{2,1,0:T(8,128)(2,1)S(1)}, bf16[4,256,256]{2,1,0:T(8,128)(2,1)S(1)}, u32[]{:S(2)}, u32[]{:S(2)}) collective-permute-start(bf16[4,256,256]{2,1,0:T(8,128)(2,1)S(1)} %get-tuple-element.383), channel_id=1, source_target_pairs={{0,8},{8,0},{64,72},{72,64},{1,9},{9,1},{65,73},{73,65},{2,10},{10... | collective-permute-start | bytes 1572872 | tf_op jit(solution)/shard_map/ppermute | solution.py:27
  363.1 24.4 %collective-permute-start.74 = (bf16[4,256,256]{2,1,0:T(8,128)(2,1)S(1)}, bf16[4,256,256]{2,1,0:T(8,128)(2,1)S(1)}, u32[]{:S(2)}, u32[]{:S(2)}) collective-permute-start(bf16[4,256,256]{2,1,0:T(8,128)(2,1)S(1)} %get-tuple-element.384), channel_id=1, source_target_pairs={{0,72},{8,64},{64,8},{72,0},{1,73},{9,65},{65,9},{73,1},{2,74},{10... | collective-permute-start | bytes 1572872 | tf_op jit(solution)/shard_map/ppermute | solution.py:27
  397.2 14.6 %collective-permute-start.76 = (bf16[128,1024]{1,0:T(8,128)(2,1)}, bf16[128,1024]{1,0:T(8,128)(2,1)}, u32[]{:S(2)}, u32[]{:S(2)}) collective-permute-start(bf16[128,1024]{1,0:T(8,128)(2,1)} %get-tuple-element.388), channel_id=1, source_target_pairs={{0,2},{2,0},{4,6},{6,4},{1,3},{3,1},{5,7},{7,5},{8,10},{10,8},{12,... | collective-permute-start | bytes 786440 | tf_op jit(solution)/shard_map/ppermute | solution.py:27
  397.2 17.5 %collective-permute-start.77 = (bf16[128,1024]{1,0:T(8,128)(2,1)}, bf16[128,1024]{1,0:T(8,128)(2,1)}, u32[]{:S(2)}, u32[]{:S(2)}) collective-permute-start(bf16[128,1024]{1,0:T(8,128)(2,1)} %get-tuple-element.389), channel_id=1, source_target_pairs={{0,4},{2,6},{4,0},{6,2},{1,5},{3,7},{5,1},{7,3},{8,12},{10,14},{12... | collective-permute-start | bytes 786440 | tf_op jit(solution)/shard_map/ppermute | solution.py:27
  399.0 15.9 %collective-permute-start.78 = (bf16[128,1024]{1,0:T(8,128)(2,1)}, bf16[128,1024]{1,0:T(8,128)(2,1)}, u32[]{:S(2)}, u32[]{:S(2)}) collective-permute-start(bf16[128,1024]{1,0:T(8,128)(2,1)} %get-tuple-element.390), channel_id=1, source_target_pairs={{0,6},{2,4},{4,2},{6,0},{1,7},{3,5},{5,3},{7,1},{8,14},{10,12},{12... | collective-permute-start | bytes 786440 | tf_op jit(solution)/shard_map/ppermute | solution.py:27
  405.9 14.8 %collective-permute-start.47 = (bf16[64,1024]{1,0:T(8,128)(2,1)S(1)}, bf16[64,1024]{1,0:T(8,128)(2,1)S(1)}, u32[]{:S(2)}, u32[]{:S(2)}) collective-permute-start(bf16[64,1024]{1,0:T(8,128)(2,1)S(1)} %broadcast_select_fusion.1), channel_id=1, source_target_pairs={{0,8},{8,0},{1,9},{9,1},{2,10},{10,2},{3,11},{11,3},{4,12},{12,4},... | collective-permute-start | bytes 393224 | tf_op jit(solution)/shard_map/ppermute | solution.py:27
  420.9 15.8 %collective-permute-start.82 = (bf16[4,144,256]{2,1,0:T(8,128)(2,1)S(1)}, bf16[4,144,256]{2,1,0:T(8,128)(2,1)S(1)}, u32[]{:S(2)}, u32[]{:S(2)}) collective-permute-start(bf16[4,144,256]{2,1,0:T(8,128)(2,1)S(1)} %get-tuple-element.417), channel_id=1, source_target_pairs={{0,8},{8,0},{64,72},{72,64},{1,9},{9,1},{65,73},{73,65},{2,10},{10... | collective-permute-start | bytes 884744 | tf_op jit(solution)/shard_map/ppermute | solution.py:27
  423.9 14.4 %collective-permute-start.83 = (bf16[4,144,256]{2,1,0:T(8,128)(2,1)S(1)}, bf16[4,144,256]{2,1,0:T(8,128)(2,1)S(1)}, u32[]{:S(2)}, u32[]{:S(2)}) collective-permute-start(bf16[4,144,256]{2,1,0:T(8,128)(2,1)S(1)} %get-tuple-element.418), channel_id=1, source_target_pairs={{0,72},{8,64},{64,8},{72,0},{1,73},{9,65},{65,9},{73,1},{2,74},{10... | collective-permute-start | bytes 884744 | tf_op jit(solution)/shard_map/ppermute | solution.py:27
  (173 other events, 1982.0 us)
Sparse Core Ops, SparseCore 0:
  13.6 80.0 all-gather.4
  95.4 59.9 all-gather.6
